TPU v7x, 32 devices: a whole 2x2x4 slice. The times are simulated.
32 devices in a mesh: dp: 8 (over z, x), fsdp: 4 (over y, core).
Axes of the slice: x: 2, y: 2, z: 4, core: 2. Of those that a mesh axis runs over, the one named last changes fastest.
Arguments:
- features: bfloat16 [64, 4, 256, 128], P(('dp', 'fsdp')), may hold values from -6 to 6
- view_count: int32 [64], P(('dp', 'fsdp')), may hold values from 2 to 4
- plane_offsets: int32 [64, 4, 128], P(('dp', 'fsdp')), may hold values from 0 to 15
- depth_grad: float32 [64, 4, 256], P(('dp', 'fsdp')), may hold values from -6 to 6
- gain_self: bfloat16 [128], P('fsdp'), may hold values from 0.5 to 1.5
- self_qkv: bfloat16 [128, 384], P('fsdp'), may hold values from -0.5 to 0.5
- self_out: bfloat16 [128, 128], P('fsdp'), may hold values from -1.5 to 1.5
- gain_cross: bfloat16 [128], P('fsdp'), may hold values from 0.5 to 1.5
- cross_qkv: bfloat16 [128, 384], P('fsdp'), may hold values from -0.5 to 0.5
- cross_out: bfloat16 [128, 128], P('fsdp'), may hold values from -1.5 to 1.5
- gain_ff: bfloat16 [128], P('fsdp'), may hold values from 0.5 to 1.5
- ff_in: bfloat16 [128, 512], P('fsdp'), may hold values from -0.5 to 0.5
- ff_out: bfloat16 [512, 128], P('fsdp'), may hold values from -0.25 to 0.25
- refine: bfloat16 [128, 1152], P('fsdp'), may hold values from -0.1875 to 0.1875
Outputs:
- depth: float32 [64, 4, 256], P(('dp', 'fsdp'))
- features_grad: float32 [64, 4, 256, 128], P(('dp', 'fsdp'))
- gain_self_grad: float32 [128], P('fsdp')
- self_qkv_grad: float32 [128, 384], P('fsdp')
- self_out_grad: float32 [128, 128], P('fsdp')
- gain_cross_grad: float32 [128], P('fsdp')
- cross_qkv_grad: float32 [128, 384], P('fsdp')
- cross_out_grad: float32 [128, 128], P('fsdp')
- gain_ff_grad: float32 [128], P('fsdp')
- ff_in_grad: float32 [128, 512], P('fsdp')
- ff_out_grad: float32 [512, 128], P('fsdp')
- refine_grad: float32 [128, 1152], P('fsdp')
Inputs may be any that keep to these rules, and one draw needn't show every extreme that they name: Views of a scene from view_count on are padding.
All inputs are finite; a program needn't handle non-finite values.
Results may differ from a plain program's by a relative error of at most 0.03.
The roundings to bfloat16 on the way count: a program that leaves them out, or rounds other values in their place, can miss the bound.
Values may be sent and summed in bfloat16 or wider, within the bound.
No kernel may reach another device: no remote copies, remote signals or barrier semaphores. Data moves between devices by JAX's collectives and lax.ppermute only.
A program may use at most 128 MiB of HBM per device.

v0:
```python
import functools

import jax
import jax.numpy as jnp
from jax import lax
from jax.experimental import pallas as pl
from jax.experimental.pallas import tpu as pltpu
from jax.sharding import PartitionSpec as P

C = 128
FFH = 512
PLANES = 128
WIN = 8
VIEWS = 4
HV = 16
PIX = HV * HV
TOK = VIEWS * WIN * WIN
HALF = PIX // 2
PAD_ROWS = 16
MASKED = -1e30
SCALE = C**-0.5
LOG2E = 1.4426950408889634
F32 = jnp.float32
BF16 = jnp.bfloat16
BLOCKS = (3, 1, 3, 1, 4, 4, 9)
VMEM_LIMIT = 60 * 1024 * 1024

ERF_P = 0.39
ERF_C = (0.23532522, 0.09138841, 0.6495594, -0.63540028, 0.88666437, -0.22753713)


def mm(left, right):
    return lax.dot_general(left, right, (((1,), (0,)), ((), ())), preferred_element_type=F32)


def mm_nt(left, right):
    return lax.dot_general(left, right, (((1,), (1,)), ((), ())), preferred_element_type=F32)


def mm_tn(left, right):
    return lax.dot_general(left, right, (((0,), (0,)), ((), ())), preferred_element_type=F32)


def norm_forward(value, gain):
    centred = value - jnp.mean(value, -1, keepdims=True)
    spread = jnp.mean(centred * centred, -1, keepdims=True)
    rstd = lax.rsqrt(spread + 1e-05)
    xhat = centred * rstd
    return xhat, jnp.broadcast_to(rstd, value.shape), (xhat * gain).astype(BF16)


def norm_backward(d_normed, xhat, rstd, gain):
    d_xhat = d_normed * gain
    mean_d = jnp.mean(d_xhat, -1, keepdims=True)
    mean_dx = jnp.mean(d_xhat * xhat, -1, keepdims=True)
    d_gain = jnp.sum((d_normed * xhat).reshape(-1, 8, C), 0)
    return rstd * (d_xhat - mean_d - xhat * mean_dx), d_gain


def split_two(value):
    high = value.astype(BF16)
    return jnp.concatenate([high, (value - high.astype(F32)).astype(BF16)], -1)


def iota(shape, axis):
    return lax.broadcasted_iota(jnp.int32, shape, axis)


def fsdp_bits(parts):
    return parts.bit_length() - 1


def pack_kernel(parts, index_ref, *refs):
    out = refs[-1]
    rows = C // parts
    at = 0
    for ref, blocks in zip(refs[3:10], BLOCKS):
        if ref.shape[0] == blocks * rows and ref.shape[1] == C:
            out[at : at + blocks * rows, :] = ref[...]
        else:
            for block in range(blocks):
                out[at + block * rows : at + (block + 1) * rows, :] = ref[:, block * C : (block + 1) * C]
        at += blocks * rows
    lane = iota((rows, C), 1)
    place = (lane == iota((rows, C), 0) + index_ref[0] * rows).astype(BF16)
    line = iota((PAD_ROWS, C), 0)
    gains = jnp.zeros((PAD_ROWS, C), F32)
    for which in range(3):
        row = mm(jnp.broadcast_to(refs[which][...], (8, rows)), place)[:1]
        gains = jnp.where(line == which, row, gains)
    out[at : at + PAD_ROWS, :] = gains.astype(BF16)


def unpack_kernel(parts, index_ref, left, right, *outs):
    rows = C // parts
    at = 0
    for out, blocks in zip(outs[3:10], BLOCKS):
        total = left[at : at + blocks * rows, :].astype(F32) + right[at : at + blocks * rows, :].astype(F32)
        if out.shape[0] == blocks * rows and out.shape[1] == C:
            out[...] = total
        else:
            for block in range(blocks):
                out[:, block * C : (block + 1) * C] = total[block * rows : (block + 1) * rows]
        at += blocks * rows
    gains = left[at : at + PAD_ROWS, :].astype(F32) + right[at : at + PAD_ROWS, :].astype(F32)
    lane = iota((C, rows), 0)
    place = (lane == iota((C, rows), 1) + index_ref[0] * rows).astype(F32)
    picked = lax.dot_general(
        gains, place, (((1,), (0,)), ((), ())), precision=lax.Precision.HIGHEST, preferred_element_type=F32
    )
    for which in range(3):
        outs[which][...] = picked[which : which + 1]


def main_kernel(
    scenes,
    parts,
    count_ref,
    index_ref,
    features,
    offsets,
    depth_grad,
    packed,
    depth_out,
    grad_out,
    grads_out,
    w_sq, w_so, w_cq, w_co, w_fi, w_fo, w_rf,
    t_sq, t_so, t_cq, t_co, t_fi, t_fo, t_rf,
    gains,
    bias,
    x0s,
    xh_a, xh_b, xh_c, rs_a, rs_b, rs_c,
    no_a, no_b, no_c,
    qkv_a, qkv_b, p_a, p_b, o_a, o_b,
    gd, act,
    x3s, d3s,
    low, rev,
    pads, taps, back_taps,
    g_sq, g_so, g_cq, g_co, g_fi, g_fo, g_rf, g_gain,
):
    rows = C // parts
    halves = HV // WIN

    at = 0
    for ref, blocks in zip((w_sq, w_so, w_cq, w_co, w_fi, w_fo, w_rf), BLOCKS):
        for shard in range(parts):
            if ref is w_fo:
                ref[shard * blocks * rows : (shard + 1) * blocks * rows, :] = packed[shard, at : at + blocks * rows, :]
            else:
                for block in range(blocks):
                    ref[shard * rows : (shard + 1) * rows, block * C : (block + 1) * C] = packed[
                        shard, at + block * rows : at + (block + 1) * rows, :
                    ]
        at += blocks * rows
    total = packed[0, at : at + PAD_ROWS, :].astype(F32)
    for shard in range(1, parts):
        total = total + packed[shard, at : at + PAD_ROWS, :].astype(F32)
    gains[...] = total[:8]
    for source, target in ((w_sq, t_sq), (w_so, t_so), (w_cq, t_cq), (w_co, t_co), (w_fi, t_fi), (w_rf, t_rf)):
        for block in range(source.shape[1] // C):
            target[block * C : (block + 1) * C, :] = source[:, block * C : (block + 1) * C].T
    for block in range(FFH // C):
        t_fo[:, block * C : (block + 1) * C] = w_fo[block * C : (block + 1) * C, :].T

    for ref in (g_sq, g_so, g_cq, g_co, g_fi, g_fo, g_rf, g_gain, pads):
        ref[...] = jnp.zeros_like(ref)
    for ref in (taps, back_taps):
        ref[:, :HV, :] = jnp.zeros((VIEWS, HV, 3 * C), BF16)
        ref[:, HV + PIX :, :] = jnp.zeros((VIEWS, HV, 3 * C), BF16)

    gain_a = gains[0:1, :]
    gain_b = gains[1:2, :]
    gain_c = gains[2:3, :]

    def forward(step, carry):
        scene = step // halves
        half = step % halves

        @pl.when(half == 0)
        def _():
            live = count_ref[scene]
            of_key = iota((TOK, TOK), 1) // (WIN * WIN)
            of_query = iota((TOK, TOK), 0) // (WIN * WIN)
            bias[...] = jnp.where((of_key < live) & (of_key != of_query), 0.0, MASKED)

        piece = features[scene, :, pl.ds(pl.multiple_of(half * HALF, HALF), HALF), :]
        x0s[...] = piece.astype(F32).reshape(VIEWS, WIN, 2, WIN, C)
        for side in range(2):
            spot = pl.ds(side * TOK, TOK)
            x0 = x0s[:, :, side].reshape(TOK, C)
            xhat, rstd, normed = norm_forward(x0, gain_a)
            xh_a[step, spot, :] = xhat
            rs_a[step, spot, :] = rstd
            no_a[step, spot, :] = normed
            qkv = mm(normed, w_sq[...]).astype(BF16)
            qkv_a[step, spot, :] = qkv
            mixed = []
            for view in range(VIEWS):
                lines = slice(view * WIN * WIN, (view + 1) * WIN * WIN)
                scores = mm_nt(qkv[lines, :C], qkv[lines, C : 2 * C]) * (SCALE * LOG2E)
                expo = jnp.exp2(scores - jnp.max(scores, -1, keepdims=True))
                probs = (expo * (1.0 / jnp.sum(expo, -1, keepdims=True))).astype(BF16)
                p_a[step, pl.ds(side * TOK + view * WIN * WIN, WIN * WIN), :] = probs
                mixed.append(mm(probs, qkv[lines, 2 * C :]))
            mixed = jnp.concatenate(mixed, 0).astype(BF16)
            o_a[step, spot, :] = mixed
            x1 = x0 + mm(mixed, w_so[...])
            xhat, rstd, normed = norm_forward(x1, gain_b)
            xh_b[step, spot, :] = xhat
            rs_b[step, spot, :] = rstd
            no_b[step, spot, :] = normed
            qkv = mm(normed, w_cq[...]).astype(BF16)
            qkv_b[step, spot, :] = qkv
            scores = mm_nt(qkv[:, :C], qkv[:, C : 2 * C]) * (SCALE * LOG2E) + bias[...]
            expo = jnp.exp2(scores - jnp.max(scores, -1, keepdims=True))
            probs = (expo * (1.0 / jnp.sum(expo, -1, keepdims=True))).astype(BF16)
            p_b[step, spot, :] = probs
            mixed = mm(probs, qkv[:, 2 * C :]).astype(BF16)
            o_b[step, spot, :] = mixed
            x2 = x1 + mm(mixed, w_co[...])
            xhat, rstd, normed = norm_forward(x2, gain_c)
            xh_c[step, spot, :] = xhat
            rs_c[step, spot, :] = rstd
            no_c[step, spot, :] = normed
            x3 = x2
            for block in range(FFH // C):
                cols = slice(block * C, (block + 1) * C)
                inner = mm(normed, w_fi[:, cols])
                t = 1.0 / (1.0 + (ERF_P * 0.5**0.5) * jnp.abs(inner))
                bell = jnp.exp2(inner * inner * (-0.5 * LOG2E))
                poly = 0.5 * ERF_C[5] * t + 0.5 * ERF_C[4]
                for coef in ERF_C[3::-1]:
                    poly = poly * t + 0.5 * coef
                tail = poly * t * bell
                cdf = jnp.where(inner >= 0.0, 1.0 - tail, tail)
                active = (inner * cdf).astype(BF16)
                gd[step, spot, cols] = cdf + inner * bell * 0.3989422804014327
                act[step, spot, cols] = active
                x3 = x3 + mm(active, w_fo[cols, :])
            x3s[scene, :, half, :, side] = x3.reshape(VIEWS, WIN, WIN, C)
        return carry

    lax.fori_loop(0, scenes * halves, forward, 0)

    row = iota((HALF, HALF), 0)
    lane = iota((HALF, HALF), 1)
    flip = (row + lane == HALF - 1).astype(BF16)
    eye = row == lane
    skew_keep = jnp.where((lane < HV) & (lane <= row % HV), 0.5 * SCALE, 0.0)
    back_keep = jnp.where((lane < HV) & (HV - 1 - lane <= row % HV), 0.5 * SCALE, 0.0)
    column = iota((PIX, C), 0) % HV
    not_first = column > 0
    not_last = column < HV - 1
    depth_values = 1.0 + 3.0 * iota((1, PLANES), 1).astype(F32) / (PLANES - 1)

    def im2col(value, pad, dest):
        pad[8 : 8 + PIX, :] = value
        dest[HV : HV + PIX, C : 2 * C] = value.astype(BF16)
        before = jnp.where(not_first, pad[7 : 7 + PIX, :], 0.0).astype(BF16)
        after = jnp.where(not_last, pad[9 : 9 + PIX, :], 0.0).astype(BF16)
        return before, after

    def head(scene, carry):
        live = count_ref[scene]
        for view in range(VIEWS):
            piece = x3s[scene, view].reshape(PIX, C).astype(BF16)
            low[view] = piece
            for part in range(2):
                lines = slice(part * HALF, (part + 1) * HALF)
                rev[view, lines, :] = mm(flip, piece[lines]).astype(BF16)
        d3s[scene] = jnp.zeros(d3s.shape[1:], F32)
        for view in range(VIEWS):
            partner = jnp.where(view + 1 < live, view + 1, 0)
            shift = offsets[scene, view : view + 1, :]
            hot = (shift == row).astype(BF16)
            hot_back = (shift == HV - 1 - row).astype(BF16)
            skewed = []
            for part in range(2):
                lines = slice(part * HALF, (part + 1) * HALF)
                corr = mm_nt(low[view, lines, :], rev[partner, lines, :])
                skewed.append(pltpu.roll(corr, 1, 1, stride=1, stride_axis=0) * skew_keep)
            cost = mm(split_two(jnp.concatenate(skewed, 0)), jnp.concatenate([hot, hot], 0))
            before, after = im2col(cost, pads.at[0, view], taps.at[view])
            taps[view, HV : HV + PIX, :C] = before
            taps[view, HV : HV + PIX, 2 * C :] = after
            columns = jnp.concatenate([taps[view, HV * a : HV * a + PIX, :] for a in range(3)], -1)
            refined = cost + mm(columns, t_rf[...])
            expo = jnp.exp2((refined - jnp.max(refined, -1, keepdims=True)) * LOG2E)
            inverse = 1.0 / jnp.sum(expo, -1, keepdims=True)
            depth = jnp.sum(expo * depth_values, -1, keepdims=True) * inverse
            valid = jnp.where(view < live, 1.0, 0.0)
            incoming = []
            for part in range(2):
                lines = slice(part * HALF, (part + 1) * HALF)
                depth_out[scene, view : view + 1, lines] = (
                    jnp.sum(jnp.where(eye, depth[lines], 0.0), 0, keepdims=True) * valid
                )
                incoming.append(
                    jnp.sum(jnp.where(eye, depth_grad[scene, view : view + 1, lines], 0.0), 1, keepdims=True)
                )
            weight = jnp.concatenate(incoming, 0) * (inverse * valid)
            d_refined = expo * (weight * depth_values - weight * depth)
            before, after = im2col(d_refined, pads.at[1, view], back_taps.at[view])
            back_taps[view, HV : HV + PIX, :C] = after
            back_taps[view, HV : HV + PIX, 2 * C :] = before
            g_rf[...] += mm_tn(back_taps[view, HV : HV + PIX, C : 2 * C], columns)
            d_cost = d_refined
            for a in range(3):
                shifted = back_taps[view, HV * (2 - a) : HV * (2 - a) + PIX, :]
                for b in range(3):
                    tap = 3 * a + b
                    d_cost = d_cost + mm(shifted[:, b * C : (b + 1) * C], w_rf[:, tap * C : (tap + 1) * C])
            d_skewed = mm_nt(split_two(d_cost), jnp.concatenate([hot_back, hot_back], -1))
            for part in range(2):
                lines = slice(part * HALF, (part + 1) * HALF)
                d_corr = pltpu.roll(
                    d_skewed[lines] * back_keep, HALF - HV + 1, 1, stride=1, stride_axis=0
                ).astype(BF16)
                shape = (WIN, 2, WIN, C)
                d3s[scene, view, part] += mm(d_corr, low[partner, lines, :]).reshape(shape)
                d3s[scene, partner, part] += mm_tn(d_corr, low[view, lines, :]).reshape(shape)
        return carry

    lax.fori_loop(0, scenes, head, 0)

    def backward(step, carry):
        scene = step // halves
        half = step % halves
        for side in range(2):
            spot = pl.ds(side * TOK, TOK)
            d3 = d3s[scene, :, half, :, side].reshape(TOK, C)
            d_low = d3.astype(BF16)
            normed = no_c[step, spot, :]
            g_fo[...] += mm_tn(d_low, act[step, spot, :])
            d_normed = jnp.zeros((TOK, C), F32)
            d_inners = []
            for block in range(FFH // C):
                cols = slice(block * C, (block + 1) * C)
                d_inner = (mm(d_low, t_fo[:, cols]) * gd[step, spot, cols]).astype(BF16)
                d_inners.append(d_inner)
            d_inner = jnp.concatenate(d_inners, -1)
            g_fi[...] += mm_tn(normed, d_inner)
            d_normed = mm(d_inner, t_fi[...])
            d_hidden, d_gain = norm_backward(d_normed, xh_c[step, spot, :], rs_c[step, spot, :], gain_c)
            g_gain[2] += d_gain
            d2 = d3 + d_hidden
            d_low = d2.astype(BF16)
            qkv = qkv_b[step, spot, :]
            g_co[...] += mm_tn(o_b[step, spot, :], d_low)
            d_mixed = mm(d_low, t_co[...]).astype(BF16)
            probs = p_b[step, spot, :]
            d_values = mm_tn(probs, d_mixed)
            d_probs = mm_nt(d_mixed, qkv[:, 2 * C :])
            probs = probs.astype(F32)
            delta = jnp.sum(d_probs * probs, -1, keepdims=True)
            d_raw = (probs * ((d_probs - delta) * SCALE)).astype(BF16)
            d_query = mm(d_raw, qkv[:, C : 2 * C])
            d_keys = mm_tn(d_raw, qkv[:, :C])
            d_packed = jnp.concatenate([d_query, d_keys, d_values], -1).astype(BF16)
            g_cq[...] += mm_tn(no_b[step, spot, :], d_packed)
            d_normed = mm(d_packed, t_cq[...])
            d_hidden, d_gain = norm_backward(d_normed, xh_b[step, spot, :], rs_b[step, spot, :], gain_b)
            g_gain[1] += d_gain
            d1 = d2 + d_hidden
            d_low = d1.astype(BF16)
            qkv = qkv_a[step, spot, :]
            g_so[...] += mm_tn(o_a[step, spot, :], d_low)
            d_mixed = mm(d_low, t_so[...]).astype(BF16)
            pieces = []
            for view in range(VIEWS):
                lines = slice(view * WIN * WIN, (view + 1) * WIN * WIN)
                probs = p_a[step, pl.ds(side * TOK + view * WIN * WIN, WIN * WIN), :]
                d_values = mm_tn(probs, d_mixed[lines])
                d_probs = mm_nt(d_mixed[lines], qkv[lines, 2 * C :])
                probs = probs.astype(F32)
                delta = jnp.sum(d_probs * probs, -1, keepdims=True)
                d_raw = (probs * ((d_probs - delta) * SCALE)).astype(BF16)
                d_query = mm(d_raw, qkv[lines, C : 2 * C])
                d_keys = mm_tn(d_raw, qkv[lines, :C])
                pieces.append(jnp.concatenate([d_query, d_keys, d_values], -1))
            d_packed = jnp.concatenate(pieces, 0).astype(BF16)
            g_sq[...] += mm_tn(no_a[step, spot, :], d_packed)
            d_normed = mm(d_packed, t_sq[...])
            d_hidden, d_gain = norm_backward(d_normed, xh_a[step, spot, :], rs_a[step, spot, :], gain_a)
            g_gain[0] += d_gain
            grad_out[scene, :, half, :, side] = (d1 + d_hidden).reshape(VIEWS, WIN, WIN, C)
        return carry

    lax.fori_loop(0, scenes * halves, backward, 0)

    bits = fsdp_bits(parts)
    line = iota((PAD_ROWS, C), 0)
    gain_rows = jnp.zeros((PAD_ROWS, C), F32)
    for which in range(3):
        gain_rows = jnp.where(line == which, jnp.sum(g_gain[which], 0, keepdims=True), gain_rows)
    gain_rows = gain_rows.astype(BF16)
    for block in range(FFH // C):
        w_fo[block * C : (block + 1) * C, :] = g_fo[:, block * C : (block + 1) * C].T.astype(BF16)
    for shard in range(parts):
        apart = shard ^ index_ref[0]
        slot = jnp.int32(0)
        for bit in range(bits):
            slot = slot + ((apart >> bit) & 1) * (1 << (bits - 1 - bit))
        at = 0
        for ref, blocks in zip((g_sq, g_so, g_cq, g_co, g_fi, w_fo, g_rf), BLOCKS):
            if ref is w_fo:
                grads_out[slot, at : at + blocks * rows, :] = ref[shard * blocks * rows : (shard + 1) * blocks * rows, :]
            else:
                for block in range(blocks):
                    grads_out[slot, at + block * rows : at + (block + 1) * rows, :] = ref[
                        shard * rows : (shard + 1) * rows, block * C : (block + 1) * C
                    ].astype(BF16)
            at += blocks * rows
        grads_out[slot, at : at + PAD_ROWS, :] = gain_rows


VMEM = pl.BlockSpec(memory_space=pltpu.VMEM)
SMEM = pl.BlockSpec(memory_space=pltpu.SMEM)


def exchange(value, axis, bit):
    size = lax.axis_size(axis)
    return lax.ppermute(value, axis, [(i, i ^ (1 << bit)) for i in range(size)])


def local(
    features,
    view_count,
    plane_offsets,
    depth_grad,
    gain_self,
    self_qkv,
    self_out,
    gain_cross,
    cross_qkv,
    cross_out,
    gain_ff,
    ff_in,
    ff_out,
    refine,
):
    parts = lax.axis_size("fsdp")
    copies = lax.axis_size("dp")
    scenes = features.shape[0]
    rows = C // parts
    shard_rows = sum(BLOCKS) * rows + PAD_ROWS
    index = lax.axis_index("fsdp").astype(jnp.int32).reshape(1)
    params = pltpu.CompilerParams(vmem_limit_bytes=VMEM_LIMIT)

    pack = pl.pallas_call(
        functools.partial(pack_kernel, parts),
        out_shape=jax.ShapeDtypeStruct((shard_rows, C), BF16),
        in_specs=[SMEM] + [VMEM] * 10,
        out_specs=VMEM,
        compiler_params=params,
        name="pack",
    )
    shard = pack(
        index,
        gain_self.reshape(1, rows),
        gain_cross.reshape(1, rows),
        gain_ff.reshape(1, rows),
        self_qkv,
        self_out,
        cross_qkv,
        cross_out,
        ff_in,
        ff_out,
        refine,
    )
    packed = lax.all_gather(shard, "fsdp", axis=0)

    steps = scenes * (HV // WIN)
    span = 2 * TOK
    scratch = [
        ((C, 3 * C), BF16), ((C, C), BF16), ((C, 3 * C), BF16), ((C, C), BF16),
        ((C, FFH), BF16), ((FFH, C), BF16), ((C, 9 * PLANES), BF16),
        ((3 * C, C), BF16), ((C, C), BF16), ((3 * C, C), BF16), ((C, C), BF16),
        ((FFH, C), BF16), ((C, FFH), BF16), ((9 * PLANES, C), BF16),
        ((8, C), F32),
        ((TOK, TOK), F32),
        ((VIEWS, WIN, 2, WIN, C), F32),
    ]
    scratch += [((steps, span, C), F32)] * 6
    scratch += [((steps, span, C), BF16)] * 3
    scratch += [
        ((steps, span, 3 * C), BF16), ((steps, span, 3 * C), BF16),
        ((steps, span, WIN * WIN), BF16), ((steps, span, TOK), BF16),
        ((steps, span, C), BF16), ((steps, span, C), BF16),
        ((steps, span, FFH), F32), ((steps, span, FFH), BF16),
        ((scenes, VIEWS, 2, WIN, 2, WIN, C), F32), ((scenes, VIEWS, 2, WIN, 2, WIN, C), F32),
        ((VIEWS, PIX, C), BF16), ((VIEWS, PIX, C), BF16),
        ((2, VIEWS, PIX + 16, C), F32),
        ((VIEWS, PIX + 2 * HV, 3 * C), BF16), ((VIEWS, PIX + 2 * HV, 3 * C), BF16),
        ((C, 3 * C), F32), ((C, C), F32), ((C, 3 * C), F32), ((C, C), F32),
        ((C, FFH), F32), ((C, FFH), F32), ((C, 9 * PLANES), F32), ((3, 8, C), F32),
    ]
    main = pl.pallas_call(
        functools.partial(main_kernel, scenes, parts),
        out_shape=(
            jax.ShapeDtypeStruct((scenes, VIEWS, PIX), F32),
            jax.ShapeDtypeStruct((scenes, VIEWS, 2, WIN, 2, WIN, C), F32),
            jax.ShapeDtypeStruct((parts, shard_rows, C), BF16),
        ),
        in_specs=[SMEM, SMEM] + [VMEM] * 4,
        out_specs=(VMEM, VMEM, VMEM),
        scratch_shapes=[pltpu.VMEM(shape, kind) for shape, kind in scratch],
        compiler_params=params,
        name="layer",
    )
    depth, grad_features, grads = main(view_count, index, features, plane_offsets, depth_grad, packed)

    for bit in range(fsdp_bits(parts)):
        half = grads.shape[0] // 2
        grads = grads[:half] + exchange(grads[half:], "fsdp", bit)
    grads = grads[0]
    bits = fsdp_bits(copies)
    for bit in range(bits - 1):
        grads = grads + exchange(grads, "dp", bit)
    other = exchange(grads, "dp", bits - 1)

    unpack = pl.pallas_call(
        functools.partial(unpack_kernel, parts),
        out_shape=tuple(jax.ShapeDtypeStruct((1, rows), F32) for _ in range(3))
        + tuple(
            jax.ShapeDtypeStruct(piece.shape, F32)
            for piece in (self_qkv, self_out, cross_qkv, cross_out, ff_in, ff_out, refine)
        ),
        in_specs=[SMEM, VMEM, VMEM],
        out_specs=(VMEM,) * 10,
        compiler_params=params,
        name="unpack",
    )
    ga, gb, gc, d_sq, d_so, d_cq, d_co, d_fi, d_fo, d_rf = unpack(index, grads, other)
    return (
        depth,
        grad_features.reshape(features.shape),
        ga.reshape(rows),
        d_sq,
        d_so,
        gb.reshape(rows),
        d_cq,
        d_co,
        gc.reshape(rows),
        d_fi,
        d_fo,
        d_rf,
    )


def solution(mesh):
    placed = (
        P(("dp", "fsdp"), None, None, None),
        P(("dp", "fsdp")),
        P(("dp", "fsdp"), None, None),
        P(("dp", "fsdp"), None, None),
        P("fsdp"),
        P("fsdp", None),
        P("fsdp", None),
        P("fsdp"),
        P("fsdp", None),
        P("fsdp", None),
        P("fsdp"),
        P("fsdp", None),
        P("fsdp", None),
        P("fsdp", None),
    )
    return jax.shard_map(
        local,
        mesh=mesh,
        in_specs=placed,
        out_specs=(
            P(("dp", "fsdp"), None, None),
            P(("dp", "fsdp"), None, None, None),
            P("fsdp"),
            P("fsdp", None),
            P("fsdp", None),
            P("fsdp"),
            P("fsdp", None),
            P("fsdp", None),
            P("fsdp"),
            P("fsdp", None),
            P("fsdp", None),
            P("fsdp", None),
        ),
        check_vma=False,
    )
```

profile of v0, /device:TPU:0, one launch (start us, length us, event | category | flops | bytes accessed | tf_op | source)
XLA Modules:
  0.0 115.6 jit_solution(11875948062024537204)
XLA Ops:
  0.7 1.9 %pack.1 = bf16[816,128]{1,0:T(8,128)(2,1)} custom-call(s32[1]{0:T(128)} %bitcast.index_ref, bf16[1,32]{1,0:T(2,128)(2,1)} %bitcast.12, bf16[1,32]{1,0:T(2,128)(2,1)} %bitcast.13, bf16[1,32]{1,0:T(2,128)(2,1)} %bitcast.14, bf16[32,384]{1,0:T(8,128)(2,1)} %refs_3_.1, bf16[32,128]{1,0:T(8,128)(2,1)} %refs_4_.1, bf16[32,384]{1,0:T(8,128)(2,1)} %refs_5_.1, ...), custom_call_target="tpu_custom_call" | custom-call | tf_op jit(solution)/shard_map/pack/pallas_call | solution.py:458
  2.5 11.9 %all-gather = bf16[3264,128]{1,0:T(8,128)(2,1)} all-gather(bf16[816,128]{1,0:T(8,128)(2,1)} %pack.1), channel_id=2, replica_groups=mesh['dp'=8,'fsdp'=4] {'fsdp'}, dimensions={0}, use_global_device_ids=true | all-gather | bytes 1044480 | tf_op jit(solution)/shard_map/all_gather | solution.py:471
  14.4 65.4 %layer.1 = (f32[2,4,256]{2,1,0:T(4,128)}, f32[2,4,2,8,2,8,128]{6,5,4,3,2,1,0:T(8,128)}, bf16[4,816,128]{2,1,0:T(8,128)(2,1)}) custom-call(s32[2]{0:T(128)} %count_ref.1, s32[1]{0:T(128)} %bitcast.index_ref, bf16[2,4,256,128]{3,2,1,0:T(8,128)(2,1)} %features.1, s32[2,4,128]{2,1,0:T(4,128)} %offsets.1, f32[2,4,256]{2,1,0:T(4,128)} %depth_grad.1, ...), custom_call_target="tpu_custom_call" | custom-call | tf_op jit(solution)/shard_map/layer/pallas_call | solution.py:511
  79.9 0.0 copy-start
  79.9 1.1 slice.13
  81.0 0.4 collective-permute-start
  81.4 1.4 %collective-permute-done = bf16[2,816,128]{2,1,0:T(8,128)(2,1)S(1)} collective-permute-done((bf16[2,816,128]{2,1,0:T(8,128)(2,1)S(1)}, bf16[2,816,128]{2,1,0:T(8,128)(2,1)S(1)}, u32[]{:S(2)}, u32[]{:S(2)}) %collective-permute-start) | collective-permute-done | bytes 417824 | tf_op jit(solution)/shard_map/ppermute | solution.py:423
  82.8 0.0 copy-done
  82.8 0.1 slice_add_fusion
  82.9 0.2 collective-permute-start.1
  83.1 7.3 %collective-permute-done.1 = bf16[1,816,128]{2,1,0:T(8,128)(2,1)S(1)} collective-permute-done((bf16[1,816,128]{2,1,0:T(8,128)(2,1)S(1)}, bf16[1,816,128]{2,1,0:T(8,128)(2,1)S(1)}, u32[]{:S(2)}, u32[]{:S(2)}) %collective-permute-start.1) | collective-permute-done | bytes 208928 | tf_op jit(solution)/shard_map/ppermute | solution.py:423
  90.4 1.5 %collective-permute-start.2 = (bf16[816,128]{1,0:T(8,128)(2,1)S(1)}, bf16[816,128]{1,0:T(8,128)(2,1)S(1)}, u32[]{:S(2)}, u32[]{:S(2)}) collective-permute-start(bf16[816,128]{1,0:T(8,128)(2,1)S(1)} %fusion), channel_id=1, source_target_pairs={{0,4},{4,0},{8,12},{12,8},{16,20},{20,16},{24,28},{28,24},{1,5},{5... | collective-permute-start | bytes 626696 | tf_op jit(solution)/shard_map/ppermute | solution.py:423
  91.9 5.1 %collective-permute-done.2 = bf16[816,128]{1,0:T(8,128)(2,1)S(1)} collective-permute-done((bf16[816,128]{1,0:T(8,128)(2,1)S(1)}, bf16[816,128]{1,0:T(8,128)(2,1)S(1)}, u32[]{:S(2)}, u32[]{:S(2)}) %collective-permute-start.2) | collective-permute-done | bytes 208928 | tf_op jit(solution)/shard_map/ppermute | solution.py:423
  97.1 0.1 add.14
  97.1 1.6 %collective-permute-start.3 = (bf16[816,128]{1,0:T(8,128)(2,1)S(1)}, bf16[816,128]{1,0:T(8,128)(2,1)S(1)}, u32[]{:S(2)}, u32[]{:S(2)}) collective-permute-start(bf16[816,128]{1,0:T(8,128)(2,1)S(1)} %add.14), channel_id=1, source_target_pairs={{0,8},{4,12},{8,0},{12,4},{16,24},{20,28},{24,16},{28,20},{1,9},{5... | collective-permute-start | bytes 626696 | tf_op jit(solution)/shard_map/ppermute | solution.py:423
  98.8 4.2 %collective-permute-done.3 = bf16[816,128]{1,0:T(8,128)(2,1)S(1)} collective-permute-done((bf16[816,128]{1,0:T(8,128)(2,1)S(1)}, bf16[816,128]{1,0:T(8,128)(2,1)S(1)}, u32[]{:S(2)}, u32[]{:S(2)}) %collective-permute-start.3) | collective-permute-done | bytes 208928 | tf_op jit(solution)/shard_map/ppermute | solution.py:423
  103.0 0.1 add.15.left
  103.1 0.0 copy-start.1
  103.1 2.6 %collective-permute-start.4 = (bf16[816,128]{1,0:T(8,128)(2,1)S(1)}, bf16[816,128]{1,0:T(8,128)(2,1)S(1)}, u32[]{:S(2)}, u32[]{:S(2)}) collective-permute-start(bf16[816,128]{1,0:T(8,128)(2,1)S(1)} %add.15.left), channel_id=1, source_target_pairs={{0,16},{4,20},{8,24},{12,28},{16,0},{20,4},{24,8},{28,12},{1,17},{... | collective-permute-start | bytes 626696 | tf_op jit(solution)/shard_map/ppermute | solution.py:423
  105.7 7.4 %collective-permute-done.4.right = bf16[816,128]{1,0:T(8,128)(2,1)S(1)} collective-permute-done((bf16[816,128]{1,0:T(8,128)(2,1)S(1)}, bf16[816,128]{1,0:T(8,128)(2,1)S(1)}, u32[]{:S(2)}, u32[]{:S(2)}) %collective-permute-start.4) | collective-permute-done | bytes 208928 | tf_op jit(solution)/shard_map/ppermute | solution.py:423
  113.1 0.0 copy-done.1
  113.1 0.0 copy-start.2
  113.1 0.7 copy-done.2
  113.7 1.8 %unpack.1 = (f32[1,32]{1,0:T(1,128)}, f32[1,32]{1,0:T(1,128)}, f32[1,32]{1,0:T(1,128)}, f32[32,384]{1,0:T(8,128)}, f32[32,128]{1,0:T(8,128)}, /*index=5*/f32[32,...) custom-call(s32[1]{0:T(128)} %bitcast.index_ref, ...), custom_call_target="tpu_custom_call" | custom-call | tf_op jit(solution)/shard_map/unpack/pallas_call | solution.py:534
  (2 shorter events, 0.0 us)
Async XLA Ops:
  79.9 2.9 %copy-start = (bf16[4,816,128]{2,1,0:T(8,128)(2,1)S(1)}, bf16[4,816,128]{2,1,0:T(8,128)(2,1)}, u32[]{:S(2)}) copy-start(bf16[4,816,128]{2,1,0:T(8,128)(2,1)} %get-tuple-element.27) | copy-start | bytes 2506756
  81.0 1.8 %collective-permute-start = (bf16[2,816,128]{2,1,0:T(8,128)(2,1)S(1)}, bf16[2,816,128]{2,1,0:T(8,128)(2,1)S(1)}, u32[]{:S(2)}, u32[]{:S(2)}) collective-permute-start(bf16[2,816,128]{2,1,0:T(8,128)(2,1)S(1)} %slice.13), channel_id=1, source_target_pairs={{0,1},{1,0},{2,3},{3,2},{4,5},{5,4},{6,7},{7,6},{8,9},{9,8},{10,11... | collective-permute-start | bytes 1253384 | tf_op jit(solution)/shard_map/ppermute | solution.py:423
  82.9 7.5 %collective-permute-start.1 = (bf16[1,816,128]{2,1,0:T(8,128)(2,1)S(1)}, bf16[1,816,128]{2,1,0:T(8,128)(2,1)S(1)}, u32[]{:S(2)}, u32[]{:S(2)}) collective-permute-start(bf16[1,816,128]{2,1,0:T(8,128)(2,1)S(1)} %slice.17), channel_id=1, source_target_pairs={{0,2},{1,3},{2,0},{3,1},{4,6},{5,7},{6,4},{7,5},{8,10},{9,11},{10,... | collective-permute-start | bytes 626696 | tf_op jit(solution)/shard_map/ppermute | solution.py:423
  90.4 6.7 %collective-permute-start.2 = (bf16[816,128]{1,0:T(8,128)(2,1)S(1)}, bf16[816,128]{1,0:T(8,128)(2,1)S(1)}, u32[]{:S(2)}, u32[]{:S(2)}) collective-permute-start(bf16[816,128]{1,0:T(8,128)(2,1)S(1)} %fusion), channel_id=1, source_target_pairs={{0,4},{4,0},{8,12},{12,8},{16,20},{20,16},{24,28},{28,24},{1,5},{5... | collective-permute-start | bytes 626696 | tf_op jit(solution)/shard_map/ppermute | solution.py:423
  97.1 5.9 %collective-permute-start.3 = (bf16[816,128]{1,0:T(8,128)(2,1)S(1)}, bf16[816,128]{1,0:T(8,128)(2,1)S(1)}, u32[]{:S(2)}, u32[]{:S(2)}) collective-permute-start(bf16[816,128]{1,0:T(8,128)(2,1)S(1)} %add.14), channel_id=1, source_target_pairs={{0,8},{4,12},{8,0},{12,4},{16,24},{20,28},{24,16},{28,20},{1,9},{5... | collective-permute-start | bytes 626696 | tf_op jit(solution)/shard_map/ppermute | solution.py:423
  103.1 10.0 %copy-start.1 = (bf16[816,128]{1,0:T(8,128)(2,1)}, bf16[816,128]{1,0:T(8,128)(2,1)S(1)}, u32[]{:S(2)}) copy-start(bf16[816,128]{1,0:T(8,128)(2,1)S(1)} %add.15.left) | copy-start | bytes 626692
  103.1 10.0 %collective-permute-start.4 = (bf16[816,128]{1,0:T(8,128)(2,1)S(1)}, bf16[816,128]{1,0:T(8,128)(2,1)S(1)}, u32[]{:S(2)}, u32[]{:S(2)}) collective-permute-start(bf16[816,128]{1,0:T(8,128)(2,1)S(1)} %add.15.left), channel_id=1, source_target_pairs={{0,16},{4,20},{8,24},{12,28},{16,0},{20,4},{24,8},{28,12},{1,17},{... | collective-permute-start | bytes 626696 | tf_op jit(solution)/shard_map/ppermute | solution.py:423
  113.1 0.7 copy-start.2
where the time goes:
time: 116 us
  Pallas kernels  69.1 us (60%)
  waiting for transfers between devices  25.5 us (22%)
  blocking collectives  11.9 us (10%)
  starting transfers between devices  6.39 us (6%)
  local copies, waits for them, and re-layouts  1.8 us (2%)
    pallas_call x1, Pallas kernels, local(): main(view_count, index, features, plane_offsets, depth_grad, packed)  65.4 us
    ppermute x5, waiting for transfers between devices, exchange(): return lax.ppermute(value, axis, [(i, i ^ 1 << bit) for i in range(size)])  25.5 us
    all_gather x1, blocking collectives, local(): packed = lax.all_gather(shard, 'fsdp', axis=0)  11.9 us
    ppermute x5, starting transfers between devices, exchange(): return lax.ppermute(value, axis, [(i, i ^ 1 << bit) for i in range(size)])  6.39 us
  transfers between devices with their start and end apart: 5, of which 5 were waited for; matrix products, arithmetic and copies ran while one was open for 0% of the time, Pallas kernels for 0%

commit v1 on v0

--- a/solution.py
+++ b/solution.py
@@ -125,7 +125,7 @@
     grad_out,
     grads_out,
     w_sq, w_so, w_cq, w_co, w_fi, w_fo, w_rf,
-    t_sq, t_so, t_cq, t_co, t_fi, t_fo, t_rf,
+    t_sq, t_so, t_cq, t_co, t_fi, t_fo, t_rf, b_rf,
     gains,
     bias,
     x0s,
@@ -136,6 +136,7 @@
     x3s, d3s,
     low, rev,
     pads, taps, back_taps,
+    tables, eye, flip, hots,
     g_sq, g_so, g_cq, g_co, g_fi, g_fo, g_rf, g_gain,
 ):
     rows = C // parts
@@ -159,6 +160,8 @@
     for source, target in ((w_sq, t_sq), (w_so, t_so), (w_cq, t_cq), (w_co, t_co), (w_fi, t_fi), (w_rf, t_rf)):
         for block in range(source.shape[1] // C):
             target[block * C : (block + 1) * C, :] = source[:, block * C : (block + 1) * C].T
+    for block in range(9):
+        b_rf[block * C : (block + 1) * C, :] = w_rf[:, block * C : (block + 1) * C]
     for block in range(FFH // C):
         t_fo[:, block * C : (block + 1) * C] = w_fo[block * C : (block + 1) * C, :].T
 
@@ -171,6 +174,13 @@
     gain_a = gains[0:1, :]
     gain_b = gains[1:2, :]
     gain_c = gains[2:3, :]
+
+    places = [slice(side * TOK, (side + 1) * TOK) for side in range(2)]
+    windows = [slice(at * WIN * WIN, (at + 1) * WIN * WIN) for at in range(2 * VIEWS)]
+
+    def soft(scores):
+        expo = jnp.exp2(scores - jnp.max(scores, -1, keepdims=True))
+        return (expo * (1.0 / jnp.sum(expo, -1, keepdims=True))).astype(BF16)
 
     def forward(step, carry):
         scene = step // halves
@@ -185,205 +195,221 @@
 
         piece = features[scene, :, pl.ds(pl.multiple_of(half * HALF, HALF), HALF), :]
         x0s[...] = piece.astype(F32).reshape(VIEWS, WIN, 2, WIN, C)
+        x0 = jnp.concatenate([x0s[:, :, side].reshape(TOK, C) for side in range(2)], 0)
+        xhat, rstd, normed = norm_forward(x0, gain_a)
+        xh_a[step] = xhat
+        rs_a[step] = rstd
+        no_a[step] = normed
+        qkv = mm(normed, w_sq[...]).astype(BF16)
+        qkv_a[step] = qkv
+        scores = jnp.concatenate([mm_nt(qkv[at, :C], qkv[at, C : 2 * C]) for at in windows], 0)
+        probs = soft(scores * (SCALE * LOG2E))
+        p_a[step] = probs
+        mixed = jnp.concatenate([mm(probs[at], qkv[at, 2 * C :]) for at in windows], 0).astype(BF16)
+        o_a[step] = mixed
+        x1 = x0 + mm(mixed, w_so[...])
+        xhat, rstd, normed = norm_forward(x1, gain_b)
+        xh_b[step] = xhat
+        rs_b[step] = rstd
+        no_b[step] = normed
+        qkv = mm(normed, w_cq[...]).astype(BF16)
+        qkv_b[step] = qkv
+        scores = [mm_nt(qkv[at, :C], qkv[at, C : 2 * C]) * (SCALE * LOG2E) + bias[...] for at in places]
+        probs = soft(jnp.concatenate(scores, 0))
+        p_b[step] = probs
+        mixed = jnp.concatenate([mm(probs[at], qkv[at, 2 * C :]) for at in places], 0).astype(BF16)
+        o_b[step] = mixed
+        x2 = x1 + mm(mixed, w_co[...])
+        xhat, rstd, normed = norm_forward(x2, gain_c)
+        xh_c[step] = xhat
+        rs_c[step] = rstd
+        no_c[step] = normed
+        x3 = x2
+        for block in range(FFH // C):
+            cols = slice(block * C, (block + 1) * C)
+            inner = mm(normed, w_fi[:, cols])
+            t = 1.0 / (1.0 + (ERF_P * 0.5**0.5) * jnp.abs(inner))
+            bell = jnp.exp2(inner * inner * (-0.5 * LOG2E))
+            poly = 0.5 * ERF_C[5] * t + 0.5 * ERF_C[4]
+            for coef in ERF_C[3::-1]:
+                poly = poly * t + 0.5 * coef
+            tail = poly * t * bell
+            cdf = jnp.where(inner >= 0.0, 1.0 - tail, tail)
+            gd[step, :, cols] = cdf + inner * bell * 0.3989422804014327
+            act[step, :, cols] = (inner * cdf).astype(BF16)
+        x3 = x2 + mm(act[step], w_fo[...])
         for side in range(2):
-            spot = pl.ds(side * TOK, TOK)
-            x0 = x0s[:, :, side].reshape(TOK, C)
-            xhat, rstd, normed = norm_forward(x0, gain_a)
-            xh_a[step, spot, :] = xhat
-            rs_a[step, spot, :] = rstd
-            no_a[step, spot, :] = normed
-            qkv = mm(normed, w_sq[...]).astype(BF16)
-            qkv_a[step, spot, :] = qkv
-            mixed = []
-            for view in range(VIEWS):
-                lines = slice(view * WIN * WIN, (view + 1) * WIN * WIN)
-                scores = mm_nt(qkv[lines, :C], qkv[lines, C : 2 * C]) * (SCALE * LOG2E)
-                expo = jnp.exp2(scores - jnp.max(scores, -1, keepdims=True))
-                probs = (expo * (1.0 / jnp.sum(expo, -1, keepdims=True))).astype(BF16)
-                p_a[step, pl.ds(side * TOK + view * WIN * WIN, WIN * WIN), :] = probs
-                mixed.append(mm(probs, qkv[lines, 2 * C :]))
-            mixed = jnp.concatenate(mixed, 0).astype(BF16)
-            o_a[step, spot, :] = mixed
-            x1 = x0 + mm(mixed, w_so[...])
-            xhat, rstd, normed = norm_forward(x1, gain_b)
-            xh_b[step, spot, :] = xhat
-            rs_b[step, spot, :] = rstd
-            no_b[step, spot, :] = normed
-            qkv = mm(normed, w_cq[...]).astype(BF16)
-            qkv_b[step, spot, :] = qkv
-            scores = mm_nt(qkv[:, :C], qkv[:, C : 2 * C]) * (SCALE * LOG2E) + bias[...]
-            expo = jnp.exp2(scores - jnp.max(scores, -1, keepdims=True))
-            probs = (expo * (1.0 / jnp.sum(expo, -1, keepdims=True))).astype(BF16)
-            p_b[step, spot, :] = probs
-            mixed = mm(probs, qkv[:, 2 * C :]).astype(BF16)
-            o_b[step, spot, :] = mixed
-            x2 = x1 + mm(mixed, w_co[...])
-            xhat, rstd, normed = norm_forward(x2, gain_c)
-            xh_c[step, spot, :] = xhat
-            rs_c[step, spot, :] = rstd
-            no_c[step, spot, :] = normed
-            x3 = x2
-            for block in range(FFH // C):
-                cols = slice(block * C, (block + 1) * C)
-                inner = mm(normed, w_fi[:, cols])
-                t = 1.0 / (1.0 + (ERF_P * 0.5**0.5) * jnp.abs(inner))
-                bell = jnp.exp2(inner * inner * (-0.5 * LOG2E))
-                poly = 0.5 * ERF_C[5] * t + 0.5 * ERF_C[4]
-                for coef in ERF_C[3::-1]:
-                    poly = poly * t + 0.5 * coef
-                tail = poly * t * bell
-                cdf = jnp.where(inner >= 0.0, 1.0 - tail, tail)
-                active = (inner * cdf).astype(BF16)
-                gd[step, spot, cols] = cdf + inner * bell * 0.3989422804014327
-                act[step, spot, cols] = active
-                x3 = x3 + mm(active, w_fo[cols, :])
-            x3s[scene, :, half, :, side] = x3.reshape(VIEWS, WIN, WIN, C)
+            x3s[scene, :, half, :, side] = x3[places[side]].reshape(VIEWS, WIN, WIN, C)
         return carry
 
     lax.fori_loop(0, scenes * halves, forward, 0)
 
-    row = iota((HALF, HALF), 0)
-    lane = iota((HALF, HALF), 1)
-    flip = (row + lane == HALF - 1).astype(BF16)
-    eye = row == lane
-    skew_keep = jnp.where((lane < HV) & (lane <= row % HV), 0.5 * SCALE, 0.0)
-    back_keep = jnp.where((lane < HV) & (HV - 1 - lane <= row % HV), 0.5 * SCALE, 0.0)
-    column = iota((PIX, C), 0) % HV
-    not_first = column > 0
-    not_last = column < HV - 1
+    row = iota((HV, C), 0)
+    lane = iota((HV, C), 1)
+    tables[0:HV, :] = jnp.where((lane < HV) & (lane <= row), 0.5 * SCALE, 0.0)
+    tables[HV : 2 * HV, :] = jnp.where((lane < HV) & (HV - 1 - lane <= row), 0.5 * SCALE, 0.0)
+    tables[2 * HV : 3 * HV, :] = jnp.where(row > 0, 1.0, 0.0)
+    tables[3 * HV : 4 * HV, :] = jnp.where(row < HV - 1, 1.0, 0.0)
+    eye[...] = jnp.where(iota((HALF, HALF), 0) == iota((HALF, HALF), 1), 1.0, 0.0)
+    flip[...] = (iota((HALF, HALF), 0) + iota((HALF, HALF), 1) == HALF - 1).astype(BF16)
+    hots[...] = jnp.zeros_like(hots)
     depth_values = 1.0 + 3.0 * iota((1, PLANES), 1).astype(F32) / (PLANES - 1)
-
-    def im2col(value, pad, dest):
+    upper = [slice(part * HALF, (part + 1) * HALF) for part in range(2)]
+    views = range(VIEWS)
+
+    def by_row(value, table):
+        return (value.reshape(-1, HV, C) * table).reshape(value.shape)
+
+    def im2col(value, pad, dest, first, last):
         pad[8 : 8 + PIX, :] = value
         dest[HV : HV + PIX, C : 2 * C] = value.astype(BF16)
-        before = jnp.where(not_first, pad[7 : 7 + PIX, :], 0.0).astype(BF16)
-        after = jnp.where(not_last, pad[9 : 9 + PIX, :], 0.0).astype(BF16)
-        return before, after
+        before = by_row(pad[7 : 7 + PIX, :], tables[2 * HV : 3 * HV, :])
+        after = by_row(pad[9 : 9 + PIX, :], tables[3 * HV : 4 * HV, :])
+        dest[HV : HV + PIX, first * C : (first + 1) * C] = before.astype(BF16)
+        dest[HV : HV + PIX, last * C : (last + 1) * C] = after.astype(BF16)
 
     def head(scene, carry):
         live = count_ref[scene]
-        for view in range(VIEWS):
-            piece = x3s[scene, view].reshape(PIX, C).astype(BF16)
-            low[view] = piece
-            for part in range(2):
-                lines = slice(part * HALF, (part + 1) * HALF)
-                rev[view, lines, :] = mm(flip, piece[lines]).astype(BF16)
-        d3s[scene] = jnp.zeros(d3s.shape[1:], F32)
-        for view in range(VIEWS):
-            partner = jnp.where(view + 1 < live, view + 1, 0)
+        goes_on = {1: live > 2, 2: live > 3}
+
+        def partner_of(ref, view, at):
+            if view in goes_on:
+                return jnp.where(goes_on[view], ref[view + 1, at, :], ref[0, at, :])
+            return ref[(view + 1) % VIEWS, at, :]
+
+        for view in views:
+            low[view] = x3s[scene, view].reshape(PIX, C).astype(BF16)
             shift = offsets[scene, view : view + 1, :]
-            hot = (shift == row).astype(BF16)
-            hot_back = (shift == HV - 1 - row).astype(BF16)
-            skewed = []
-            for part in range(2):
-                lines = slice(part * HALF, (part + 1) * HALF)
-                corr = mm_nt(low[view, lines, :], rev[partner, lines, :])
-                skewed.append(pltpu.roll(corr, 1, 1, stride=1, stride_axis=0) * skew_keep)
-            cost = mm(split_two(jnp.concatenate(skewed, 0)), jnp.concatenate([hot, hot], 0))
-            before, after = im2col(cost, pads.at[0, view], taps.at[view])
-            taps[view, HV : HV + PIX, :C] = before
-            taps[view, HV : HV + PIX, 2 * C :] = after
-            columns = jnp.concatenate([taps[view, HV * a : HV * a + PIX, :] for a in range(3)], -1)
-            refined = cost + mm(columns, t_rf[...])
-            expo = jnp.exp2((refined - jnp.max(refined, -1, keepdims=True)) * LOG2E)
+            hots[0, view, 0:HV, :] = (shift == row).astype(BF16)
+            hots[0, view, C : C + HV, :] = (shift == row).astype(BF16)
+            hots[1, view, 0:HV, :] = (shift == HV - 1 - row).astype(BF16)
+        for view in views:
+            for at in upper:
+                rev[view, at, :] = mm(flip[...], low[view, at, :]).astype(BF16)
+        corrs = [[mm_nt(low[view, at, :], partner_of(rev, view, at)) for at in upper] for view in views]
+        skewed = [
+            [by_row(pltpu.roll(corr, 1, 1, stride=1, stride_axis=0), tables[0:HV, :]) for corr in corrs[view]]
+            for view in views
+        ]
+        cost = [mm(split_two(jnp.concatenate(skewed[view], 0)), hots[0, view]) for view in views]
+        for view in views:
+            im2col(cost[view], pads.at[0, view], taps.at[view], 0, 2)
+        refined = [
+            cost[view]
+            + mm(
+                jnp.concatenate([taps[view, HV * a : HV * a + PIX, :] for a in range(3)], -1),
+                t_rf[...],
+            )
+            for view in views
+        ]
+        d_refined = []
+        for view in views:
+            expo = jnp.exp2((refined[view] - jnp.max(refined[view], -1, keepdims=True)) * LOG2E)
             inverse = 1.0 / jnp.sum(expo, -1, keepdims=True)
             depth = jnp.sum(expo * depth_values, -1, keepdims=True) * inverse
             valid = jnp.where(view < live, 1.0, 0.0)
             incoming = []
-            for part in range(2):
-                lines = slice(part * HALF, (part + 1) * HALF)
-                depth_out[scene, view : view + 1, lines] = (
-                    jnp.sum(jnp.where(eye, depth[lines], 0.0), 0, keepdims=True) * valid
-                )
-                incoming.append(
-                    jnp.sum(jnp.where(eye, depth_grad[scene, view : view + 1, lines], 0.0), 1, keepdims=True)
-                )
+            for at in upper:
+                depth_out[scene, view : view + 1, at] = jnp.sum(eye[...] * depth[at], 0, keepdims=True) * valid
+                incoming.append(jnp.sum(eye[...] * depth_grad[scene, view : view + 1, at], 1, keepdims=True))
             weight = jnp.concatenate(incoming, 0) * (inverse * valid)
-            d_refined = expo * (weight * depth_values - weight * depth)
-            before, after = im2col(d_refined, pads.at[1, view], back_taps.at[view])
-            back_taps[view, HV : HV + PIX, :C] = after
-            back_taps[view, HV : HV + PIX, 2 * C :] = before
+            d_refined.append(expo * (weight * depth_values - weight * depth))
+        for view in views:
+            im2col(d_refined[view], pads.at[1, view], back_taps.at[view], 2, 0)
+        d_cost = [
+            d_refined[view]
+            + mm(
+                jnp.concatenate([back_taps[view, HV * (2 - a) : HV * (2 - a) + PIX, :] for a in range(3)], -1),
+                b_rf[...],
+            )
+            for view in views
+        ]
+        for view in views:
+            columns = jnp.concatenate([taps[view, HV * a : HV * a + PIX, :] for a in range(3)], -1)
             g_rf[...] += mm_tn(back_taps[view, HV : HV + PIX, C : 2 * C], columns)
-            d_cost = d_refined
-            for a in range(3):
-                shifted = back_taps[view, HV * (2 - a) : HV * (2 - a) + PIX, :]
-                for b in range(3):
-                    tap = 3 * a + b
-                    d_cost = d_cost + mm(shifted[:, b * C : (b + 1) * C], w_rf[:, tap * C : (tap + 1) * C])
-            d_skewed = mm_nt(split_two(d_cost), jnp.concatenate([hot_back, hot_back], -1))
-            for part in range(2):
-                lines = slice(part * HALF, (part + 1) * HALF)
-                d_corr = pltpu.roll(
-                    d_skewed[lines] * back_keep, HALF - HV + 1, 1, stride=1, stride_axis=0
+        d_skewed = [
+            mm_nt(split_two(d_cost[view]), jnp.concatenate([hots[1, view, :C, :]] * 2, -1)) for view in views
+        ]
+        d_corr = [
+            [
+                pltpu.roll(
+                    by_row(d_skewed[view][at], tables[HV : 2 * HV, :]), HALF - HV + 1, 1, stride=1, stride_axis=0
                 ).astype(BF16)
-                shape = (WIN, 2, WIN, C)
-                d3s[scene, view, part] += mm(d_corr, low[partner, lines, :]).reshape(shape)
-                d3s[scene, partner, part] += mm_tn(d_corr, low[view, lines, :]).reshape(shape)
+                for at in upper
+            ]
+            for view in views
+        ]
+        for part in range(2):
+            at = upper[part]
+            total = [mm(d_corr[view][part], partner_of(low, view, at)) for view in views]
+            for view in views:
+                there = mm_tn(d_corr[view][part], low[view, at, :])
+                if view in goes_on:
+                    total[view + 1] = total[view + 1] + jnp.where(goes_on[view], there, 0.0)
+                    total[0] = total[0] + jnp.where(goes_on[view], 0.0, there)
+                else:
+                    total[(view + 1) % VIEWS] = total[(view + 1) % VIEWS] + there
+            for view in views:
+                d3s[scene, view, part] = total[view].reshape(WIN, 2, WIN, C)
         return carry
 
     lax.fori_loop(0, scenes, head, 0)
+
+    def soft_back(probs, d_probs):
+        probs = probs.astype(F32)
+        delta = jnp.sum(d_probs * probs, -1, keepdims=True)
+        return (probs * ((d_probs - delta) * SCALE)).astype(BF16)
 
     def backward(step, carry):
         scene = step // halves
         half = step % halves
+        d3 = jnp.concatenate([d3s[scene, :, half, :, side].reshape(TOK, C) for side in range(2)], 0)
+        d_low = d3.astype(BF16)
+        d_inners = []
+        for block in range(FFH // C):
+            cols = slice(block * C, (block + 1) * C)
+            d_inners.append((mm(d_low, t_fo[:, cols]) * gd[step, :, cols]).astype(BF16))
+        d_inner = jnp.concatenate(d_inners, -1)
+        d_normed = mm(d_inner, t_fi[...])
+        g_fo[...] += mm_tn(d_low, act[step])
+        g_fi[...] += mm_tn(no_c[step], d_inner)
+        d_hidden, d_gain = norm_backward(d_normed, xh_c[step], rs_c[step], gain_c)
+        g_gain[2] += d_gain
+        d2 = d3 + d_hidden
+        d_low = d2.astype(BF16)
+        qkv = qkv_b[step]
+        d_mixed = mm(d_low, t_co[...]).astype(BF16)
+        g_co[...] += mm_tn(o_b[step], d_low)
+        probs = p_b[step]
+        d_values = jnp.concatenate([mm_tn(probs[at], d_mixed[at]) for at in places], 0)
+        d_probs = jnp.concatenate([mm_nt(d_mixed[at], qkv[at, 2 * C :]) for at in places], 0)
+        d_raw = soft_back(probs, d_probs)
+        d_query = jnp.concatenate([mm(d_raw[at], qkv[at, C : 2 * C]) for at in places], 0)
+        d_keys = jnp.concatenate([mm_tn(d_raw[at], qkv[at, :C]) for at in places], 0)
+        d_packed = jnp.concatenate([d_query, d_keys, d_values], -1).astype(BF16)
+        d_normed = mm(d_packed, t_cq[...])
+        g_cq[...] += mm_tn(no_b[step], d_packed)
+        d_hidden, d_gain = norm_backward(d_normed, xh_b[step], rs_b[step], gain_b)
+        g_gain[1] += d_gain
+        d1 = d2 + d_hidden
+        d_low = d1.astype(BF16)
+        qkv = qkv_a[step]
+        d_mixed = mm(d_low, t_so[...]).astype(BF16)
+        g_so[...] += mm_tn(o_a[step], d_low)
+        probs = p_a[step]
+        d_values = jnp.concatenate([mm_tn(probs[at], d_mixed[at]) for at in windows], 0)
+        d_probs = jnp.concatenate([mm_nt(d_mixed[at], qkv[at, 2 * C :]) for at in windows], 0)
+        d_raw = soft_back(probs, d_probs)
+        d_query = jnp.concatenate([mm(d_raw[at], qkv[at, C : 2 * C]) for at in windows], 0)
+        d_keys = jnp.concatenate([mm_tn(d_raw[at], qkv[at, :C]) for at in windows], 0)
+        d_packed = jnp.concatenate([d_query, d_keys, d_values], -1).astype(BF16)
+        d_normed = mm(d_packed, t_sq[...])
+        g_sq[...] += mm_tn(no_a[step], d_packed)
+        d_hidden, d_gain = norm_backward(d_normed, xh_a[step], rs_a[step], gain_a)
+        g_gain[0] += d_gain
+        d0 = d1 + d_hidden
         for side in range(2):
-            spot = pl.ds(side * TOK, TOK)
-            d3 = d3s[scene, :, half, :, side].reshape(TOK, C)
-            d_low = d3.astype(BF16)
-            normed = no_c[step, spot, :]
-            g_fo[...] += mm_tn(d_low, act[step, spot, :])
-            d_normed = jnp.zeros((TOK, C), F32)
-            d_inners = []
-            for block in range(FFH // C):
-                cols = slice(block * C, (block + 1) * C)
-                d_inner = (mm(d_low, t_fo[:, cols]) * gd[step, spot, cols]).astype(BF16)
-                d_inners.append(d_inner)
-            d_inner = jnp.concatenate(d_inners, -1)
-            g_fi[...] += mm_tn(normed, d_inner)
-            d_normed = mm(d_inner, t_fi[...])
-            d_hidden, d_gain = norm_backward(d_normed, xh_c[step, spot, :], rs_c[step, spot, :], gain_c)
-            g_gain[2] += d_gain
-            d2 = d3 + d_hidden
-            d_low = d2.astype(BF16)
-            qkv = qkv_b[step, spot, :]
-            g_co[...] += mm_tn(o_b[step, spot, :], d_low)
-            d_mixed = mm(d_low, t_co[...]).astype(BF16)
-            probs = p_b[step, spot, :]
-            d_values = mm_tn(probs, d_mixed)
-            d_probs = mm_nt(d_mixed, qkv[:, 2 * C :])
-            probs = probs.astype(F32)
-            delta = jnp.sum(d_probs * probs, -1, keepdims=True)
-            d_raw = (probs * ((d_probs - delta) * SCALE)).astype(BF16)
-            d_query = mm(d_raw, qkv[:, C : 2 * C])
-            d_keys = mm_tn(d_raw, qkv[:, :C])
-            d_packed = jnp.concatenate([d_query, d_keys, d_values], -1).astype(BF16)
-            g_cq[...] += mm_tn(no_b[step, spot, :], d_packed)
-            d_normed = mm(d_packed, t_cq[...])
-            d_hidden, d_gain = norm_backward(d_normed, xh_b[step, spot, :], rs_b[step, spot, :], gain_b)
-            g_gain[1] += d_gain
-            d1 = d2 + d_hidden
-            d_low = d1.astype(BF16)
-            qkv = qkv_a[step, spot, :]
-            g_so[...] += mm_tn(o_a[step, spot, :], d_low)
-            d_mixed = mm(d_low, t_so[...]).astype(BF16)
-            pieces = []
-            for view in range(VIEWS):
-                lines = slice(view * WIN * WIN, (view + 1) * WIN * WIN)
-                probs = p_a[step, pl.ds(side * TOK + view * WIN * WIN, WIN * WIN), :]
-                d_values = mm_tn(probs, d_mixed[lines])
-                d_probs = mm_nt(d_mixed[lines], qkv[lines, 2 * C :])
-                probs = probs.astype(F32)
-                delta = jnp.sum(d_probs * probs, -1, keepdims=True)
-                d_raw = (probs * ((d_probs - delta) * SCALE)).astype(BF16)
-                d_query = mm(d_raw, qkv[lines, C : 2 * C])
-                d_keys = mm_tn(d_raw, qkv[lines, :C])
-                pieces.append(jnp.concatenate([d_query, d_keys, d_values], -1))
-            d_packed = jnp.concatenate(pieces, 0).astype(BF16)
-            g_sq[...] += mm_tn(no_a[step, spot, :], d_packed)
-            d_normed = mm(d_packed, t_sq[...])
-            d_hidden, d_gain = norm_backward(d_normed, xh_a[step, spot, :], rs_a[step, spot, :], gain_a)
-            g_gain[0] += d_gain
-            grad_out[scene, :, half, :, side] = (d1 + d_hidden).reshape(VIEWS, WIN, WIN, C)
+            grad_out[scene, :, half, :, side] = d0[places[side]].reshape(VIEWS, WIN, WIN, C)
         return carry
 
     lax.fori_loop(0, scenes * halves, backward, 0)
@@ -476,7 +502,7 @@
         ((C, 3 * C), BF16), ((C, C), BF16), ((C, 3 * C), BF16), ((C, C), BF16),
         ((C, FFH), BF16), ((FFH, C), BF16), ((C, 9 * PLANES), BF16),
         ((3 * C, C), BF16), ((C, C), BF16), ((3 * C, C), BF16), ((C, C), BF16),
-        ((FFH, C), BF16), ((C, FFH), BF16), ((9 * PLANES, C), BF16),
+        ((FFH, C), BF16), ((C, FFH), BF16), ((9 * PLANES, C), BF16), ((9 * PLANES, C), BF16),
         ((8, C), F32),
         ((TOK, TOK), F32),
         ((VIEWS, WIN, 2, WIN, C), F32),
@@ -492,6 +518,7 @@
         ((VIEWS, PIX, C), BF16), ((VIEWS, PIX, C), BF16),
         ((2, VIEWS, PIX + 16, C), F32),
         ((VIEWS, PIX + 2 * HV, 3 * C), BF16), ((VIEWS, PIX + 2 * HV, 3 * C), BF16),
+        ((4 * HV, C), F32), ((HALF, HALF), F32), ((HALF, HALF), BF16), ((2, VIEWS, 2 * C, C), BF16),
         ((C, 3 * C), F32), ((C, C), F32), ((C, 3 * C), F32), ((C, C), F32),
         ((C, FFH), F32), ((C, FFH), F32), ((C, 9 * PLANES), F32), ((3, 8, C), F32),
     ]

time: 116 us -> 84.9 us (0.73)
  Pallas kernels: 69.1 us -> 38.1 us
    pallas_call x1, Pallas kernels: 65.4 us -> 34.4 us  [local(): main(view_count, index, features, plane_offsets, depth_grad, packed)]
where the time goes in v1:
time: 84.9 us; the launch traced here: 84.6 us
  Pallas kernels  38.1 us (45%)
  waiting for transfers between devices  25.4 us (30%)
  blocking collectives  11.9 us (14%)
  starting transfers between devices  6.48 us (8%)
  local copies, waits for them, and re-layouts  1.8 us (2%)
    pallas_call x1, Pallas kernels, local(): main(view_count, index, features, plane_offsets, depth_grad, packed)  34.4 us
    ppermute x5, waiting for transfers between devices, exchange(): return lax.ppermute(value, axis, [(i, i ^ 1 << bit) for i in range(size)])  25.4 us
    all_gather x1, blocking collectives, local(): packed = lax.all_gather(shard, 'fsdp', axis=0)  11.9 us
    ppermute x5, starting transfers between devices, exchange(): return lax.ppermute(value, axis, [(i, i ^ 1 << bit) for i in range(size)])  6.48 us
    pallas_call x1, Pallas kernels, local(): pack(index, gain_self.reshape(1, rows), gain_cross.reshape(1, rows), gain...  1.85 us
    pallas_call x1, Pallas kernels, local(): unpack(index, grads, other)  1.84 us
  transfers between devices with their start and end apart: 5, of which 5 were waited for; matrix products, arithmetic and copies ran while one was open for 0% of the time, Pallas kernels for 0%

profile of v1, /device:TPU:0, one launch (start us, length us, event | category | flops | bytes accessed | tf_op | source)
XLA Modules:
  0.0 84.6 jit_solution(15480219968837896847)
XLA Ops:
  0.7 1.9 %pack.1 = bf16[816,128]{1,0:T(8,128)(2,1)} custom-call(s32[1]{0:T(128)} %bitcast.index_ref, bf16[1,32]{1,0:T(2,128)(2,1)} %bitcast.12, bf16[1,32]{1,0:T(2,128)(2,1)} %bitcast.13, bf16[1,32]{1,0:T(2,128)(2,1)} %bitcast.14, bf16[32,384]{1,0:T(8,128)(2,1)} %refs_3_.1, bf16[32,128]{1,0:T(8,128)(2,1)} %refs_4_.1, bf16[32,384]{1,0:T(8,128)(2,1)} %refs_5_.1, ...), custom_call_target="tpu_custom_call" | custom-call | tf_op jit(solution)/shard_map/pack/pallas_call | solution.py:484
  2.5 11.9 %all-gather = bf16[3264,128]{1,0:T(8,128)(2,1)} all-gather(bf16[816,128]{1,0:T(8,128)(2,1)} %pack.1), channel_id=2, replica_groups=mesh['dp'=8,'fsdp'=4] {'fsdp'}, dimensions={0}, use_global_device_ids=true | all-gather | bytes 1044480 | tf_op jit(solution)/shard_map/all_gather | solution.py:497
  14.4 34.4 %layer.1 = (f32[2,4,256]{2,1,0:T(4,128)}, f32[2,4,2,8,2,8,128]{6,5,4,3,2,1,0:T(8,128)}, bf16[4,816,128]{2,1,0:T(8,128)(2,1)}) custom-call(s32[2]{0:T(128)} %count_ref.1, s32[1]{0:T(128)} %bitcast.index_ref, bf16[2,4,256,128]{3,2,1,0:T(8,128)(2,1)} %features.1, s32[2,4,128]{2,1,0:T(4,128)} %offsets.1, f32[2,4,256]{2,1,0:T(4,128)} %depth_grad.1, ...), custom_call_target="tpu_custom_call" | custom-call | tf_op jit(solution)/shard_map/layer/pallas_call | solution.py:538
  48.9 0.0 copy-start
  48.9 1.1 %slice.13 = bf16[2,816,128]{2,1,0:T(8,128)(2,1)S(1)} slice(bf16[4,816,128]{2,1,0:T(8,128)(2,1)} %get-tuple-element.27), slice={[2:4], [0:816], [0:128]} | slice | bytes 835584 | tf_op jit(solution)/shard_map/slice | solution.py:542
  50.0 0.4 collective-permute-start
  50.4 1.4 %collective-permute-done = bf16[2,816,128]{2,1,0:T(8,128)(2,1)S(1)} collective-permute-done((bf16[2,816,128]{2,1,0:T(8,128)(2,1)S(1)}, bf16[2,816,128]{2,1,0:T(8,128)(2,1)S(1)}, u32[]{:S(2)}, u32[]{:S(2)}) %collective-permute-start) | collective-permute-done | bytes 417824 | tf_op jit(solution)/shard_map/ppermute | solution.py:449
  51.8 0.0 copy-done
  51.8 0.1 slice_add_fusion
  51.9 0.2 collective-permute-start.1
  52.1 7.3 %collective-permute-done.1 = bf16[1,816,128]{2,1,0:T(8,128)(2,1)S(1)} collective-permute-done((bf16[1,816,128]{2,1,0:T(8,128)(2,1)S(1)}, bf16[1,816,128]{2,1,0:T(8,128)(2,1)S(1)}, u32[]{:S(2)}, u32[]{:S(2)}) %collective-permute-start.1) | collective-permute-done | bytes 208928 | tf_op jit(solution)/shard_map/ppermute | solution.py:449
  59.4 1.6 %collective-permute-start.2 = (bf16[816,128]{1,0:T(8,128)(2,1)S(1)}, bf16[816,128]{1,0:T(8,128)(2,1)S(1)}, u32[]{:S(2)}, u32[]{:S(2)}) collective-permute-start(bf16[816,128]{1,0:T(8,128)(2,1)S(1)} %fusion), channel_id=1, source_target_pairs={{0,4},{4,0},{8,12},{12,8},{16,20},{20,16},{24,28},{28,24},{1,5},{5... | collective-permute-start | bytes 626696 | tf_op jit(solution)/shard_map/ppermute | solution.py:449
  61.0 5.1 %collective-permute-done.2 = bf16[816,128]{1,0:T(8,128)(2,1)S(1)} collective-permute-done((bf16[816,128]{1,0:T(8,128)(2,1)S(1)}, bf16[816,128]{1,0:T(8,128)(2,1)S(1)}, u32[]{:S(2)}, u32[]{:S(2)}) %collective-permute-start.2) | collective-permute-done | bytes 208928 | tf_op jit(solution)/shard_map/ppermute | solution.py:449
  66.1 0.1 add.14
  66.1 1.6 %collective-permute-start.3 = (bf16[816,128]{1,0:T(8,128)(2,1)S(1)}, bf16[816,128]{1,0:T(8,128)(2,1)S(1)}, u32[]{:S(2)}, u32[]{:S(2)}) collective-permute-start(bf16[816,128]{1,0:T(8,128)(2,1)S(1)} %add.14), channel_id=1, source_target_pairs={{0,8},{4,12},{8,0},{12,4},{16,24},{20,28},{24,16},{28,20},{1,9},{5... | collective-permute-start | bytes 626696 | tf_op jit(solution)/shard_map/ppermute | solution.py:449
  67.8 4.2 %collective-permute-done.3 = bf16[816,128]{1,0:T(8,128)(2,1)S(1)} collective-permute-done((bf16[816,128]{1,0:T(8,128)(2,1)S(1)}, bf16[816,128]{1,0:T(8,128)(2,1)S(1)}, u32[]{:S(2)}, u32[]{:S(2)}) %collective-permute-start.3) | collective-permute-done | bytes 208928 | tf_op jit(solution)/shard_map/ppermute | solution.py:449
  72.0 0.1 add.15.left
  72.1 0.0 copy-start.1
  72.1 2.7 %collective-permute-start.4 = (bf16[816,128]{1,0:T(8,128)(2,1)S(1)}, bf16[816,128]{1,0:T(8,128)(2,1)S(1)}, u32[]{:S(2)}, u32[]{:S(2)}) collective-permute-start(bf16[816,128]{1,0:T(8,128)(2,1)S(1)} %add.15.left), channel_id=1, source_target_pairs={{0,16},{4,20},{8,24},{12,28},{16,0},{20,4},{24,8},{28,12},{1,17},{... | collective-permute-start | bytes 626696 | tf_op jit(solution)/shard_map/ppermute | solution.py:449
  74.7 7.3 %collective-permute-done.4.right = bf16[816,128]{1,0:T(8,128)(2,1)S(1)} collective-permute-done((bf16[816,128]{1,0:T(8,128)(2,1)S(1)}, bf16[816,128]{1,0:T(8,128)(2,1)S(1)}, u32[]{:S(2)}, u32[]{:S(2)}) %collective-permute-start.4) | collective-permute-done | bytes 208928 | tf_op jit(solution)/shard_map/ppermute | solution.py:449
  82.1 0.0 copy-done.1
  82.1 0.0 copy-start.2
  82.1 0.7 copy-done.2
  82.8 1.8 %unpack.1 = (f32[1,32]{1,0:T(1,128)}, f32[1,32]{1,0:T(1,128)}, f32[1,32]{1,0:T(1,128)}, f32[32,384]{1,0:T(8,128)}, f32[32,128]{1,0:T(8,128)}, /*index=5*/f32[32,...) custom-call(s32[1]{0:T(128)} %bitcast.index_ref, ...), custom_call_target="tpu_custom_call" | custom-call | tf_op jit(solution)/shard_map/unpack/pallas_call | solution.py:561
  (2 shorter events, 0.0 us)
Async XLA Ops:
  48.9 2.9 %copy-start = (bf16[4,816,128]{2,1,0:T(8,128)(2,1)S(1)}, bf16[4,816,128]{2,1,0:T(8,128)(2,1)}, u32[]{:S(2)}) copy-start(bf16[4,816,128]{2,1,0:T(8,128)(2,1)} %get-tuple-element.27) | copy-start | bytes 2506756
  50.0 1.8 %collective-permute-start = (bf16[2,816,128]{2,1,0:T(8,128)(2,1)S(1)}, bf16[2,816,128]{2,1,0:T(8,128)(2,1)S(1)}, u32[]{:S(2)}, u32[]{:S(2)}) collective-permute-start(bf16[2,816,128]{2,1,0:T(8,128)(2,1)S(1)} %slice.13), channel_id=1, source_target_pairs={{0,1},{1,0},{2,3},{3,2},{4,5},{5,4},{6,7},{7,6},{8,9},{9,8},{10,11... | collective-permute-start | bytes 1253384 | tf_op jit(solution)/shard_map/ppermute | solution.py:449
  51.9 7.5 %collective-permute-start.1 = (bf16[1,816,128]{2,1,0:T(8,128)(2,1)S(1)}, bf16[1,816,128]{2,1,0:T(8,128)(2,1)S(1)}, u32[]{:S(2)}, u32[]{:S(2)}) collective-permute-start(bf16[1,816,128]{2,1,0:T(8,128)(2,1)S(1)} %slice.17), channel_id=1, source_target_pairs={{0,2},{1,3},{2,0},{3,1},{4,6},{5,7},{6,4},{7,5},{8,10},{9,11},{10,... | collective-permute-start | bytes 626696 | tf_op jit(solution)/shard_map/ppermute | solution.py:449
  59.4 6.7 %collective-permute-start.2 = (bf16[816,128]{1,0:T(8,128)(2,1)S(1)}, bf16[816,128]{1,0:T(8,128)(2,1)S(1)}, u32[]{:S(2)}, u32[]{:S(2)}) collective-permute-start(bf16[816,128]{1,0:T(8,128)(2,1)S(1)} %fusion), channel_id=1, source_target_pairs={{0,4},{4,0},{8,12},{12,8},{16,20},{20,16},{24,28},{28,24},{1,5},{5... | collective-permute-start | bytes 626696 | tf_op jit(solution)/shard_map/ppermute | solution.py:449
  66.1 5.9 %collective-permute-start.3 = (bf16[816,128]{1,0:T(8,128)(2,1)S(1)}, bf16[816,128]{1,0:T(8,128)(2,1)S(1)}, u32[]{:S(2)}, u32[]{:S(2)}) collective-permute-start(bf16[816,128]{1,0:T(8,128)(2,1)S(1)} %add.14), channel_id=1, source_target_pairs={{0,8},{4,12},{8,0},{12,4},{16,24},{20,28},{24,16},{28,20},{1,9},{5... | collective-permute-start | bytes 626696 | tf_op jit(solution)/shard_map/ppermute | solution.py:449
  72.1 10.0 %copy-start.1 = (bf16[816,128]{1,0:T(8,128)(2,1)}, bf16[816,128]{1,0:T(8,128)(2,1)S(1)}, u32[]{:S(2)}) copy-start(bf16[816,128]{1,0:T(8,128)(2,1)S(1)} %add.15.left) | copy-start | bytes 626692
  72.1 10.0 %collective-permute-start.4 = (bf16[816,128]{1,0:T(8,128)(2,1)S(1)}, bf16[816,128]{1,0:T(8,128)(2,1)S(1)}, u32[]{:S(2)}, u32[]{:S(2)}) collective-permute-start(bf16[816,128]{1,0:T(8,128)(2,1)S(1)} %add.15.left), channel_id=1, source_target_pairs={{0,16},{4,20},{8,24},{12,28},{16,0},{20,4},{24,8},{28,12},{1,17},{... | collective-permute-start | bytes 626696 | tf_op jit(solution)/shard_map/ppermute | solution.py:449
  82.1 0.7 copy-start.2

commit v2 on v1

v2 whole, which is shorter than its diff:
```python
import functools

import jax
import jax.numpy as jnp
from jax import lax
from jax.experimental import pallas as pl
from jax.experimental.pallas import tpu as pltpu
from jax.sharding import PartitionSpec as P

C = 128
FFH = 512
PLANES = 128
WIN = 8
VIEWS = 4
HV = 16
PIX = HV * HV
TOK = VIEWS * WIN * WIN
HALF = PIX // 2
GAIN_ROWS = 16
MASKED = -1e30
SCALE = C**-0.5
LOG2E = 1.4426950408889634
F32 = jnp.float32
BF16 = jnp.bfloat16
BLOCKS = (3, 1, 3, 1, 4, 4, 9)
MIB = 1024 * 1024

ERF_P = 0.39
ERF_C = (0.23532522, 0.09138841, 0.6495594, -0.63540028, 0.88666437, -0.22753713)


def mm(left, right):
    return lax.dot_general(left, right, (((1,), (0,)), ((), ())), preferred_element_type=F32)


def mm_nt(left, right):
    return lax.dot_general(left, right, (((1,), (1,)), ((), ())), preferred_element_type=F32)


def mm_tn(left, right):
    return lax.dot_general(left, right, (((0,), (0,)), ((), ())), preferred_element_type=F32)


def norm_forward(value, gain):
    centred = value - jnp.mean(value, -1, keepdims=True)
    spread = jnp.mean(centred * centred, -1, keepdims=True)
    rstd = lax.rsqrt(spread + 1e-05)
    xhat = centred * rstd
    return xhat, jnp.broadcast_to(rstd, value.shape), (xhat * gain).astype(BF16)


def norm_backward(d_normed, xhat, rstd, gain):
    d_xhat = d_normed * gain
    mean_d = jnp.mean(d_xhat, -1, keepdims=True)
    mean_dx = jnp.mean(d_xhat * xhat, -1, keepdims=True)
    d_gain = jnp.sum((d_normed * xhat).reshape(-1, 8, C), 0)
    return rstd * (d_xhat - mean_d - xhat * mean_dx), d_gain


def split_two(value):
    high = value.astype(BF16)
    return jnp.concatenate([high, (value - high.astype(F32)).astype(BF16)], -1)


def iota(shape, axis):
    return lax.broadcasted_iota(jnp.int32, shape, axis)


def bits_of(size):
    return size.bit_length() - 1


def rows_of(parts):
    return -(-(sum(BLOCKS) * (C // parts) + GAIN_ROWS) // 32) * 32


def place_of(parts):
    return lax.axis_index("fsdp").astype(jnp.int32), (lax.axis_index("dp") & 1).astype(jnp.int32)


def pack_kernel(parts, *refs):
    gains, weights, out, scratch, sems = refs[:3], refs[3:10], refs[10], refs[11], refs[12]
    rows = C // parts
    copies = []

    def copy(source, target):
        copies.append(pltpu.make_async_copy(source, target, sems.at[len(copies)]))
        copies[-1].start()

    for which in range(3):
        copy(gains[which], scratch.at[which])
    at = 0
    for ref, blocks in zip(weights, BLOCKS):
        if ref.shape[0] == blocks * rows and ref.shape[1] == C:
            copy(ref, out.at[at : at + blocks * rows, :])
        else:
            for block in range(blocks):
                copy(ref.at[:, block * C : (block + 1) * C], out.at[at + block * rows : at + (block + 1) * rows, :])
        at += blocks * rows
    for one in copies[:3]:
        one.wait()
    place = (iota((rows, C), 1) == iota((rows, C), 0) + place_of(parts)[0] * rows).astype(BF16)
    line = iota((GAIN_ROWS, C), 0)
    total = jnp.zeros((GAIN_ROWS, C), F32)
    for which in range(3):
        row = mm(jnp.broadcast_to(scratch[which], (8, rows)), place)[:1]
        total = jnp.where(line == which, row, total)
    out[at : at + GAIN_ROWS, :] = total.astype(BF16)
    if at + GAIN_ROWS < out.shape[0]:
        out[at + GAIN_ROWS :, :] = jnp.zeros((out.shape[0] - at - GAIN_ROWS, C), BF16)
    for one in copies[3:]:
        one.wait()


def unpack_kernel(parts, *refs):
    terms = (len(refs) - 11) // 2
    own, other, outs = refs[:terms], refs[terms : 2 * terms], refs[2 * terms :]
    rows = C // parts
    me, side = place_of(parts)
    whole = outs[-1]
    half = own[0].shape[0]
    for first, pieces in ((side, own), (1 - side, other)):
        whole[pl.ds(pl.multiple_of(first * half, 16), half), :] = sum(piece[...].astype(F32) for piece in pieces)
    at = 0
    for out, blocks in zip(outs[3:10], BLOCKS):
        if out.shape[0] == blocks * rows and out.shape[1] == C:
            out[...] = whole[at : at + blocks * rows, :]
        else:
            for block in range(blocks):
                out[:, block * C : (block + 1) * C] = whole[at + block * rows : at + (block + 1) * rows, :]
        at += blocks * rows
    lane = iota((C, rows), 0)
    place = (lane == iota((C, rows), 1) + me * rows).astype(F32)
    picked = lax.dot_general(
        whole[at : at + GAIN_ROWS, :],
        place,
        (((1,), (0,)), ((), ())),
        precision=lax.Precision.HIGHEST,
        preferred_element_type=F32,
    )
    for which in range(3):
        outs[which][...] = picked[which : which + 1]


def merge(*threads):
    spent = [0.0] * len(threads)
    left = set(range(len(threads)))
    while left:
        which = min(left, key=lambda i: (spent[i], i))
        try:
            spent[which] += next(threads[which])
        except StopIteration:
            left.remove(which)


def paced(thread, rate):
    for share in thread:
        yield share * rate


def soft(scores):
    expo = jnp.exp2(scores - jnp.max(scores, -1, keepdims=True))
    return (expo * (1.0 / jnp.sum(expo, -1, keepdims=True))).astype(BF16)


def soft_back(probs, d_probs):
    probs = probs.astype(F32)
    delta = jnp.sum(d_probs * probs, -1, keepdims=True)
    return (probs * ((d_probs - delta) * SCALE)).astype(BF16)


def joined(pieces):
    return jnp.concatenate(pieces, 0)


def main_kernel(
    scenes,
    parts,
    count_ref,
    features_hbm,
    offsets,
    depth_grad,
    *refs,
):
    packed = refs[:parts]
    (
    depth_out,
    grad_hbm,
    keep_out,
    send_out,
    w_sq, w_so, w_cq, w_co, w_fi, w_fo, w_rf,
    t_sq, t_so, t_cq, t_co, t_fi, t_fo, t_rf, b_rf,
    gains,
    bias,
    x0s, x2s,
    xh_a, xh_b, xh_c, rs_a, rs_b, rs_c,
    no_a, no_b, no_c,
    qkv_a, qkv_b, p_a, p_b, o_a, o_b,
    gd, act,
    x3s, d3s,
    low, rev,
    pads, taps, back_taps,
    tables, eye, flip, hots,
    g_sq, g_so, g_cq, g_co, g_fi, g_fo, g_rf, g_gain,
    features, grad_out, sems,
    ) = refs[parts:]
    rows = C // parts
    me, side_of_rows = place_of(parts)
    bring = pltpu.make_async_copy(features_hbm, features, sems.at[0])
    bring.start()
    sent = []

    total = jnp.zeros((GAIN_ROWS, C), F32)
    for apart, piece in enumerate(packed):
        shard = me ^ apart
        at = 0
        for ref, blocks in zip((w_sq, w_so, w_cq, w_co, w_fi, w_fo, w_rf), BLOCKS):
            if ref is w_fo:
                spot = pl.ds(pl.multiple_of(shard * (blocks * rows), 16), blocks * rows)
                ref[spot, :] = piece[at : at + blocks * rows, :]
            else:
                spot = pl.ds(pl.multiple_of(shard * rows, 16), rows)
                for block in range(blocks):
                    ref[spot, block * C : (block + 1) * C] = piece[at + block * rows : at + (block + 1) * rows, :]
            at += blocks * rows
        total = total + piece[at : at + GAIN_ROWS, :].astype(F32)
    gains[...] = total[:8]
    for source, target in ((w_sq, t_sq), (w_so, t_so), (w_cq, t_cq), (w_co, t_co), (w_fi, t_fi), (w_rf, t_rf)):
        for block in range(source.shape[1] // C):
            target[block * C : (block + 1) * C, :] = source[:, block * C : (block + 1) * C].T
    for block in range(9):
        b_rf[block * C : (block + 1) * C, :] = w_rf[:, block * C : (block + 1) * C]
    for block in range(FFH // C):
        t_fo[:, block * C : (block + 1) * C] = w_fo[block * C : (block + 1) * C, :].T

    for ref in (g_sq, g_so, g_cq, g_co, g_fi, g_fo, g_rf, g_gain, pads, hots):
        ref[...] = jnp.zeros_like(ref)
    for ref in (taps, back_taps):
        for scene in range(scenes):
            ref[scene, :, :HV, :] = jnp.zeros((VIEWS, HV, 3 * C), BF16)
            ref[scene, :, HV + PIX :, :] = jnp.zeros((VIEWS, HV, 3 * C), BF16)

    row = iota((HV, C), 0)
    lane = iota((HV, C), 1)
    tables[0:HV, :] = jnp.where((lane < HV) & (lane <= row), 0.5 * SCALE, 0.0)
    tables[HV : 2 * HV, :] = jnp.where((lane < HV) & (HV - 1 - lane <= row), 0.5 * SCALE, 0.0)
    tables[2 * HV : 3 * HV, :] = jnp.where(row > 0, 1.0, 0.0)
    tables[3 * HV : 4 * HV, :] = jnp.where(row < HV - 1, 1.0, 0.0)
    eye[...] = jnp.where(iota((HALF, HALF), 0) == iota((HALF, HALF), 1), 1.0, 0.0)
    flip[...] = (iota((HALF, HALF), 0) + iota((HALF, HALF), 1) == HALF - 1).astype(BF16)
    of_key = iota((TOK, TOK), 1) // (WIN * WIN)
    of_query = iota((TOK, TOK), 0) // (WIN * WIN)
    for scene in range(scenes):
        live = count_ref[scene]
        bias[scene] = jnp.where((of_key < live) & (of_key != of_query), 0.0, MASKED)

    gain_a = gains[0:1, :]
    gain_b = gains[1:2, :]
    gain_c = gains[2:3, :]
    depth_values = 1.0 + 3.0 * iota((1, PLANES), 1).astype(F32) / (PLANES - 1)
    upper = [slice(part * HALF, (part + 1) * HALF) for part in range(2)]
    views = range(VIEWS)
    places = [slice(side * TOK, (side + 1) * TOK) for side in range(2)]
    windows = [slice(at * WIN * WIN, (at + 1) * WIN * WIN) for at in range(2 * VIEWS)]

    def attend(scene, half):
        step = 2 * scene + half
        piece = features[scene, :, half * HALF : (half + 1) * HALF, :]
        x0s[step] = piece.astype(F32).reshape(VIEWS, WIN, 2, WIN, C)
        x0 = joined([x0s[step, :, :, side].reshape(TOK, C) for side in range(2)])
        xhat, rstd, normed = norm_forward(x0, gain_a)
        xh_a[step] = xhat
        rs_a[step] = rstd
        no_a[step] = normed
        yield 400
        qkv = mm(normed, w_sq[...]).astype(BF16)
        qkv_a[step] = qkv
        yield 300
        scores = joined([mm_nt(qkv[at, :C], qkv[at, C : 2 * C]) for at in windows])
        yield 200
        probs = soft(scores * (SCALE * LOG2E))
        p_a[step] = probs
        yield 400
        mixed = joined([mm(probs[at], qkv[at, 2 * C :]) for at in windows]).astype(BF16)
        o_a[step] = mixed
        yield 300
        x1 = x0 + mm(mixed, w_so[...])
        yield 200
        xhat, rstd, normed = norm_forward(x1, gain_b)
        xh_b[step] = xhat
        rs_b[step] = rstd
        no_b[step] = normed
        yield 400
        qkv = mm(normed, w_cq[...]).astype(BF16)
        qkv_b[step] = qkv
        yield 300
        scores = [mm_nt(qkv[at, :C], qkv[at, C : 2 * C]) * (SCALE * LOG2E) + bias[scene] for at in places]
        yield 300
        probs = soft(joined(scores))
        p_b[step] = probs
        yield 500
        mixed = joined([mm(probs[at], qkv[at, 2 * C :]) for at in places]).astype(BF16)
        o_b[step] = mixed
        yield 300
        x2 = x1 + mm(mixed, w_co[...])
        x2s[step] = x2
        yield 200
        xhat, rstd, normed = norm_forward(x2, gain_c)
        xh_c[step] = xhat
        rs_c[step] = rstd
        no_c[step] = normed
        yield 400

    def feed(scene, half):
        step = 2 * scene + half
        for block in range(FFH // C):
            cols = slice(block * C, (block + 1) * C)
            for at in places:
                inner = mm(no_c[step, at, :], w_fi[:, cols])
                t = 1.0 / (1.0 + (ERF_P * 0.5**0.5) * jnp.abs(inner))
                bell = jnp.exp2(inner * inner * (-0.5 * LOG2E))
                poly = 0.5 * ERF_C[5] * t + 0.5 * ERF_C[4]
                for coef in ERF_C[3::-1]:
                    poly = poly * t + 0.5 * coef
                tail = poly * t * bell
                cdf = jnp.where(inner >= 0.0, 1.0 - tail, tail)
                gd[step, at, cols] = cdf + inner * bell * 0.3989422804014327
                act[step, at, cols] = (inner * cdf).astype(BF16)
                yield 260
        x3 = x2s[step] + mm(act[step], w_fo[...])
        for side in range(2):
            x3s[scene, :, half, :, side] = x3[places[side]].reshape(VIEWS, WIN, WIN, C)
        yield 300

    def by_row(value, table):
        return (value.reshape(-1, HV, C) * table).reshape(value.shape)

    def im2col(value, pad, dest, first, last):
        pad[8 : 8 + PIX, :] = value
        dest[HV : HV + PIX, C : 2 * C] = value.astype(BF16)
        before = by_row(pad[7 : 7 + PIX, :], tables[2 * HV : 3 * HV, :])
        after = by_row(pad[9 : 9 + PIX, :], tables[3 * HV : 4 * HV, :])
        dest[HV : HV + PIX, first * C : (first + 1) * C] = before.astype(BF16)
        dest[HV : HV + PIX, last * C : (last + 1) * C] = after.astype(BF16)

    def head(scene):
        live = count_ref[scene]
        goes_on = {1: live > 2, 2: live > 3}

        def partner_of(ref, view, at):
            if view in goes_on:
                return jnp.where(goes_on[view], ref[scene, view + 1, at, :], ref[scene, 0, at, :])
            return ref[scene, (view + 1) % VIEWS, at, :]

        for view in views:
            low[scene, view] = x3s[scene, view].reshape(PIX, C).astype(BF16)
            shift = offsets[scene, view : view + 1, :]
            hots[scene, 0, view, 0:HV, :] = (shift == row).astype(BF16)
            hots[scene, 0, view, C : C + HV, :] = (shift == row).astype(BF16)
            hots[scene, 1, view, 0:HV, :] = (shift == HV - 1 - row).astype(BF16)
        yield 150
        for view in views:
            for at in upper:
                rev[scene, view, at, :] = mm(flip[...], low[scene, view, at, :]).astype(BF16)
        yield 250
        corrs = [[mm_nt(low[scene, view, at, :], partner_of(rev, view, at)) for at in upper] for view in views]
        yield 250
        skewed = [
            [by_row(pltpu.roll(corr, 1, 1, stride=1, stride_axis=0), tables[0:HV, :]) for corr in corrs[view]]
            for view in views
        ]
        yield 300
        cost = [mm(split_two(joined(skewed[view])), hots[scene, 0, view]) for view in views]
        yield 300
        for view in views:
            im2col(cost[view], pads.at[scene, 0, view], taps.at[scene, view], 0, 2)
            yield 80
        refined = []
        for view in views:
            columns = jnp.concatenate([taps[scene, view, HV * a : HV * a + PIX, :] for a in range(3)], -1)
            refined.append(cost[view] + mm(columns, t_rf[...]))
            yield 320
        d_refined = []
        for view in views:
            expo = jnp.exp2((refined[view] - jnp.max(refined[view], -1, keepdims=True)) * LOG2E)
            inverse = 1.0 / jnp.sum(expo, -1, keepdims=True)
            depth = jnp.sum(expo * depth_values, -1, keepdims=True) * inverse
            valid = jnp.where(view < live, 1.0, 0.0)
            incoming = []
            for at in upper:
                depth_out[scene, view : view + 1, at] = jnp.sum(eye[...] * depth[at], 0, keepdims=True) * valid
                incoming.append(jnp.sum(eye[...] * depth_grad[scene, view : view + 1, at], 1, keepdims=True))
            weight = joined(incoming) * (inverse * valid)
            d_refined.append(expo * (weight * depth_values - weight * depth))
            yield 250
        for view in views:
            im2col(d_refined[view], pads.at[scene, 1, view], back_taps.at[scene, view], 2, 0)
            yield 80
        d_cost = []
        for view in views:
            columns = jnp.concatenate(
                [back_taps[scene, view, HV * (2 - a) : HV * (2 - a) + PIX, :] for a in range(3)], -1
            )
            d_cost.append(d_refined[view] + mm(columns, b_rf[...]))
            yield 320
        for view in views:
            columns = jnp.concatenate([taps[scene, view, HV * a : HV * a + PIX, :] for a in range(3)], -1)
            g_rf[...] += mm_tn(back_taps[scene, view, HV : HV + PIX, C : 2 * C], columns)
            yield 250
        d_skewed = [
            mm_nt(split_two(d_cost[view]), jnp.concatenate([hots[scene, 1, view, :C, :]] * 2, -1)) for view in views
        ]
        yield 300
        d_corr = [
            [
                pltpu.roll(
                    by_row(d_skewed[view][at], tables[HV : 2 * HV, :]), HALF - HV + 1, 1, stride=1, stride_axis=0
                ).astype(BF16)
                for at in upper
            ]
            for view in views
        ]
        yield 250
        for part in range(2):
            at = upper[part]
            total = [mm(d_corr[view][part], partner_of(low, view, at)) for view in views]
            for view in views:
                there = mm_tn(d_corr[view][part], low[scene, view, at, :])
                if view in goes_on:
                    total[view + 1] = total[view + 1] + jnp.where(goes_on[view], there, 0.0)
                    total[0] = total[0] + jnp.where(goes_on[view], 0.0, there)
                else:
                    total[(view + 1) % VIEWS] = total[(view + 1) % VIEWS] + there
            for view in views:
                d3s[scene, view, part] = total[view].reshape(WIN, 2, WIN, C)
            yield 250

    def back(scene, half):
        step = 2 * scene + half
        d3 = joined([d3s[scene, :, half, :, side].reshape(TOK, C) for side in range(2)])
        d_low = d3.astype(BF16)
        d_inners = []
        for block in range(FFH // C):
            cols = slice(block * C, (block + 1) * C)
            d_inners.append((mm(d_low, t_fo[:, cols]) * gd[step, :, cols]).astype(BF16))
            yield 100
        d_inner = jnp.concatenate(d_inners, -1)
        d_normed = mm(d_inner, t_fi[...])
        yield 300
        g_fo[...] += mm_tn(d_low, act[step])
        yield 250
        g_fi[...] += mm_tn(no_c[step], d_inner)
        yield 250
        d_hidden, d_gain = norm_backward(d_normed, xh_c[step], rs_c[step], gain_c)
        g_gain[2] += d_gain
        d2 = d3 + d_hidden
        yield 300
        d_low = d2.astype(BF16)
        qkv = qkv_b[step]
        d_mixed = mm(d_low, t_co[...]).astype(BF16)
        yield 200
        g_co[...] += mm_tn(o_b[step], d_low)
        probs = p_b[step]
        d_values = joined([mm_tn(probs[at], d_mixed[at]) for at in places])
        d_probs = joined([mm_nt(d_mixed[at], qkv[at, 2 * C :]) for at in places])
        yield 400
        d_raw = soft_back(probs, d_probs)
        yield 300
        d_query = joined([mm(d_raw[at], qkv[at, C : 2 * C]) for at in places])
        d_keys = joined([mm_tn(d_raw[at], qkv[at, :C]) for at in places])
        d_packed = jnp.concatenate([d_query, d_keys, d_values], -1).astype(BF16)
        yield 400
        d_normed = mm(d_packed, t_cq[...])
        yield 200
        g_cq[...] += mm_tn(no_b[step], d_packed)
        yield 200
        d_hidden, d_gain = norm_backward(d_normed, xh_b[step], rs_b[step], gain_b)
        g_gain[1] += d_gain
        d1 = d2 + d_hidden
        yield 300
        d_low = d1.astype(BF16)
        qkv = qkv_a[step]
        d_mixed = mm(d_low, t_so[...]).astype(BF16)
        yield 200
        g_so[...] += mm_tn(o_a[step], d_low)
        probs = p_a[step]
        d_values = joined([mm_tn(probs[at], d_mixed[at]) for at in windows])
        d_probs = joined([mm_nt(d_mixed[at], qkv[at, 2 * C :]) for at in windows])
        yield 400
        d_raw = soft_back(probs, d_probs)
        yield 200
        d_query = joined([mm(d_raw[at], qkv[at, C : 2 * C]) for at in windows])
        d_keys = joined([mm_tn(d_raw[at], qkv[at, :C]) for at in windows])
        d_packed = jnp.concatenate([d_query, d_keys, d_values], -1).astype(BF16)
        yield 300
        d_normed = mm(d_packed, t_sq[...])
        yield 200
        g_sq[...] += mm_tn(no_a[step], d_packed)
        yield 200
        d_hidden, d_gain = norm_backward(d_normed, xh_a[step], rs_a[step], gain_a)
        g_gain[0] += d_gain
        d0 = d1 + d_hidden
        for side in range(2):
            grad_out[scene, :, half, :, side] = d0[places[side]].reshape(VIEWS, WIN, WIN, C)
        sent.append(
            pltpu.make_async_copy(grad_out.at[scene, :, half], grad_hbm.at[scene, :, half], sems.at[1 + step])
        )
        sent[-1].start()
        yield 300

    def chain(*threads):
        for thread in threads:
            yield from thread

    def feeds(scene):
        return chain(feed(scene, 0), feed(scene, 1))

    bring.wait()
    merge(attend(0, 0))
    merge(attend(0, 1), feed(0, 0))
    for scene in range(1, scenes):
        merge(attend(scene, 0), feed(scene - 1, 1))
        merge(chain(attend(scene, 1), feed(scene, 1)), feed(scene, 0), paced(head(scene - 1), 1.0))
        merge(head(scene), paced(chain(back(scene - 1, 0), back(scene - 1, 1)), 0.6))
    merge(back(scenes - 1, 0), back(scenes - 1, 1))

    bits = bits_of(parts)
    line = iota((GAIN_ROWS, C), 0)
    gain_rows = jnp.zeros((GAIN_ROWS, C), F32)
    for which in range(3):
        gain_rows = jnp.where(line == which, jnp.sum(g_gain[which], 0, keepdims=True), gain_rows)
    gain_rows = gain_rows.astype(BF16)
    for block in range(FFH // C):
        w_fo[block * C : (block + 1) * C, :] = g_fo[:, block * C : (block + 1) * C].T.astype(BF16)
    half_rows = rows_of(parts) // 2
    first = side_of_rows
    for apart in range(parts):
        shard = me ^ apart
        slot = sum(((apart >> bit) & 1) << (bits - 1 - bit) for bit in range(bits))
        dest = (keep_out, send_out)[slot // (parts // 2)].at[slot % (parts // 2)]

        def put(at, value):
            height = value.shape[0]
            which, offset = divmod(at, half_rows)
            assert offset + height <= half_rows
            dest[pl.ds(pl.multiple_of((first ^ which) * half_rows + offset, 16), height), :] = value

        at = 0
        for ref, blocks in zip((g_sq, g_so, g_cq, g_co, g_fi, w_fo, g_rf), BLOCKS):
            for block in range(blocks):
                if ref is w_fo:
                    spot = pl.ds(pl.multiple_of(shard * (blocks * rows) + block * rows, 16), rows)
                    put(at, ref[spot, :])
                else:
                    spot = pl.ds(pl.multiple_of(shard * rows, 16), rows)
                    put(at, ref[spot, block * C : (block + 1) * C].astype(BF16))
                at += rows
        put(at, gain_rows)
        if at + GAIN_ROWS < rows_of(parts):
            put(at + GAIN_ROWS, jnp.zeros((rows_of(parts) - at - GAIN_ROWS, C), BF16))
    for one in sent:
        one.wait()


VMEM = pl.BlockSpec(memory_space=pltpu.VMEM)
HBM = pl.BlockSpec(memory_space=pltpu.HBM)
SMEM = pl.BlockSpec(memory_space=pltpu.SMEM)


def exchange(value, fsdp_mask, dp_mask):
    parts = lax.axis_size("fsdp")
    count = parts * lax.axis_size("dp")
    mask = dp_mask * parts + fsdp_mask
    return lax.ppermute(value, ("dp", "fsdp"), [(i, i ^ mask) for i in range(count)])


def local(
    features,
    view_count,
    plane_offsets,
    depth_grad,
    gain_self,
    self_qkv,
    self_out,
    gain_cross,
    cross_qkv,
    cross_out,
    gain_ff,
    ff_in,
    ff_out,
    refine,
):
    parts = lax.axis_size("fsdp")
    copies = lax.axis_size("dp")
    scenes = features.shape[0]
    rows = C // parts
    shard_rows = rows_of(parts)
    small = pltpu.CompilerParams(vmem_limit_bytes=8 * MIB)

    pack = pl.pallas_call(
        functools.partial(pack_kernel, parts),
        out_shape=jax.ShapeDtypeStruct((shard_rows, C), BF16),
        in_specs=[HBM] * 10,
        out_specs=VMEM,
        scratch_shapes=[pltpu.VMEM((3, 1, rows), BF16), pltpu.SemaphoreType.DMA((3 + sum(BLOCKS),))],
        compiler_params=pltpu.CompilerParams(vmem_limit_bytes=60 * MIB),
        name="pack",
    )
    shard = pack(
        gain_self.reshape(1, rows),
        gain_cross.reshape(1, rows),
        gain_ff.reshape(1, rows),
        self_qkv,
        self_out,
        cross_qkv,
        cross_out,
        ff_in,
        ff_out,
        refine,
    )
    packed = {0: shard}
    for bit in reversed(range(bits_of(parts))):
        packed |= {apart | (1 << bit): exchange(piece, 1 << bit, 0) for apart, piece in packed.items()}
    packed = [packed[apart] for apart in range(parts)]

    steps = scenes * (HV // WIN)
    span = 2 * TOK
    scratch = [
        ((C, 3 * C), BF16), ((C, C), BF16), ((C, 3 * C), BF16), ((C, C), BF16),
        ((C, FFH), BF16), ((FFH, C), BF16), ((C, 9 * PLANES), BF16),
        ((3 * C, C), BF16), ((C, C), BF16), ((3 * C, C), BF16), ((C, C), BF16),
        ((FFH, C), BF16), ((C, FFH), BF16), ((9 * PLANES, C), BF16), ((9 * PLANES, C), BF16),
        ((8, C), F32),
        ((scenes, TOK, TOK), F32),
        ((steps, VIEWS, WIN, 2, WIN, C), F32),
        ((steps, span, C), F32),
    ]
    scratch += [((steps, span, C), F32)] * 6
    scratch += [((steps, span, C), BF16)] * 3
    scratch += [
        ((steps, span, 3 * C), BF16), ((steps, span, 3 * C), BF16),
        ((steps, span, WIN * WIN), BF16), ((steps, span, TOK), BF16),
        ((steps, span, C), BF16), ((steps, span, C), BF16),
        ((steps, span, FFH), F32), ((steps, span, FFH), BF16),
        ((scenes, VIEWS, 2, WIN, 2, WIN, C), F32), ((scenes, VIEWS, 2, WIN, 2, WIN, C), F32),
        ((scenes, VIEWS, PIX, C), BF16), ((scenes, VIEWS, PIX, C), BF16),
        ((scenes, 2, VIEWS, PIX + 16, C), F32),
        ((scenes, VIEWS, PIX + 2 * HV, 3 * C), BF16), ((scenes, VIEWS, PIX + 2 * HV, 3 * C), BF16),
        ((4 * HV, C), F32), ((HALF, HALF), F32), ((HALF, HALF), BF16), ((scenes, 2, VIEWS, 2 * C, C), BF16),
        ((C, 3 * C), F32), ((C, C), F32), ((C, 3 * C), F32), ((C, C), F32),
        ((C, FFH), F32), ((C, FFH), F32), ((C, 9 * PLANES), F32), ((3, 8, C), F32),
    ]
    main = pl.pallas_call(
        functools.partial(main_kernel, scenes, parts),
        out_shape=(
            jax.ShapeDtypeStruct((scenes, VIEWS, PIX), F32),
            jax.ShapeDtypeStruct((scenes, VIEWS, 2, WIN, 2, WIN, C), F32),
            jax.ShapeDtypeStruct((parts // 2, shard_rows, C), BF16),
            jax.ShapeDtypeStruct((parts // 2, shard_rows, C), BF16),
        ),
        in_specs=[SMEM, HBM] + [VMEM] * (2 + parts),
        out_specs=(VMEM, HBM, VMEM, VMEM),
        scratch_shapes=[pltpu.VMEM(shape, kind) for shape, kind in scratch]
        + [
            pltpu.VMEM(features.shape, BF16),
            pltpu.VMEM((scenes, VIEWS, 2, WIN, 2, WIN, C), F32),
            pltpu.SemaphoreType.DMA((1 + steps,)),
        ],
        compiler_params=pltpu.CompilerParams(vmem_limit_bytes=52 * MIB),
        name="layer",
    )
    depth, grad_features, keep, send = main(view_count, features, plane_offsets, depth_grad, *packed)

    for bit in range(bits_of(parts)):
        if bit > 0:
            keep, send = keep[: keep.shape[0] // 2], keep[keep.shape[0] // 2 :]
        if bit < bits_of(parts) - 1:
            keep = keep + exchange(send, 1 << bit, 0)
    last = parts // 2
    half = shard_rows // 2
    beside = exchange(send[0, :half], last, 0)
    across = exchange(keep[0, half:], 0, 1)
    corner = exchange(send[0, half:], last, 1)
    grads = (keep[0, :half].astype(F32) + beside) + (across.astype(F32) + corner)
    grads = grads.astype(BF16)
    for bit in reversed(range(2, bits_of(copies))):
        grads = grads + exchange(grads, 0, 1 << bit)
    if bits_of(copies) > 1:
        along = exchange(grads, 0, 2)
        swapped = exchange(grads, 0, 1)
        corner = exchange(grads, 0, 3)
        own, other = (grads, along), (swapped, corner)
    else:
        own, other = (grads,), (exchange(grads, 0, 1),)

    unpack = pl.pallas_call(
        functools.partial(unpack_kernel, parts),
        out_shape=tuple(jax.ShapeDtypeStruct((1, rows), F32) for _ in range(3))
        + tuple(
            jax.ShapeDtypeStruct(piece.shape, F32)
            for piece in (self_qkv, self_out, cross_qkv, cross_out, ff_in, ff_out, refine)
        ),
        in_specs=[VMEM] * (2 * len(own)),
        out_specs=(VMEM,) * 10,
        scratch_shapes=[pltpu.VMEM((shard_rows, C), F32)],
        compiler_params=small,
        name="unpack",
    )
    ga, gb, gc, d_sq, d_so, d_cq, d_co, d_fi, d_fo, d_rf = unpack(*own, *other)
    return (
        depth,
        grad_features.reshape(features.shape),
        ga.reshape(rows),
        d_sq,
        d_so,
        gb.reshape(rows),
        d_cq,
        d_co,
        gc.reshape(rows),
        d_fi,
        d_fo,
        d_rf,
    )


def solution(mesh):
    placed = (
        P(("dp", "fsdp"), None, None, None),
        P(("dp", "fsdp")),
        P(("dp", "fsdp"), None, None),
        P(("dp", "fsdp"), None, None),
        P("fsdp"),
        P("fsdp", None),
        P("fsdp", None),
        P("fsdp"),
        P("fsdp", None),
        P("fsdp", None),
        P("fsdp"),
        P("fsdp", None),
        P("fsdp", None),
        P("fsdp", None),
    )
    return jax.shard_map(
        local,
        mesh=mesh,
        in_specs=placed,
        out_specs=(
            P(("dp", "fsdp"), None, None),
            P(("dp", "fsdp"), None, None, None),
            P("fsdp"),
            P("fsdp", None),
            P("fsdp", None),
            P("fsdp"),
            P("fsdp", None),
            P("fsdp", None),
            P("fsdp"),
            P("fsdp", None),
            P("fsdp", None),
            P("fsdp", None),
        ),
        check_vma=False,
    )
```

time: 84.9 us -> 66.4 us (0.78)
  blocking collectives: 11.9 us -> 0 us
  Pallas kernels: 38.1 us -> 29.4 us
  starting transfers between devices: 6.48 us -> 13.1 us
  waiting for transfers between devices: 25.4 us -> 21.7 us
    all_gather x1 -> x0, blocking collectives: 11.9 us -> none  [local(): packed = lax.all_gather(shard, 'fsdp', axis=0)]
    pallas_call x3, Pallas kernels: 38.1 us -> 29.4 us  [the longest x1 26.6 us: local(): main(view_count, features, plane_offsets, depth_grad, *packed)]
    ppermute x5 -> x11, starting transfers between devices: 6.48 us -> 13.1 us  [exchange(): lax.ppermute(value, ('dp', 'fsdp'), [(i, i ^ mask) for i in range(count)])]
    ppermute x5 -> x11, waiting for transfers between devices: 25.4 us -> 21.7 us  [exchange(): lax.ppermute(value, ('dp', 'fsdp'), [(i, i ^ mask) for i in range(count)])]
    slice x2 -> x0, local copies, waits for them, and re-layouts: 1.12 us -> none  [local(): grads = grads[:half] + exchange(grads[half:], 'fsdp', bit)]
  transfers between devices with their start and end apart: 5 -> 11, of which waited for: 5 -> 9; matrix products, arithmetic and copies ran while one was open for 0% -> 0% of each run, Pallas kernels for 0% -> 0%
where the time goes in v2:
time: 66.4 us; the launch traced here: 66.1 us
  Pallas kernels  29.4 us (44%)
  waiting for transfers between devices  21.7 us (33%)
  starting transfers between devices  13.1 us (20%)
  local copies, waits for them, and re-layouts  0.96 us (1%)
  between operations  0.73 us (1%)
    pallas_call x1, Pallas kernels, local(): main(view_count, features, plane_offsets, depth_grad, *packed)  26.6 us
    ppermute x11, waiting for transfers between devices, exchange(): lax.ppermute(value, ('dp', 'fsdp'), [(i, i ^ mask) for i in range(count)])  21.7 us
    ppermute x11, starting transfers between devices, exchange(): lax.ppermute(value, ('dp', 'fsdp'), [(i, i ^ mask) for i in range(count)])  13.1 us
    pallas_call x1, Pallas kernels, local(): pack(gain_self.reshape(1, rows), gain_cross.reshape(1, rows), gain_ff.res...  1.86 us
  transfers between devices with their start and end apart: 11, of which 9 were waited for; matrix products, arithmetic and copies ran while one was open for 0% of the time, Pallas kernels for 0%

profile of v2, /device:TPU:0, one launch (start us, length us, event | category | flops | bytes accessed | tf_op | source)
XLA Modules:
  0.0 66.1 jit_solution(15777548834272533533)
XLA Ops:
  0.7 1.9 %pack.1.refs_0_ = bf16[832,128]{1,0:T(8,128)(2,1)} custom-call(bf16[1,32]{1,0:T(2,128)(2,1)} %bitcast.18, bf16[1,32]{1,0:T(2,128)(2,1)} %bitcast.19, bf16[1,32]{1,0:T(2,128)(2,1)} %bitcast.20, bf16[32,384]{1,0:T(8,128)(2,1)} %refs_3_.1, bf16[32,128]{1,0:T(8,128)(2,1)} %refs_4_.1, bf16[32,384]{1,0:T(8,128)(2,1)} %refs_5_.1, bf16[32,128]{1,0:T(8,128)(2,1)} %refs_6_.1, ...), custom_call_target="tpu_custom_call" | custom-call | tf_op jit(solution)/shard_map/pack/pallas_call | solution.py:609
  2.5 3.0 %collective-permute-start.1 = (bf16[832,128]{1,0:T(8,128)(2,1)}, bf16[832,128]{1,0:T(8,128)(2,1)S(1)}, u32[]{:S(2)}, u32[]{:S(2)}) collective-permute-start(bf16[832,128]{1,0:T(8,128)(2,1)} %pack.1.refs_0_), channel_id=1, source_target_pairs={{0,2},{1,3},{2,0},{3,1},{4,6},{5,7},{6,4},{7,5},{8,10},{9,11},{10,... | collective-permute-start | bytes 638984 | tf_op jit(solution)/shard_map/ppermute | solution.py:574
  5.6 5.5 %collective-permute-done.1.refs_2_ = bf16[832,128]{1,0:T(8,128)(2,1)S(1)} collective-permute-done((bf16[832,128]{1,0:T(8,128)(2,1)}, bf16[832,128]{1,0:T(8,128)(2,1)S(1)}, u32[]{:S(2)}, u32[]{:S(2)}) %collective-permute-start.1) | collective-permute-done | bytes 213024 | tf_op jit(solution)/shard_map/ppermute | solution.py:574
  11.0 1.5 %collective-permute-done.2.refs_3_ = bf16[832,128]{1,0:T(8,128)(2,1)S(1)} collective-permute-done((bf16[832,128]{1,0:T(8,128)(2,1)S(1)}, bf16[832,128]{1,0:T(8,128)(2,1)S(1)}, u32[]{:S(2)}, u32[]{:S(2)}) %collective-permute-start.2) | collective-permute-done | bytes 213024 | tf_op jit(solution)/shard_map/ppermute | solution.py:574
  12.5 0.9 %copy-done = bf16[832,128]{1,0:T(8,128)(2,1)S(1)} copy-done((bf16[832,128]{1,0:T(8,128)(2,1)S(1)}, bf16[832,128]{1,0:T(8,128)(2,1)}, u32[]{:S(2)}) %copy-start) | copy-done | bytes 213016
  13.4 26.6 %layer.1 = (f32[2,4,256]{2,1,0:T(4,128)}, f32[2,4,2,8,2,8,128]{6,5,4,3,2,1,0:T(8,128)}, bf16[2,832,128]{2,1,0:T(8,128)(2,1)S(1)}, bf16[2,832,128]{2,1,0:T(8,128)(2,1)S(1)}) custom-call(s32[2]{0:T(128)S(1)} %copy-done.3, bf16[2,4,256,128]{3,2,1,0:T(8,128)(2,1)} %features_hbm.1, s32[2,4,128]{2,1,0:T(4,128)S(1)} %copy-done.2, f32[2,4,256]{2,1,0:T(4,128)S(1)} %copy-done.1, ...), custom_call_target="tpu_custom_call" | custom-call | tf_op jit(solution)/shard_map/layer/pallas_call | solution.py:672
  40.1 0.2 collective-permute-start.3
  40.3 1.6 %collective-permute-done.3 = bf16[2,832,128]{2,1,0:T(8,128)(2,1)S(1)} collective-permute-done((bf16[2,832,128]{2,1,0:T(8,128)(2,1)S(1)}, bf16[2,832,128]{2,1,0:T(8,128)(2,1)S(1)}, u32[]{:S(2)}, u32[]{:S(2)}) %collective-permute-start.3) | collective-permute-done | bytes 426016 | tf_op jit(solution)/shard_map/ppermute | solution.py:574
  41.9 0.1 add.15
  42.1 1.8 %collective-permute-start.4 = (bf16[416,128]{1,0:T(8,128)(2,1)S(1)}, bf16[416,128]{1,0:T(8,128)(2,1)S(1)}, u32[]{:S(2)}, u32[]{:S(2)}) collective-permute-start(bf16[416,128]{1,0:T(8,128)(2,1)S(1)} %get-tuple-element.40), channel_id=1, source_target_pairs={{0,2},{1,3},{2,0},{3,1},{4,6},{5,7},{6,4},{7,5},{8,10},{9,11},{10,... | collective-permute-start | bytes 319496 | tf_op jit(solution)/shard_map/ppermute | solution.py:574
  43.9 1.4 %collective-permute-start.6 = (bf16[416,128]{1,0:T(8,128)(2,1)S(1)}, bf16[416,128]{1,0:T(8,128)(2,1)S(1)}, u32[]{:S(2)}, u32[]{:S(2)}) collective-permute-start(bf16[416,128]{1,0:T(8,128)(2,1)S(1)} %get-tuple-element.41), channel_id=1, source_target_pairs={{0,6},{1,7},{2,4},{3,5},{4,2},{5,3},{6,0},{7,1},{8,14},{9,15},{10,... | collective-permute-start | bytes 319496 | tf_op jit(solution)/shard_map/ppermute | solution.py:574
  45.3 0.3 collective-permute-start.5
  45.6 3.1 %collective-permute-done.4 = bf16[416,128]{1,0:T(8,128)(2,1)S(1)} collective-permute-done((bf16[416,128]{1,0:T(8,128)(2,1)S(1)}, bf16[416,128]{1,0:T(8,128)(2,1)S(1)}, u32[]{:S(2)}, u32[]{:S(2)}) %collective-permute-start.4) | collective-permute-done | bytes 106528 | tf_op jit(solution)/shard_map/ppermute | solution.py:574
  48.8 1.9 %collective-permute-done.6 = bf16[416,128]{1,0:T(8,128)(2,1)S(1)} collective-permute-done((bf16[416,128]{1,0:T(8,128)(2,1)S(1)}, bf16[416,128]{1,0:T(8,128)(2,1)S(1)}, u32[]{:S(2)}, u32[]{:S(2)}) %collective-permute-start.6) | collective-permute-done | bytes 106528 | tf_op jit(solution)/shard_map/ppermute | solution.py:574
  50.6 0.2 collective-permute-done.5
  50.8 0.1 fusion.1
  50.8 2.8 %collective-permute-start.7 = (bf16[416,128]{1,0:T(8,128)(2,1)S(1)}, bf16[416,128]{1,0:T(8,128)(2,1)S(1)}, u32[]{:S(2)}, u32[]{:S(2)}) collective-permute-start(bf16[416,128]{1,0:T(8,128)(2,1)S(1)} %fusion.1), channel_id=1, source_target_pairs={{0,16},{1,17},{2,18},{3,19},{4,20},{5,21},{6,22},{7,23},{8,24},{9,... | collective-permute-start | bytes 319496 | tf_op jit(solution)/shard_map/ppermute | solution.py:574
  53.6 4.5 %collective-permute-done.7 = bf16[416,128]{1,0:T(8,128)(2,1)S(1)} collective-permute-done((bf16[416,128]{1,0:T(8,128)(2,1)S(1)}, bf16[416,128]{1,0:T(8,128)(2,1)S(1)}, u32[]{:S(2)}, u32[]{:S(2)}) %collective-permute-start.7) | collective-permute-done | bytes 106528 | tf_op jit(solution)/shard_map/ppermute | solution.py:574
  58.1 1.7 %collective-permute-start.10 = (bf16[416,128]{1,0:T(8,128)(2,1)S(1)}, bf16[416,128]{1,0:T(8,128)(2,1)S(1)}, u32[]{:S(2)}, u32[]{:S(2)}) collective-permute-start(bf16[416,128]{1,0:T(8,128)(2,1)S(1)} %add.19.refs_0_), channel_id=1, source_target_pairs={{0,12},{1,13},{2,14},{3,15},{4,8},{5,9},{6,10},{7,11},{8,4},{9,5},... | collective-permute-start | bytes 319496 | tf_op jit(solution)/shard_map/ppermute | solution.py:574
  59.8 0.5 collective-permute-start.9
  60.4 1.3 %collective-permute-start.8 = (bf16[416,128]{1,0:T(8,128)(2,1)S(1)}, bf16[416,128]{1,0:T(8,128)(2,1)S(1)}, u32[]{:S(2)}, u32[]{:S(2)}) collective-permute-start(bf16[416,128]{1,0:T(8,128)(2,1)S(1)} %add.19.refs_0_), channel_id=1, source_target_pairs={{0,8},{1,9},{2,10},{3,11},{4,12},{5,13},{6,14},{7,15},{8,0},{9,1},... | collective-permute-start | bytes 319496 | tf_op jit(solution)/shard_map/ppermute | solution.py:574
  61.7 3.0 %collective-permute-done.10.refs_3_ = bf16[416,128]{1,0:T(8,128)(2,1)S(1)} collective-permute-done((bf16[416,128]{1,0:T(8,128)(2,1)S(1)}, bf16[416,128]{1,0:T(8,128)(2,1)S(1)}, u32[]{:S(2)}, u32[]{:S(2)}) %collective-permute-start.10) | collective-permute-done | bytes 106528 | tf_op jit(solution)/shard_map/ppermute | solution.py:574
  64.7 0.6 collective-permute-done.9.refs_2_
  65.3 0.9 %unpack.1 = (f32[1,32]{1,0:T(1,128)}, f32[1,32]{1,0:T(1,128)}, f32[1,32]{1,0:T(1,128)}, f32[32,384]{1,0:T(8,128)}, f32[32,128]{1,0:T(8,128)}, /*index=5*/f32[32,...) custom-call(bf16[416,128]{1,0:T(8,128)(2,1)S(1)} %add.19.refs_0_, ...), custom_call_target="tpu_custom_call" | custom-call | tf_op jit(solution)/shard_map/unpack/pallas_call | solution.py:709
  (13 shorter events, 0.1 us)
Async XLA Ops:
  0.6 11.9 %copy-start.1 = (f32[2,4,256]{2,1,0:T(4,128)S(1)}, f32[2,4,256]{2,1,0:T(4,128)}, u32[]{:S(2)}) copy-start(f32[2,4,256]{2,1,0:T(4,128)} %depth_grad.1) | copy-start | bytes 24580
  0.7 11.9 %copy-start.2 = (s32[2,4,128]{2,1,0:T(4,128)S(1)}, s32[2,4,128]{2,1,0:T(4,128)}, u32[]{:S(2)}) copy-start(s32[2,4,128]{2,1,0:T(4,128)} %offsets.1) | copy-start | bytes 12292
  0.7 11.8 %copy-start.3 = (s32[2]{0:T(128)S(1)}, s32[2]{0:T(128)}, u32[]{:S(2)}) copy-start(s32[2]{0:T(128)} %count_ref.1) | copy-start | bytes 28
  2.5 8.5 %collective-permute-start.1 = (bf16[832,128]{1,0:T(8,128)(2,1)}, bf16[832,128]{1,0:T(8,128)(2,1)S(1)}, u32[]{:S(2)}, u32[]{:S(2)}) collective-permute-start(bf16[832,128]{1,0:T(8,128)(2,1)} %pack.1.refs_0_), channel_id=1, source_target_pairs={{0,2},{1,3},{2,0},{3,1},{4,6},{5,7},{6,4},{7,5},{8,10},{9,11},{10,... | collective-permute-start | bytes 638984 | tf_op jit(solution)/shard_map/ppermute | solution.py:574
  5.6 5.5 %collective-permute-start = (bf16[832,128]{1,0:T(8,128)(2,1)}, bf16[832,128]{1,0:T(8,128)(2,1)S(1)}, u32[]{:S(2)}, u32[]{:S(2)}) collective-permute-start(bf16[832,128]{1,0:T(8,128)(2,1)} %pack.1.refs_0_), channel_id=1, source_target_pairs={{0,1},{1,0},{2,3},{3,2},{4,5},{5,4},{6,7},{7,6},{8,9},{9,8},{10,11... | collective-permute-start | bytes 638984 | tf_op jit(solution)/shard_map/ppermute | solution.py:574
  11.0 1.5 %collective-permute-start.2 = (bf16[832,128]{1,0:T(8,128)(2,1)S(1)}, bf16[832,128]{1,0:T(8,128)(2,1)S(1)}, u32[]{:S(2)}, u32[]{:S(2)}) collective-permute-start(bf16[832,128]{1,0:T(8,128)(2,1)S(1)} %collective-permute-done.1.refs_2_), channel_id=1, source_target_pairs={{0,1},{1,0},{2,3},{3,2},{4,5},{5,4},{6,7},{7,6},{8,9},{9,8},{10,11... | collective-permute-start | bytes 638984 | tf_op jit(solution)/shard_map/ppermute | solution.py:574
  12.5 0.9 %copy-start = (bf16[832,128]{1,0:T(8,128)(2,1)S(1)}, bf16[832,128]{1,0:T(8,128)(2,1)}, u32[]{:S(2)}) copy-start(bf16[832,128]{1,0:T(8,128)(2,1)} %pack.1.refs_0_) | copy-start | bytes 638980
  40.1 1.8 %collective-permute-start.3 = (bf16[2,832,128]{2,1,0:T(8,128)(2,1)S(1)}, bf16[2,832,128]{2,1,0:T(8,128)(2,1)S(1)}, u32[]{:S(2)}, u32[]{:S(2)}) collective-permute-start(bf16[2,832,128]{2,1,0:T(8,128)(2,1)S(1)} %get-tuple-element.29), channel_id=1, source_target_pairs={{0,1},{1,0},{2,3},{3,2},{4,5},{5,4},{6,7},{7,6},{8,9},{9,8},{10,11... | collective-permute-start | bytes 1277960 | tf_op jit(solution)/shard_map/ppermute | solution.py:574
  42.1 6.7 %collective-permute-start.4 = (bf16[416,128]{1,0:T(8,128)(2,1)S(1)}, bf16[416,128]{1,0:T(8,128)(2,1)S(1)}, u32[]{:S(2)}, u32[]{:S(2)}) collective-permute-start(bf16[416,128]{1,0:T(8,128)(2,1)S(1)} %get-tuple-element.40), channel_id=1, source_target_pairs={{0,2},{1,3},{2,0},{3,1},{4,6},{5,7},{6,4},{7,5},{8,10},{9,11},{10,... | collective-permute-start | bytes 319496 | tf_op jit(solution)/shard_map/ppermute | solution.py:574
  43.9 6.7 %collective-permute-start.6 = (bf16[416,128]{1,0:T(8,128)(2,1)S(1)}, bf16[416,128]{1,0:T(8,128)(2,1)S(1)}, u32[]{:S(2)}, u32[]{:S(2)}) collective-permute-start(bf16[416,128]{1,0:T(8,128)(2,1)S(1)} %get-tuple-element.41), channel_id=1, source_target_pairs={{0,6},{1,7},{2,4},{3,5},{4,2},{5,3},{6,0},{7,1},{8,14},{9,15},{10,... | collective-permute-start | bytes 319496 | tf_op jit(solution)/shard_map/ppermute | solution.py:574
  45.3 5.4 %collective-permute-start.5 = (bf16[416,128]{1,0:T(8,128)(2,1)S(1)}, bf16[416,128]{1,0:T(8,128)(2,1)S(1)}, u32[]{:S(2)}, u32[]{:S(2)}) collective-permute-start(bf16[416,128]{1,0:T(8,128)(2,1)S(1)} %get-tuple-element.42), channel_id=1, source_target_pairs={{0,4},{1,5},{2,6},{3,7},{4,0},{5,1},{6,2},{7,3},{8,12},{9,13},{10,... | collective-permute-start | bytes 319496 | tf_op jit(solution)/shard_map/ppermute | solution.py:574
  50.8 7.3 %collective-permute-start.7 = (bf16[416,128]{1,0:T(8,128)(2,1)S(1)}, bf16[416,128]{1,0:T(8,128)(2,1)S(1)}, u32[]{:S(2)}, u32[]{:S(2)}) collective-permute-start(bf16[416,128]{1,0:T(8,128)(2,1)S(1)} %fusion.1), channel_id=1, source_target_pairs={{0,16},{1,17},{2,18},{3,19},{4,20},{5,21},{6,22},{7,23},{8,24},{9,... | collective-permute-start | bytes 319496 | tf_op jit(solution)/shard_map/ppermute | solution.py:574
  58.1 6.6 %collective-permute-start.10 = (bf16[416,128]{1,0:T(8,128)(2,1)S(1)}, bf16[416,128]{1,0:T(8,128)(2,1)S(1)}, u32[]{:S(2)}, u32[]{:S(2)}) collective-permute-start(bf16[416,128]{1,0:T(8,128)(2,1)S(1)} %add.19.refs_0_), channel_id=1, source_target_pairs={{0,12},{1,13},{2,14},{3,15},{4,8},{5,9},{6,10},{7,11},{8,4},{9,5},... | collective-permute-start | bytes 319496 | tf_op jit(solution)/shard_map/ppermute | solution.py:574
  59.8 5.4 %collective-permute-start.9 = (bf16[416,128]{1,0:T(8,128)(2,1)S(1)}, bf16[416,128]{1,0:T(8,128)(2,1)S(1)}, u32[]{:S(2)}, u32[]{:S(2)}) collective-permute-start(bf16[416,128]{1,0:T(8,128)(2,1)S(1)} %add.19.refs_0_), channel_id=1, source_target_pairs={{0,4},{1,5},{2,6},{3,7},{4,0},{5,1},{6,2},{7,3},{8,12},{9,13},{10,... | collective-permute-start | bytes 319496 | tf_op jit(solution)/shard_map/ppermute | solution.py:574
  60.4 4.9 %collective-permute-start.8 = (bf16[416,128]{1,0:T(8,128)(2,1)S(1)}, bf16[416,128]{1,0:T(8,128)(2,1)S(1)}, u32[]{:S(2)}, u32[]{:S(2)}) collective-permute-start(bf16[416,128]{1,0:T(8,128)(2,1)S(1)} %add.19.refs_0_), channel_id=1, source_target_pairs={{0,8},{1,9},{2,10},{3,11},{4,12},{5,13},{6,14},{7,15},{8,0},{9,1},... | collective-permute-start | bytes 319496 | tf_op jit(solution)/shard_map/ppermute | solution.py:574

commit v3 on v2

--- a/solution.py
+++ b/solution.py
@@ -25,9 +25,6 @@
 BLOCKS = (3, 1, 3, 1, 4, 4, 9)
 MIB = 1024 * 1024
 
-ERF_P = 0.39
-ERF_C = (0.23532522, 0.09138841, 0.6495594, -0.63540028, 0.88666437, -0.22753713)
-
 
 def mm(left, right):
     return lax.dot_general(left, right, (((1,), (0,)), ((), ())), preferred_element_type=F32)
@@ -39,6 +36,16 @@
 
 def mm_tn(left, right):
     return lax.dot_general(left, right, (((0,), (0,)), ((), ())), preferred_element_type=F32)
+
+
+def paired(value):
+    half = value.shape[0] // 2
+    return jnp.concatenate([value[:half], value[half:]], -1)
+
+
+def unpaired(value):
+    half = value.shape[1] // 2
+    return jnp.concatenate([value[:, :half], value[:, half:]], 0)
 
 
 def norm_forward(value, gain):
@@ -76,6 +83,17 @@
 
 def place_of(parts):
     return lax.axis_index("fsdp").astype(jnp.int32), (lax.axis_index("dp") & 1).astype(jnp.int32)
+
+
+def gain_lines(parts, gains):
+    rows = C // parts
+    place = (iota((rows, C), 1) == iota((rows, C), 0) + place_of(parts)[0] * rows).astype(BF16)
+    line = iota((GAIN_ROWS, C), 0)
+    total = jnp.zeros((GAIN_ROWS, C), F32)
+    for which in range(3):
+        row = mm(jnp.broadcast_to(gains[which][...], (8, rows)), place)[:1]
+        total = jnp.where(line == which, row, total)
+    return total
 
 
 def pack_kernel(parts, *refs):
@@ -99,12 +117,7 @@
         at += blocks * rows
     for one in copies[:3]:
         one.wait()
-    place = (iota((rows, C), 1) == iota((rows, C), 0) + place_of(parts)[0] * rows).astype(BF16)
-    line = iota((GAIN_ROWS, C), 0)
-    total = jnp.zeros((GAIN_ROWS, C), F32)
-    for which in range(3):
-        row = mm(jnp.broadcast_to(scratch[which], (8, rows)), place)[:1]
-        total = jnp.where(line == which, row, total)
+    total = gain_lines(parts, [scratch.at[which] for which in range(3)])
     out[at : at + GAIN_ROWS, :] = total.astype(BF16)
     if at + GAIN_ROWS < out.shape[0]:
         out[at + GAIN_ROWS :, :] = jnp.zeros((out.shape[0] - at - GAIN_ROWS, C), BF16)
@@ -142,8 +155,8 @@
         outs[which][...] = picked[which : which + 1]
 
 
-def merge(*threads):
-    spent = [0.0] * len(threads)
+def merge(*threads, apart=0.0):
+    spent = [apart * i for i in range(len(threads))]
     left = set(range(len(threads)))
     while left:
         which = min(left, key=lambda i: (spent[i], i))
@@ -182,7 +195,7 @@
     depth_grad,
     *refs,
 ):
-    packed = refs[:parts]
+    own_gains, own, packed, refs = refs[:3], refs[3:10], refs[10 : 9 + parts], refs[9 + parts :]
     (
     depth_out,
     grad_hbm,
@@ -203,35 +216,47 @@
     tables, eye, flip, hots,
     g_sq, g_so, g_cq, g_co, g_fi, g_fo, g_rf, g_gain,
     features, grad_out, sems,
-    ) = refs[parts:]
+    ) = refs
     rows = C // parts
     me, side_of_rows = place_of(parts)
     bring = pltpu.make_async_copy(features_hbm, features, sems.at[0])
     bring.start()
     sent = []
 
-    total = jnp.zeros((GAIN_ROWS, C), F32)
-    for apart, piece in enumerate(packed):
+    total = gain_lines(parts, own_gains)
+    for apart in range(parts):
         shard = me ^ apart
         at = 0
-        for ref, blocks in zip((w_sq, w_so, w_cq, w_co, w_fi, w_fo, w_rf), BLOCKS):
-            if ref is w_fo:
-                spot = pl.ds(pl.multiple_of(shard * (blocks * rows), 16), blocks * rows)
-                ref[spot, :] = piece[at : at + blocks * rows, :]
+        for which, (ref, blocks) in enumerate(zip((w_sq, w_so, w_cq, w_co, w_fi, w_fo, w_rf), BLOCKS)):
+            height = blocks * rows if ref is w_fo else rows
+            spot = pl.ds(pl.multiple_of(shard * height, 16), height)
+            if apart == 0:
+                ref[spot, :] = own[which][...]
+            elif ref is w_fo:
+                ref[spot, :] = packed[apart - 1][at : at + height, :]
             else:
-                spot = pl.ds(pl.multiple_of(shard * rows, 16), rows)
                 for block in range(blocks):
-                    ref[spot, block * C : (block + 1) * C] = piece[at + block * rows : at + (block + 1) * rows, :]
+                    ref[spot, block * C : (block + 1) * C] = packed[apart - 1][
+                        at + block * rows : at + (block + 1) * rows, :
+                    ]
             at += blocks * rows
-        total = total + piece[at : at + GAIN_ROWS, :].astype(F32)
+        if apart > 0:
+            total = total + packed[apart - 1][at : at + GAIN_ROWS, :].astype(F32)
     gains[...] = total[:8]
-    for source, target in ((w_sq, t_sq), (w_so, t_so), (w_cq, t_cq), (w_co, t_co), (w_fi, t_fi), (w_rf, t_rf)):
+    for source, target in ((w_sq, t_sq), (w_so, t_so), (w_cq, t_cq), (w_co, t_co)):
         for block in range(source.shape[1] // C):
             target[block * C : (block + 1) * C, :] = source[:, block * C : (block + 1) * C].T
-    for block in range(9):
-        b_rf[block * C : (block + 1) * C, :] = w_rf[:, block * C : (block + 1) * C]
     for block in range(FFH // C):
+        t_fi[block * C : (block + 1) * C, :] = w_fi[:, block * C : (block + 1) * C].T
         t_fo[:, block * C : (block + 1) * C] = w_fo[block * C : (block + 1) * C, :].T
+    for tap in range(9):
+        block = w_rf[:, tap * C : (tap + 1) * C]
+        for ref, piece, at in ((t_rf, block.T, tap), (b_rf, block, 3 * (2 - tap // 3) + tap % 3)):
+            ref[at * C : (at + 1) * C, :C] = piece
+            ref[(at + 3) * C : (at + 4) * C, C:] = piece
+    for ref in (t_rf, b_rf):
+        ref[9 * C :, :C] = jnp.zeros((3 * C, C), BF16)
+        ref[: 3 * C, C:] = jnp.zeros((3 * C, C), BF16)
 
     for ref in (g_sq, g_so, g_cq, g_co, g_fi, g_fo, g_rf, g_gain, pads, hots):
         ref[...] = jnp.zeros_like(ref)
@@ -263,52 +288,55 @@
     places = [slice(side * TOK, (side + 1) * TOK) for side in range(2)]
     windows = [slice(at * WIN * WIN, (at + 1) * WIN * WIN) for at in range(2 * VIEWS)]
 
-    def attend(scene, half):
+    def attend(scene, half, side):
         step = 2 * scene + half
-        piece = features[scene, :, half * HALF : (half + 1) * HALF, :]
-        x0s[step] = piece.astype(F32).reshape(VIEWS, WIN, 2, WIN, C)
-        x0 = joined([x0s[step, :, :, side].reshape(TOK, C) for side in range(2)])
+        spot = places[side]
+        if side == 0:
+            piece = features[scene, :, half * HALF : (half + 1) * HALF, :]
+            x0s[step] = piece.astype(F32).reshape(VIEWS, WIN, 2, WIN, C)
+            yield 60
+        x0 = x0s[step, :, :, side].reshape(TOK, C)
         xhat, rstd, normed = norm_forward(x0, gain_a)
-        xh_a[step] = xhat
-        rs_a[step] = rstd
-        no_a[step] = normed
+        xh_a[step, spot, :] = xhat
+        rs_a[step, spot, :] = rstd
+        no_a[step, spot, :] = normed
         yield 400
         qkv = mm(normed, w_sq[...]).astype(BF16)
-        qkv_a[step] = qkv
+        qkv_a[step, spot, :] = qkv
         yield 300
-        scores = joined([mm_nt(qkv[at, :C], qkv[at, C : 2 * C]) for at in windows])
+        scores = joined([mm_nt(qkv[at, :C], qkv[at, C : 2 * C]) for at in windows[:VIEWS]])
         yield 200
         probs = soft(scores * (SCALE * LOG2E))
-        p_a[step] = probs
+        p_a[step, spot, :] = probs
         yield 400
-        mixed = joined([mm(probs[at], qkv[at, 2 * C :]) for at in windows]).astype(BF16)
-        o_a[step] = mixed
+        mixed = joined([mm(probs[at], qkv[at, 2 * C :]) for at in windows[:VIEWS]]).astype(BF16)
+        o_a[step, spot, :] = mixed
         yield 300
         x1 = x0 + mm(mixed, w_so[...])
         yield 200
         xhat, rstd, normed = norm_forward(x1, gain_b)
-        xh_b[step] = xhat
-        rs_b[step] = rstd
-        no_b[step] = normed
+        xh_b[step, spot, :] = xhat
+        rs_b[step, spot, :] = rstd
+        no_b[step, spot, :] = normed
         yield 400
         qkv = mm(normed, w_cq[...]).astype(BF16)
-        qkv_b[step] = qkv
+        qkv_b[step, spot, :] = qkv
         yield 300
-        scores = [mm_nt(qkv[at, :C], qkv[at, C : 2 * C]) * (SCALE * LOG2E) + bias[scene] for at in places]
+        scores = mm_nt(qkv[:, :C], qkv[:, C : 2 * C]) * (SCALE * LOG2E) + bias[scene]
         yield 300
-        probs = soft(joined(scores))
-        p_b[step] = probs
+        probs = soft(scores)
+        p_b[step, spot, :] = probs
         yield 500
-        mixed = joined([mm(probs[at], qkv[at, 2 * C :]) for at in places]).astype(BF16)
-        o_b[step] = mixed
+        mixed = mm(probs, qkv[:, 2 * C :]).astype(BF16)
+        o_b[step, spot, :] = mixed
         yield 300
         x2 = x1 + mm(mixed, w_co[...])
-        x2s[step] = x2
+        x2s[step, spot, :] = x2
         yield 200
         xhat, rstd, normed = norm_forward(x2, gain_c)
-        xh_c[step] = xhat
-        rs_c[step] = rstd
-        no_c[step] = normed
+        xh_c[step, spot, :] = xhat
+        rs_c[step, spot, :] = rstd
+        no_c[step, spot, :] = normed
         yield 400
 
     def feed(scene, half):
@@ -317,16 +345,11 @@
             cols = slice(block * C, (block + 1) * C)
             for at in places:
                 inner = mm(no_c[step, at, :], w_fi[:, cols])
-                t = 1.0 / (1.0 + (ERF_P * 0.5**0.5) * jnp.abs(inner))
+                cdf = 0.5 + 0.5 * lax.erf(inner * 0.5**0.5)
                 bell = jnp.exp2(inner * inner * (-0.5 * LOG2E))
-                poly = 0.5 * ERF_C[5] * t + 0.5 * ERF_C[4]
-                for coef in ERF_C[3::-1]:
-                    poly = poly * t + 0.5 * coef
-                tail = poly * t * bell
-                cdf = jnp.where(inner >= 0.0, 1.0 - tail, tail)
                 gd[step, at, cols] = cdf + inner * bell * 0.3989422804014327
                 act[step, at, cols] = (inner * cdf).astype(BF16)
-                yield 260
+                yield 100
         x3 = x2s[step] + mm(act[step], w_fo[...])
         for side in range(2):
             x3s[scene, :, half, :, side] = x3[places[side]].reshape(VIEWS, WIN, WIN, C)
@@ -343,6 +366,16 @@
         dest[HV : HV + PIX, first * C : (first + 1) * C] = before.astype(BF16)
         dest[HV : HV + PIX, last * C : (last + 1) * C] = after.astype(BF16)
 
+    def convolve(padded, kernel):
+        rows_two = padded.reshape(HV // 2 + 1, 2, HV, 3 * C)
+        columns = jnp.concatenate(
+            [rows_two[a // 2 : a // 2 + HV // 2, a % 2].reshape(HALF, 3 * C) for a in range(4)], -1
+        )
+        both = mm(columns, kernel[...])
+        return joined(
+            [both[HV * (y // 2) : HV * (y // 2 + 1), C * (y % 2) : C * (y % 2 + 1)] for y in range(HV)]
+        )
+
     def head(scene):
         live = count_ref[scene]
         goes_on = {1: live > 2, 2: live > 3}
@@ -358,28 +391,26 @@
             hots[scene, 0, view, 0:HV, :] = (shift == row).astype(BF16)
             hots[scene, 0, view, C : C + HV, :] = (shift == row).astype(BF16)
             hots[scene, 1, view, 0:HV, :] = (shift == HV - 1 - row).astype(BF16)
-        yield 150
+        yield 300
         for view in views:
-            for at in upper:
-                rev[scene, view, at, :] = mm(flip[...], low[scene, view, at, :]).astype(BF16)
-        yield 250
+            rev[scene, view] = unpaired(mm(flip[...], paired(low[scene, view])).astype(BF16))
+        yield 400
         corrs = [[mm_nt(low[scene, view, at, :], partner_of(rev, view, at)) for at in upper] for view in views]
-        yield 250
+        yield 400
         skewed = [
             [by_row(pltpu.roll(corr, 1, 1, stride=1, stride_axis=0), tables[0:HV, :]) for corr in corrs[view]]
             for view in views
         ]
-        yield 300
+        yield 500
         cost = [mm(split_two(joined(skewed[view])), hots[scene, 0, view]) for view in views]
-        yield 300
+        yield 500
         for view in views:
             im2col(cost[view], pads.at[scene, 0, view], taps.at[scene, view], 0, 2)
             yield 80
         refined = []
         for view in views:
-            columns = jnp.concatenate([taps[scene, view, HV * a : HV * a + PIX, :] for a in range(3)], -1)
-            refined.append(cost[view] + mm(columns, t_rf[...]))
-            yield 320
+            refined.append(cost[view] + convolve(taps[scene, view], t_rf))
+            yield 250
         d_refined = []
         for view in views:
             expo = jnp.exp2((refined[view] - jnp.max(refined[view], -1, keepdims=True)) * LOG2E)
@@ -398,11 +429,8 @@
             yield 80
         d_cost = []
         for view in views:
-            columns = jnp.concatenate(
-                [back_taps[scene, view, HV * (2 - a) : HV * (2 - a) + PIX, :] for a in range(3)], -1
-            )
-            d_cost.append(d_refined[view] + mm(columns, b_rf[...]))
-            yield 320
+            d_cost.append(d_refined[view] + convolve(back_taps[scene, view], b_rf))
+            yield 250
         for view in views:
             columns = jnp.concatenate([taps[scene, view, HV * a : HV * a + PIX, :] for a in range(3)], -1)
             g_rf[...] += mm_tn(back_taps[scene, view, HV : HV + PIX, C : 2 * C], columns)
@@ -437,76 +465,106 @@
 
     def back(scene, half):
         step = 2 * scene + half
-        d3 = joined([d3s[scene, :, half, :, side].reshape(TOK, C) for side in range(2)])
-        d_low = d3.astype(BF16)
-        d_inners = []
+        both = range(2)
+        d3 = [d3s[scene, :, half, :, side].reshape(TOK, C) for side in both]
+        d_low = [d3[side].astype(BF16) for side in both]
+        d_inner = [[], []]
         for block in range(FFH // C):
             cols = slice(block * C, (block + 1) * C)
-            d_inners.append((mm(d_low, t_fo[:, cols]) * gd[step, :, cols]).astype(BF16))
+            for side in both:
+                d_inner[side].append((mm(d_low[side], t_fo[:, cols]) * gd[step, places[side], cols]).astype(BF16))
             yield 100
-        d_inner = jnp.concatenate(d_inners, -1)
-        d_normed = mm(d_inner, t_fi[...])
-        yield 300
-        g_fo[...] += mm_tn(d_low, act[step])
+        d_inner = [jnp.concatenate(d_inner[side], -1) for side in both]
+        d_normed = []
+        for side in both:
+            d_normed.append(mm(d_inner[side], t_fi[...]))
+            yield 150
+        g_fo[...] += mm_tn(joined(d_low), act[step])
         yield 250
-        g_fi[...] += mm_tn(no_c[step], d_inner)
+        g_fi[...] += mm_tn(no_c[step], joined(d_inner))
         yield 250
-        d_hidden, d_gain = norm_backward(d_normed, xh_c[step], rs_c[step], gain_c)
-        g_gain[2] += d_gain
-        d2 = d3 + d_hidden
-        yield 300
-        d_low = d2.astype(BF16)
-        qkv = qkv_b[step]
-        d_mixed = mm(d_low, t_co[...]).astype(BF16)
+        d2 = []
+        for side in both:
+            spot = places[side]
+            d_hidden, d_gain = norm_backward(d_normed[side], xh_c[step, spot, :], rs_c[step, spot, :], gain_c)
+            g_gain[2] += d_gain
+            d2.append(d3[side] + d_hidden)
+            yield 150
+        d_low = [d2[side].astype(BF16) for side in both]
+        qkv = [qkv_b[step, spot, :] for spot in places]
+        d_mixed = []
+        for side in both:
+            d_mixed.append(mm(d_low[side], t_co[...]).astype(BF16))
+            yield 100
+        g_co[...] += mm_tn(o_b[step], joined(d_low))
+        yield 100
+        d_packed = [[], []]
+        d_raw = []
+        for side in both:
+            probs = p_b[step, places[side], :]
+            d_values = mm_tn(probs, d_mixed[side])
+            d_probs = mm_nt(d_mixed[side], qkv[side][:, 2 * C :])
+            yield 150
+            d_raw.append(soft_back(probs, d_probs))
+            d_packed[side].append(d_values)
+            yield 150
+        for side in both:
+            d_query = mm(d_raw[side], qkv[side][:, C : 2 * C])
+            d_keys = mm_tn(d_raw[side], qkv[side][:, :C])
+            d_packed[side] = jnp.concatenate([d_query, d_keys] + d_packed[side], -1).astype(BF16)
+            yield 200
+        d_normed = []
+        for side in both:
+            d_normed.append(mm(d_packed[side], t_cq[...]))
+            yield 100
+        g_cq[...] += mm_tn(no_b[step], joined(d_packed))
         yield 200
-        g_co[...] += mm_tn(o_b[step], d_low)
-        probs = p_b[step]
-        d_values = joined([mm_tn(probs[at], d_mixed[at]) for at in places])
-        d_probs = joined([mm_nt(d_mixed[at], qkv[at, 2 * C :]) for at in places])
-        yield 400
-        d_raw = soft_back(probs, d_probs)
-        yield 300
-        d_query = joined([mm(d_raw[at], qkv[at, C : 2 * C]) for at in places])
-        d_keys = joined([mm_tn(d_raw[at], qkv[at, :C]) for at in places])
-        d_packed = jnp.concatenate([d_query, d_keys, d_values], -1).astype(BF16)
-        yield 400
-        d_normed = mm(d_packed, t_cq[...])
+        d1 = []
+        for side in both:
+            spot = places[side]
+            d_hidden, d_gain = norm_backward(d_normed[side], xh_b[step, spot, :], rs_b[step, spot, :], gain_b)
+            g_gain[1] += d_gain
+            d1.append(d2[side] + d_hidden)
+            yield 150
+        d_low = [d1[side].astype(BF16) for side in both]
+        qkv = [qkv_a[step, spot, :] for spot in places]
+        d_mixed = []
+        for side in both:
+            d_mixed.append(mm(d_low[side], t_so[...]).astype(BF16))
+            yield 100
+        g_so[...] += mm_tn(o_a[step], joined(d_low))
+        yield 100
+        d_packed = [[], []]
+        d_raw = []
+        for side in both:
+            probs = p_a[step, places[side], :]
+            d_values = joined([mm_tn(probs[at], d_mixed[side][at]) for at in windows[:VIEWS]])
+            d_probs = joined([mm_nt(d_mixed[side][at], qkv[side][at, 2 * C :]) for at in windows[:VIEWS]])
+            yield 150
+            d_raw.append(soft_back(probs, d_probs))
+            d_packed[side].append(d_values)
+            yield 100
+        for side in both:
+            d_query = joined([mm(d_raw[side][at], qkv[side][at, C : 2 * C]) for at in windows[:VIEWS]])
+            d_keys = joined([mm_tn(d_raw[side][at], qkv[side][at, :C]) for at in windows[:VIEWS]])
+            d_packed[side] = jnp.concatenate([d_query, d_keys] + d_packed[side], -1).astype(BF16)
+            yield 150
+        d_normed = []
+        for side in both:
+            d_normed.append(mm(d_packed[side], t_sq[...]))
+            yield 100
+        g_sq[...] += mm_tn(no_a[step], joined(d_packed))
         yield 200
-        g_cq[...] += mm_tn(no_b[step], d_packed)
-        yield 200
-        d_hidden, d_gain = norm_backward(d_normed, xh_b[step], rs_b[step], gain_b)
-        g_gain[1] += d_gain
-        d1 = d2 + d_hidden
-        yield 300
-        d_low = d1.astype(BF16)
-        qkv = qkv_a[step]
-        d_mixed = mm(d_low, t_so[...]).astype(BF16)
-        yield 200
-        g_so[...] += mm_tn(o_a[step], d_low)
-        probs = p_a[step]
-        d_values = joined([mm_tn(probs[at], d_mixed[at]) for at in windows])
-        d_probs = joined([mm_nt(d_mixed[at], qkv[at, 2 * C :]) for at in windows])
-        yield 400
-        d_raw = soft_back(probs, d_probs)
-        yield 200
-        d_query = joined([mm(d_raw[at], qkv[at, C : 2 * C]) for at in windows])
-        d_keys = joined([mm_tn(d_raw[at], qkv[at, :C]) for at in windows])
-        d_packed = jnp.concatenate([d_query, d_keys, d_values], -1).astype(BF16)
-        yield 300
-        d_normed = mm(d_packed, t_sq[...])
-        yield 200
-        g_sq[...] += mm_tn(no_a[step], d_packed)
-        yield 200
-        d_hidden, d_gain = norm_backward(d_normed, xh_a[step], rs_a[step], gain_a)
-        g_gain[0] += d_gain
-        d0 = d1 + d_hidden
-        for side in range(2):
-            grad_out[scene, :, half, :, side] = d0[places[side]].reshape(VIEWS, WIN, WIN, C)
+        for side in both:
+            spot = places[side]
+            d_hidden, d_gain = norm_backward(d_normed[side], xh_a[step, spot, :], rs_a[step, spot, :], gain_a)
+            g_gain[0] += d_gain
+            grad_out[scene, :, half, :, side] = (d1[side] + d_hidden).reshape(VIEWS, WIN, WIN, C)
+            yield 150
         sent.append(
             pltpu.make_async_copy(grad_out.at[scene, :, half], grad_hbm.at[scene, :, half], sems.at[1 + step])
         )
         sent[-1].start()
-        yield 300
 
     def chain(*threads):
         for thread in threads:
@@ -516,13 +574,22 @@
         return chain(feed(scene, 0), feed(scene, 1))
 
     bring.wait()
-    merge(attend(0, 0))
-    merge(attend(0, 1), feed(0, 0))
-    for scene in range(1, scenes):
-        merge(attend(scene, 0), feed(scene - 1, 1))
-        merge(chain(attend(scene, 1), feed(scene, 1)), feed(scene, 0), paced(head(scene - 1), 1.0))
-        merge(head(scene), paced(chain(back(scene - 1, 0), back(scene - 1, 1)), 0.6))
-    merge(back(scenes - 1, 0), back(scenes - 1, 1))
+    def whole_of(thread, total):
+        return paced(thread, 1.0 / total)
+
+    def attends(scene):
+        return [whole_of(attend(scene, half, side), 4200) for half in range(2) for side in range(2)]
+
+    def feeds(scene):
+        return whole_of(chain(feed(scene, 0), feed(scene, 1)), 2200)
+
+    def backs(*which):
+        return [whole_of(back(*one), 5400) for one in which]
+
+    merge(*attends(0), *attends(1), apart=0.02)
+    merge(feeds(0), feeds(1))
+    merge(whole_of(head(0), 7600), whole_of(head(1), 7600), apart=0.05)
+    merge(*backs((0, 0), (0, 1), (1, 0), (1, 1)), apart=0.04)
 
     bits = bits_of(parts)
     line = iota((GAIN_ROWS, C), 0)
@@ -606,22 +673,13 @@
         compiler_params=pltpu.CompilerParams(vmem_limit_bytes=60 * MIB),
         name="pack",
     )
-    shard = pack(
-        gain_self.reshape(1, rows),
-        gain_cross.reshape(1, rows),
-        gain_ff.reshape(1, rows),
-        self_qkv,
-        self_out,
-        cross_qkv,
-        cross_out,
-        ff_in,
-        ff_out,
-        refine,
-    )
+    own = [gain.reshape(1, rows) for gain in (gain_self, gain_cross, gain_ff)]
+    own += [self_qkv, self_out, cross_qkv, cross_out, ff_in, ff_out, refine]
+    shard = pack(*own)
     packed = {0: shard}
     for bit in reversed(range(bits_of(parts))):
         packed |= {apart | (1 << bit): exchange(piece, 1 << bit, 0) for apart, piece in packed.items()}
-    packed = [packed[apart] for apart in range(parts)]
+    packed = [packed[apart] for apart in range(1, parts)]
 
     steps = scenes * (HV // WIN)
     span = 2 * TOK
@@ -629,7 +687,7 @@
         ((C, 3 * C), BF16), ((C, C), BF16), ((C, 3 * C), BF16), ((C, C), BF16),
         ((C, FFH), BF16), ((FFH, C), BF16), ((C, 9 * PLANES), BF16),
         ((3 * C, C), BF16), ((C, C), BF16), ((3 * C, C), BF16), ((C, C), BF16),
-        ((FFH, C), BF16), ((C, FFH), BF16), ((9 * PLANES, C), BF16), ((9 * PLANES, C), BF16),
+        ((FFH, C), BF16), ((C, FFH), BF16), ((12 * PLANES, 2 * C), BF16), ((12 * PLANES, 2 * C), BF16),
         ((8, C), F32),
         ((scenes, TOK, TOK), F32),
         ((steps, VIEWS, WIN, 2, WIN, C), F32),
@@ -658,7 +716,7 @@
             jax.ShapeDtypeStruct((parts // 2, shard_rows, C), BF16),
             jax.ShapeDtypeStruct((parts // 2, shard_rows, C), BF16),
         ),
-        in_specs=[SMEM, HBM] + [VMEM] * (2 + parts),
+        in_specs=[SMEM, HBM] + [VMEM] * (11 + parts),
         out_specs=(VMEM, HBM, VMEM, VMEM),
         scratch_shapes=[pltpu.VMEM(shape, kind) for shape, kind in scratch]
         + [
@@ -669,7 +727,7 @@
         compiler_params=pltpu.CompilerParams(vmem_limit_bytes=52 * MIB),
         name="layer",
     )
-    depth, grad_features, keep, send = main(view_count, features, plane_offsets, depth_grad, *packed)
+    depth, grad_features, keep, send = main(view_count, features, plane_offsets, depth_grad, *own, *packed)
 
     for bit in range(bits_of(parts)):
         if bit > 0:

time: 66.4 us -> 60 us (0.904)
  Pallas kernels: 29.4 us -> 23.8 us
  local copies, waits for them, and re-layouts: 0.96 us -> 0.08 us
    pallas_call x2, Pallas kernels: 28.5 us -> 22.9 us  [the longest x1 21.1 us: local(): main(view_count, features, plane_offsets, depth_grad, *own, *packed)]
    unnamed x8 -> x26, local copies, waits for them, and re-layouts: 0.94 us -> 0.05 us
where the time goes in v3:
time: 60 us; the launch traced here: 59.8 us
  Pallas kernels  23.8 us (40%)
  waiting for transfers between devices  21.7 us (36%)
  starting transfers between devices  13.1 us (22%)
  between operations  0.88 us (1%)
    ppermute x11, waiting for transfers between devices, exchange(): lax.ppermute(value, ('dp', 'fsdp'), [(i, i ^ mask) for i in range(count)])  21.7 us
    pallas_call x1, Pallas kernels, local(): main(view_count, features, plane_offsets, depth_grad, *own, *packed)  21.1 us
    ppermute x11, starting transfers between devices, exchange(): lax.ppermute(value, ('dp', 'fsdp'), [(i, i ^ mask) for i in range(count)])  13.1 us
    pallas_call x1, Pallas kernels, local(): shard = pack(*own)  1.88 us
  transfers between devices with their start and end apart: 11, of which 9 were waited for; matrix products, arithmetic and copies ran while one was open for 0% of the time, Pallas kernels for 0%

profile of v3, /device:TPU:0, one launch (start us, length us, event | category | flops | bytes accessed | tf_op | source)
XLA Modules:
  0.0 59.8 jit_solution(13043080066658603462)
XLA Ops:
  0.8 1.9 %pack.1 = bf16[832,128]{1,0:T(8,128)(2,1)} custom-call(bf16[1,32]{1,0:T(2,128)(2,1)} %bitcast.18, bf16[1,32]{1,0:T(2,128)(2,1)} %bitcast.20, bf16[1,32]{1,0:T(2,128)(2,1)} %bitcast.22, bf16[32,384]{1,0:T(8,128)(2,1)} %refs_3_.3, bf16[32,128]{1,0:T(8,128)(2,1)} %refs_4_.3, bf16[32,384]{1,0:T(8,128)(2,1)} %refs_5_.3, bf16[32,128]{1,0:T(8,128)(2,1)} %refs_6_.3, ...), custom_call_target="tpu_custom_call" | custom-call | tf_op jit(solution)/shard_map/pack/pallas_call | solution.py:678
  2.7 3.0 %collective-permute-start.1 = (bf16[832,128]{1,0:T(8,128)(2,1)}, bf16[832,128]{1,0:T(8,128)(2,1)S(1)}, u32[]{:S(2)}, u32[]{:S(2)}) collective-permute-start(bf16[832,128]{1,0:T(8,128)(2,1)} %pack.1), channel_id=1, source_target_pairs={{0,2},{1,3},{2,0},{3,1},{4,6},{5,7},{6,4},{7,5},{8,10},{9,11},{10,... | collective-permute-start | bytes 638984 | tf_op jit(solution)/shard_map/ppermute | solution.py:641
  5.7 5.5 %collective-permute-done.1.refs_11_ = bf16[832,128]{1,0:T(8,128)(2,1)S(1)} collective-permute-done((bf16[832,128]{1,0:T(8,128)(2,1)}, bf16[832,128]{1,0:T(8,128)(2,1)S(1)}, u32[]{:S(2)}, u32[]{:S(2)}) %collective-permute-start.1) | collective-permute-done | bytes 213024 | tf_op jit(solution)/shard_map/ppermute | solution.py:641
  11.2 0.0 collective-permute-start.2
  11.2 1.5 %collective-permute-done.2.refs_12_ = bf16[832,128]{1,0:T(8,128)(2,1)S(1)} collective-permute-done((bf16[832,128]{1,0:T(8,128)(2,1)S(1)}, bf16[832,128]{1,0:T(8,128)(2,1)S(1)}, u32[]{:S(2)}, u32[]{:S(2)}) %collective-permute-start.2) | collective-permute-done | bytes 213024 | tf_op jit(solution)/shard_map/ppermute | solution.py:641
  12.7 21.1 %layer.1 = (f32[2,4,256]{2,1,0:T(4,128)}, f32[2,4,2,8,2,8,128]{6,5,4,3,2,1,0:T(8,128)}, bf16[2,832,128]{2,1,0:T(8,128)(2,1)S(1)}, bf16[2,832,128]{2,1,0:T(8,128)(2,1)S(1)}) custom-call(s32[2]{0:T(128)S(1)} %copy-done.12, bf16[2,4,256,128]{3,2,1,0:T(8,128)(2,1)} %features_hbm.1, s32[2,4,128]{2,1,0:T(4,128)S(1)} %copy-done.8, f32[2,4,256]{2,1,0:T(4,128)S(1)} %copy-done.7, ...), custom_call_target="tpu_custom_call" | custom-call | tf_op jit(solution)/shard_map/layer/pallas_call | solution.py:730
  33.8 0.2 collective-permute-start.3
  34.0 1.6 %collective-permute-done.3 = bf16[2,832,128]{2,1,0:T(8,128)(2,1)S(1)} collective-permute-done((bf16[2,832,128]{2,1,0:T(8,128)(2,1)S(1)}, bf16[2,832,128]{2,1,0:T(8,128)(2,1)S(1)}, u32[]{:S(2)}, u32[]{:S(2)}) %collective-permute-start.3) | collective-permute-done | bytes 426016 | tf_op jit(solution)/shard_map/ppermute | solution.py:641
  35.6 0.1 add.15
  35.8 1.8 %collective-permute-start.4 = (bf16[416,128]{1,0:T(8,128)(2,1)S(1)}, bf16[416,128]{1,0:T(8,128)(2,1)S(1)}, u32[]{:S(2)}, u32[]{:S(2)}) collective-permute-start(bf16[416,128]{1,0:T(8,128)(2,1)S(1)} %get-tuple-element.40), channel_id=1, source_target_pairs={{0,2},{1,3},{2,0},{3,1},{4,6},{5,7},{6,4},{7,5},{8,10},{9,11},{10,... | collective-permute-start | bytes 319496 | tf_op jit(solution)/shard_map/ppermute | solution.py:641
  37.6 1.4 %collective-permute-start.6 = (bf16[416,128]{1,0:T(8,128)(2,1)S(1)}, bf16[416,128]{1,0:T(8,128)(2,1)S(1)}, u32[]{:S(2)}, u32[]{:S(2)}) collective-permute-start(bf16[416,128]{1,0:T(8,128)(2,1)S(1)} %get-tuple-element.41), channel_id=1, source_target_pairs={{0,6},{1,7},{2,4},{3,5},{4,2},{5,3},{6,0},{7,1},{8,14},{9,15},{10,... | collective-permute-start | bytes 319496 | tf_op jit(solution)/shard_map/ppermute | solution.py:641
  39.0 0.3 collective-permute-start.5
  39.3 3.1 %collective-permute-done.4 = bf16[416,128]{1,0:T(8,128)(2,1)S(1)} collective-permute-done((bf16[416,128]{1,0:T(8,128)(2,1)S(1)}, bf16[416,128]{1,0:T(8,128)(2,1)S(1)}, u32[]{:S(2)}, u32[]{:S(2)}) %collective-permute-start.4) | collective-permute-done | bytes 106528 | tf_op jit(solution)/shard_map/ppermute | solution.py:641
  42.4 1.8 %collective-permute-done.6 = bf16[416,128]{1,0:T(8,128)(2,1)S(1)} collective-permute-done((bf16[416,128]{1,0:T(8,128)(2,1)S(1)}, bf16[416,128]{1,0:T(8,128)(2,1)S(1)}, u32[]{:S(2)}, u32[]{:S(2)}) %collective-permute-start.6) | collective-permute-done | bytes 106528 | tf_op jit(solution)/shard_map/ppermute | solution.py:641
  44.3 0.2 collective-permute-done.5
  44.5 0.1 fusion.1
  44.5 2.8 %collective-permute-start.7 = (bf16[416,128]{1,0:T(8,128)(2,1)S(1)}, bf16[416,128]{1,0:T(8,128)(2,1)S(1)}, u32[]{:S(2)}, u32[]{:S(2)}) collective-permute-start(bf16[416,128]{1,0:T(8,128)(2,1)S(1)} %fusion.1), channel_id=1, source_target_pairs={{0,16},{1,17},{2,18},{3,19},{4,20},{5,21},{6,22},{7,23},{8,24},{9,... | collective-permute-start | bytes 319496 | tf_op jit(solution)/shard_map/ppermute | solution.py:641
  47.3 4.5 %collective-permute-done.7 = bf16[416,128]{1,0:T(8,128)(2,1)S(1)} collective-permute-done((bf16[416,128]{1,0:T(8,128)(2,1)S(1)}, bf16[416,128]{1,0:T(8,128)(2,1)S(1)}, u32[]{:S(2)}, u32[]{:S(2)}) %collective-permute-start.7) | collective-permute-done | bytes 106528 | tf_op jit(solution)/shard_map/ppermute | solution.py:641
  51.8 1.7 %collective-permute-start.10 = (bf16[416,128]{1,0:T(8,128)(2,1)S(1)}, bf16[416,128]{1,0:T(8,128)(2,1)S(1)}, u32[]{:S(2)}, u32[]{:S(2)}) collective-permute-start(bf16[416,128]{1,0:T(8,128)(2,1)S(1)} %add.19.refs_0_), channel_id=1, source_target_pairs={{0,12},{1,13},{2,14},{3,15},{4,8},{5,9},{6,10},{7,11},{8,4},{9,5},... | collective-permute-start | bytes 319496 | tf_op jit(solution)/shard_map/ppermute | solution.py:641
  53.5 0.5 collective-permute-start.9
  54.0 1.3 %collective-permute-start.8 = (bf16[416,128]{1,0:T(8,128)(2,1)S(1)}, bf16[416,128]{1,0:T(8,128)(2,1)S(1)}, u32[]{:S(2)}, u32[]{:S(2)}) collective-permute-start(bf16[416,128]{1,0:T(8,128)(2,1)S(1)} %add.19.refs_0_), channel_id=1, source_target_pairs={{0,8},{1,9},{2,10},{3,11},{4,12},{5,13},{6,14},{7,15},{8,0},{9,1},... | collective-permute-start | bytes 319496 | tf_op jit(solution)/shard_map/ppermute | solution.py:641
  55.4 3.0 %collective-permute-done.10.refs_3_ = bf16[416,128]{1,0:T(8,128)(2,1)S(1)} collective-permute-done((bf16[416,128]{1,0:T(8,128)(2,1)S(1)}, bf16[416,128]{1,0:T(8,128)(2,1)S(1)}, u32[]{:S(2)}, u32[]{:S(2)}) %collective-permute-start.10) | collective-permute-done | bytes 106528 | tf_op jit(solution)/shard_map/ppermute | solution.py:641
  58.4 0.6 collective-permute-done.9.refs_2_
  58.9 0.9 %unpack.1 = (f32[1,32]{1,0:T(1,128)}, f32[1,32]{1,0:T(1,128)}, f32[1,32]{1,0:T(1,128)}, f32[32,384]{1,0:T(8,128)}, f32[32,128]{1,0:T(8,128)}, /*index=5*/f32[32,...) custom-call(bf16[416,128]{1,0:T(8,128)(2,1)S(1)} %add.19.refs_0_, ...), custom_call_target="tpu_custom_call" | custom-call | tf_op jit(solution)/shard_map/unpack/pallas_call | solution.py:767
  (31 shorter events, 0.1 us)
Async XLA Ops:
  0.6 12.0 %copy-start = (bf16[32,1152]{1,0:T(8,128)(2,1)S(1)}, bf16[32,1152]{1,0:T(8,128)(2,1)}, u32[]{:S(2)}) copy-start(bf16[32,1152]{1,0:T(8,128)(2,1)} %refs_9_.3) | copy-start | bytes 221188
  0.7 12.0 %copy-start.1 = (bf16[32,512]{1,0:T(8,128)(2,1)S(1)}, bf16[32,512]{1,0:T(8,128)(2,1)}, u32[]{:S(2)}) copy-start(bf16[32,512]{1,0:T(8,128)(2,1)} %refs_7_.3) | copy-start | bytes 98308
  0.7 12.0 %copy-start.2 = (bf16[128,128]{1,0:T(8,128)(2,1)S(1)}, bf16[128,128]{1,0:T(8,128)(2,1)}, u32[]{:S(2)}) copy-start(bf16[128,128]{1,0:T(8,128)(2,1)} %refs_8_.3) | copy-start | bytes 98308
  0.7 12.0 %copy-start.3 = (bf16[32,384]{1,0:T(8,128)(2,1)S(1)}, bf16[32,384]{1,0:T(8,128)(2,1)}, u32[]{:S(2)}) copy-start(bf16[32,384]{1,0:T(8,128)(2,1)} %refs_3_.3) | copy-start | bytes 73732
  0.7 12.0 %copy-start.4 = (bf16[32,384]{1,0:T(8,128)(2,1)S(1)}, bf16[32,384]{1,0:T(8,128)(2,1)}, u32[]{:S(2)}) copy-start(bf16[32,384]{1,0:T(8,128)(2,1)} %refs_5_.3) | copy-start | bytes 73732
  0.7 12.0 %copy-start.5 = (bf16[32,128]{1,0:T(8,128)(2,1)S(1)}, bf16[32,128]{1,0:T(8,128)(2,1)}, u32[]{:S(2)}) copy-start(bf16[32,128]{1,0:T(8,128)(2,1)} %refs_4_.3) | copy-start | bytes 24580
  0.7 12.0 %copy-start.6 = (bf16[32,128]{1,0:T(8,128)(2,1)S(1)}, bf16[32,128]{1,0:T(8,128)(2,1)}, u32[]{:S(2)}) copy-start(bf16[32,128]{1,0:T(8,128)(2,1)} %refs_6_.3) | copy-start | bytes 24580
  0.7 12.0 %copy-start.7 = (f32[2,4,256]{2,1,0:T(4,128)S(1)}, f32[2,4,256]{2,1,0:T(4,128)}, u32[]{:S(2)}) copy-start(f32[2,4,256]{2,1,0:T(4,128)} %depth_grad.1) | copy-start | bytes 24580
  0.7 12.0 %copy-start.8 = (s32[2,4,128]{2,1,0:T(4,128)S(1)}, s32[2,4,128]{2,1,0:T(4,128)}, u32[]{:S(2)}) copy-start(s32[2,4,128]{2,1,0:T(4,128)} %offsets.1) | copy-start | bytes 12292
  0.7 12.0 %copy-start.9 = (bf16[32]{0:T(256)(128)(2,1)S(1)}, bf16[32]{0:T(256)(128)(2,1)}, u32[]{:S(2)}) copy-start(bf16[32]{0:T(256)(128)(2,1)} %param.18) | copy-start | bytes 196
  0.7 12.0 %copy-start.10 = (bf16[32]{0:T(256)(128)(2,1)S(1)}, bf16[32]{0:T(256)(128)(2,1)}, u32[]{:S(2)}) copy-start(bf16[32]{0:T(256)(128)(2,1)} %param.21) | copy-start | bytes 196
  0.8 12.0 %copy-start.11 = (bf16[32]{0:T(256)(128)(2,1)S(1)}, bf16[32]{0:T(256)(128)(2,1)}, u32[]{:S(2)}) copy-start(bf16[32]{0:T(256)(128)(2,1)} %param.24) | copy-start | bytes 196
  0.8 12.0 %copy-start.12 = (s32[2]{0:T(128)S(1)}, s32[2]{0:T(128)}, u32[]{:S(2)}) copy-start(s32[2]{0:T(128)} %count_ref.1) | copy-start | bytes 28
  2.7 8.5 %collective-permute-start.1 = (bf16[832,128]{1,0:T(8,128)(2,1)}, bf16[832,128]{1,0:T(8,128)(2,1)S(1)}, u32[]{:S(2)}, u32[]{:S(2)}) collective-permute-start(bf16[832,128]{1,0:T(8,128)(2,1)} %pack.1), channel_id=1, source_target_pairs={{0,2},{1,3},{2,0},{3,1},{4,6},{5,7},{6,4},{7,5},{8,10},{9,11},{10,... | collective-permute-start | bytes 638984 | tf_op jit(solution)/shard_map/ppermute | solution.py:641
  5.7 5.5 %collective-permute-start = (bf16[832,128]{1,0:T(8,128)(2,1)}, bf16[832,128]{1,0:T(8,128)(2,1)S(1)}, u32[]{:S(2)}, u32[]{:S(2)}) collective-permute-start(bf16[832,128]{1,0:T(8,128)(2,1)} %pack.1), channel_id=1, source_target_pairs={{0,1},{1,0},{2,3},{3,2},{4,5},{5,4},{6,7},{7,6},{8,9},{9,8},{10,11... | collective-permute-start | bytes 638984 | tf_op jit(solution)/shard_map/ppermute | solution.py:641
  11.2 1.5 %collective-permute-start.2 = (bf16[832,128]{1,0:T(8,128)(2,1)S(1)}, bf16[832,128]{1,0:T(8,128)(2,1)S(1)}, u32[]{:S(2)}, u32[]{:S(2)}) collective-permute-start(bf16[832,128]{1,0:T(8,128)(2,1)S(1)} %collective-permute-done.1.refs_11_), channel_id=1, source_target_pairs={{0,1},{1,0},{2,3},{3,2},{4,5},{5,4},{6,7},{7,6},{8,9},{9,8},{10,11... | collective-permute-start | bytes 638984 | tf_op jit(solution)/shard_map/ppermute | solution.py:641
  33.8 1.8 %collective-permute-start.3 = (bf16[2,832,128]{2,1,0:T(8,128)(2,1)S(1)}, bf16[2,832,128]{2,1,0:T(8,128)(2,1)S(1)}, u32[]{:S(2)}, u32[]{:S(2)}) collective-permute-start(bf16[2,832,128]{2,1,0:T(8,128)(2,1)S(1)} %get-tuple-element.29), channel_id=1, source_target_pairs={{0,1},{1,0},{2,3},{3,2},{4,5},{5,4},{6,7},{7,6},{8,9},{9,8},{10,11... | collective-permute-start | bytes 1277960 | tf_op jit(solution)/shard_map/ppermute | solution.py:641
  35.8 6.7 %collective-permute-start.4 = (bf16[416,128]{1,0:T(8,128)(2,1)S(1)}, bf16[416,128]{1,0:T(8,128)(2,1)S(1)}, u32[]{:S(2)}, u32[]{:S(2)}) collective-permute-start(bf16[416,128]{1,0:T(8,128)(2,1)S(1)} %get-tuple-element.40), channel_id=1, source_target_pairs={{0,2},{1,3},{2,0},{3,1},{4,6},{5,7},{6,4},{7,5},{8,10},{9,11},{10,... | collective-permute-start | bytes 319496 | tf_op jit(solution)/shard_map/ppermute | solution.py:641
  37.6 6.7 %collective-permute-start.6 = (bf16[416,128]{1,0:T(8,128)(2,1)S(1)}, bf16[416,128]{1,0:T(8,128)(2,1)S(1)}, u32[]{:S(2)}, u32[]{:S(2)}) collective-permute-start(bf16[416,128]{1,0:T(8,128)(2,1)S(1)} %get-tuple-element.41), channel_id=1, source_target_pairs={{0,6},{1,7},{2,4},{3,5},{4,2},{5,3},{6,0},{7,1},{8,14},{9,15},{10,... | collective-permute-start | bytes 319496 | tf_op jit(solution)/shard_map/ppermute | solution.py:641
  39.0 5.4 %collective-permute-start.5 = (bf16[416,128]{1,0:T(8,128)(2,1)S(1)}, bf16[416,128]{1,0:T(8,128)(2,1)S(1)}, u32[]{:S(2)}, u32[]{:S(2)}) collective-permute-start(bf16[416,128]{1,0:T(8,128)(2,1)S(1)} %get-tuple-element.42), channel_id=1, source_target_pairs={{0,4},{1,5},{2,6},{3,7},{4,0},{5,1},{6,2},{7,3},{8,12},{9,13},{10,... | collective-permute-start | bytes 319496 | tf_op jit(solution)/shard_map/ppermute | solution.py:641
  44.5 7.3 %collective-permute-start.7 = (bf16[416,128]{1,0:T(8,128)(2,1)S(1)}, bf16[416,128]{1,0:T(8,128)(2,1)S(1)}, u32[]{:S(2)}, u32[]{:S(2)}) collective-permute-start(bf16[416,128]{1,0:T(8,128)(2,1)S(1)} %fusion.1), channel_id=1, source_target_pairs={{0,16},{1,17},{2,18},{3,19},{4,20},{5,21},{6,22},{7,23},{8,24},{9,... | collective-permute-start | bytes 319496 | tf_op jit(solution)/shard_map/ppermute | solution.py:641
  51.8 6.5 %collective-permute-start.10 = (bf16[416,128]{1,0:T(8,128)(2,1)S(1)}, bf16[416,128]{1,0:T(8,128)(2,1)S(1)}, u32[]{:S(2)}, u32[]{:S(2)}) collective-permute-start(bf16[416,128]{1,0:T(8,128)(2,1)S(1)} %add.19.refs_0_), channel_id=1, source_target_pairs={{0,12},{1,13},{2,14},{3,15},{4,8},{5,9},{6,10},{7,11},{8,4},{9,5},... | collective-permute-start | bytes 319496 | tf_op jit(solution)/shard_map/ppermute | solution.py:641
  53.5 5.4 %collective-permute-start.9 = (bf16[416,128]{1,0:T(8,128)(2,1)S(1)}, bf16[416,128]{1,0:T(8,128)(2,1)S(1)}, u32[]{:S(2)}, u32[]{:S(2)}) collective-permute-start(bf16[416,128]{1,0:T(8,128)(2,1)S(1)} %add.19.refs_0_), channel_id=1, source_target_pairs={{0,4},{1,5},{2,6},{3,7},{4,0},{5,1},{6,2},{7,3},{8,12},{9,13},{10,... | collective-permute-start | bytes 319496 | tf_op jit(solution)/shard_map/ppermute | solution.py:641
  54.0 4.9 %collective-permute-start.8 = (bf16[416,128]{1,0:T(8,128)(2,1)S(1)}, bf16[416,128]{1,0:T(8,128)(2,1)S(1)}, u32[]{:S(2)}, u32[]{:S(2)}) collective-permute-start(bf16[416,128]{1,0:T(8,128)(2,1)S(1)} %add.19.refs_0_), channel_id=1, source_target_pairs={{0,8},{1,9},{2,10},{3,11},{4,12},{5,13},{6,14},{7,15},{8,0},{9,1},... | collective-permute-start | bytes 319496 | tf_op jit(solution)/shard_map/ppermute | solution.py:641

commit v4 on v3

--- a/solution.py
+++ b/solution.py
@@ -186,11 +186,30 @@
     return jnp.concatenate(pieces, 0)
 
 
+def start_kernel(scenes, features, x0s, xhats, rstds):
+    for scene in range(scenes):
+        for half in range(2):
+            step = 2 * scene + half
+            piece = features[scene, :, half * HALF : (half + 1) * HALF, :]
+            piece = piece.astype(F32).reshape(VIEWS, WIN, 2, WIN, C)
+            for side in range(2):
+                spot = slice(side * TOK, (side + 1) * TOK)
+                x0 = piece[:, :, side].reshape(TOK, C)
+                centred = x0 - jnp.mean(x0, -1, keepdims=True)
+                spread = jnp.mean(centred * centred, -1, keepdims=True)
+                rstd = lax.rsqrt(spread + 1e-05)
+                x0s[step, spot, :] = x0
+                xhats[step, spot, :] = centred * rstd
+                rstds[step, spot, :] = jnp.broadcast_to(rstd, x0.shape)
+
+
 def main_kernel(
     scenes,
     parts,
     count_ref,
-    features_hbm,
+    x0s,
+    xh_a,
+    rs_a,
     offsets,
     depth_grad,
     *refs,
@@ -198,15 +217,15 @@
     own_gains, own, packed, refs = refs[:3], refs[3:10], refs[10 : 9 + parts], refs[9 + parts :]
     (
     depth_out,
-    grad_hbm,
+    grad_out,
     keep_out,
     send_out,
     w_sq, w_so, w_cq, w_co, w_fi, w_fo, w_rf,
     t_sq, t_so, t_cq, t_co, t_fi, t_fo, t_rf, b_rf,
     gains,
     bias,
-    x0s, x2s,
-    xh_a, xh_b, xh_c, rs_a, rs_b, rs_c,
+    x2s,
+    xh_b, xh_c, rs_b, rs_c,
     no_a, no_b, no_c,
     qkv_a, qkv_b, p_a, p_b, o_a, o_b,
     gd, act,
@@ -215,13 +234,9 @@
     pads, taps, back_taps,
     tables, eye, flip, hots,
     g_sq, g_so, g_cq, g_co, g_fi, g_fo, g_rf, g_gain,
-    features, grad_out, sems,
     ) = refs
     rows = C // parts
     me, side_of_rows = place_of(parts)
-    bring = pltpu.make_async_copy(features_hbm, features, sems.at[0])
-    bring.start()
-    sent = []
 
     total = gain_lines(parts, own_gains)
     for apart in range(parts):
@@ -291,16 +306,10 @@
     def attend(scene, half, side):
         step = 2 * scene + half
         spot = places[side]
-        if side == 0:
-            piece = features[scene, :, half * HALF : (half + 1) * HALF, :]
-            x0s[step] = piece.astype(F32).reshape(VIEWS, WIN, 2, WIN, C)
-            yield 60
-        x0 = x0s[step, :, :, side].reshape(TOK, C)
-        xhat, rstd, normed = norm_forward(x0, gain_a)
-        xh_a[step, spot, :] = xhat
-        rs_a[step, spot, :] = rstd
+        x0 = x0s[step, spot, :]
+        normed = (xh_a[step, spot, :] * gain_a).astype(BF16)
         no_a[step, spot, :] = normed
-        yield 400
+        yield 100
         qkv = mm(normed, w_sq[...]).astype(BF16)
         qkv_a[step, spot, :] = qkv
         yield 300
@@ -419,7 +428,7 @@
             valid = jnp.where(view < live, 1.0, 0.0)
             incoming = []
             for at in upper:
-                depth_out[scene, view : view + 1, at] = jnp.sum(eye[...] * depth[at], 0, keepdims=True) * valid
+                depth_out[scene, view : view + 1, at] = jnp.sum(eye[...] * depth[at], 0, keepdims=True)
                 incoming.append(jnp.sum(eye[...] * depth_grad[scene, view : view + 1, at], 1, keepdims=True))
             weight = joined(incoming) * (inverse * valid)
             d_refined.append(expo * (weight * depth_values - weight * depth))
@@ -559,12 +568,8 @@
             spot = places[side]
             d_hidden, d_gain = norm_backward(d_normed[side], xh_a[step, spot, :], rs_a[step, spot, :], gain_a)
             g_gain[0] += d_gain
-            grad_out[scene, :, half, :, side] = (d1[side] + d_hidden).reshape(VIEWS, WIN, WIN, C)
+            grad_out[step, spot, :] = d1[side] + d_hidden
             yield 150
-        sent.append(
-            pltpu.make_async_copy(grad_out.at[scene, :, half], grad_hbm.at[scene, :, half], sems.at[1 + step])
-        )
-        sent[-1].start()
 
     def chain(*threads):
         for thread in threads:
@@ -573,7 +578,6 @@
     def feeds(scene):
         return chain(feed(scene, 0), feed(scene, 1))
 
-    bring.wait()
     def whole_of(thread, total):
         return paced(thread, 1.0 / total)
 
@@ -625,8 +629,6 @@
         put(at, gain_rows)
         if at + GAIN_ROWS < rows_of(parts):
             put(at + GAIN_ROWS, jnp.zeros((rows_of(parts) - at - GAIN_ROWS, C), BF16))
-    for one in sent:
-        one.wait()
 
 
 VMEM = pl.BlockSpec(memory_space=pltpu.VMEM)
@@ -676,13 +678,27 @@
     own = [gain.reshape(1, rows) for gain in (gain_self, gain_cross, gain_ff)]
     own += [self_qkv, self_out, cross_qkv, cross_out, ff_in, ff_out, refine]
     shard = pack(*own)
+    steps = scenes * (HV // WIN)
+    span = 2 * TOK
+    start = pl.pallas_call(
+        functools.partial(start_kernel, scenes),
+        out_shape=(jax.ShapeDtypeStruct((steps, span, C), F32),) * 3,
+        in_specs=[VMEM],
+        out_specs=(VMEM,) * 3,
+        compiler_params=small,
+        cost_estimate=pl.CostEstimate(flops=10 * features.size, bytes_accessed=14 * features.size, transcendentals=0),
+        name="start",
+    )
+    began = start(features)
+
     packed = {0: shard}
     for bit in reversed(range(bits_of(parts))):
-        packed |= {apart | (1 << bit): exchange(piece, 1 << bit, 0) for apart, piece in packed.items()}
+        came = {apart | (1 << bit): exchange(piece, 1 << bit, 0) for apart, piece in packed.items()}
+        if len(packed) == 1:
+            came, began = lax.optimization_barrier((came, began))
+        packed |= came
     packed = [packed[apart] for apart in range(1, parts)]
 
-    steps = scenes * (HV // WIN)
-    span = 2 * TOK
     scratch = [
         ((C, 3 * C), BF16), ((C, C), BF16), ((C, 3 * C), BF16), ((C, C), BF16),
         ((C, FFH), BF16), ((FFH, C), BF16), ((C, 9 * PLANES), BF16),
@@ -690,10 +706,9 @@
         ((FFH, C), BF16), ((C, FFH), BF16), ((12 * PLANES, 2 * C), BF16), ((12 * PLANES, 2 * C), BF16),
         ((8, C), F32),
         ((scenes, TOK, TOK), F32),
-        ((steps, VIEWS, WIN, 2, WIN, C), F32),
         ((steps, span, C), F32),
     ]
-    scratch += [((steps, span, C), F32)] * 6
+    scratch += [((steps, span, C), F32)] * 4
     scratch += [((steps, span, C), BF16)] * 3
     scratch += [
         ((steps, span, 3 * C), BF16), ((steps, span, 3 * C), BF16),
@@ -712,22 +727,21 @@
         functools.partial(main_kernel, scenes, parts),
         out_shape=(
             jax.ShapeDtypeStruct((scenes, VIEWS, PIX), F32),
-            jax.ShapeDtypeStruct((scenes, VIEWS, 2, WIN, 2, WIN, C), F32),
+            jax.ShapeDtypeStruct((steps, span, C), F32),
             jax.ShapeDtypeStruct((parts // 2, shard_rows, C), BF16),
             jax.ShapeDtypeStruct((parts // 2, shard_rows, C), BF16),
         ),
-        in_specs=[SMEM, HBM] + [VMEM] * (11 + parts),
-        out_specs=(VMEM, HBM, VMEM, VMEM),
+        in_specs=[SMEM] + [VMEM] * (14 + parts),
+        out_specs=(VMEM,) * 4,
         scratch_shapes=[pltpu.VMEM(shape, kind) for shape, kind in scratch]
-        + [
-            pltpu.VMEM(features.shape, BF16),
-            pltpu.VMEM((scenes, VIEWS, 2, WIN, 2, WIN, C), F32),
-            pltpu.SemaphoreType.DMA((1 + steps,)),
-        ],
-        compiler_params=pltpu.CompilerParams(vmem_limit_bytes=52 * MIB),
+,
+        compiler_params=pltpu.CompilerParams(vmem_limit_bytes=46 * MIB),
         name="layer",
     )
-    depth, grad_features, keep, send = main(view_count, features, plane_offsets, depth_grad, *own, *packed)
+    depth, grad_features, keep, send = main(view_count, *began, plane_offsets, depth_grad, *own, *packed)
+
+    grad_features = grad_features.reshape(scenes, 2, 2, VIEWS, WIN, WIN, C).transpose(0, 3, 1, 4, 2, 5, 6)
+    grad_features = grad_features.reshape(features.shape)
 
     for bit in range(bits_of(parts)):
         if bit > 0:
@@ -766,8 +780,8 @@
     )
     ga, gb, gc, d_sq, d_so, d_cq, d_co, d_fi, d_fo, d_rf = unpack(*own, *other)
     return (
-        depth,
-        grad_features.reshape(features.shape),
+        depth * (jnp.arange(VIEWS) < view_count[:, None])[:, :, None],
+        grad_features,
         ga.reshape(rows),
         d_sq,
         d_so,

time: 60 us -> 57.3 us (0.955)
  waiting for transfers between devices: 21.7 us -> 18.6 us
  Pallas kernels: 23.8 us -> 21.5 us
  local copies, waits for them, and re-layouts: 0.08 us -> 2.18 us
  other arithmetic: 0.21 us -> 0.94 us
    ppermute x11, waiting for transfers between devices: 21.7 us -> 18.6 us  [exchange(): lax.ppermute(value, ('dp', 'fsdp'), [(i, i ^ mask) for i in range(count)])]
    pallas_call x1 -> x2, Pallas kernels: 21.1 us -> 18.7 us  [the longest x1 17.8 us: local(): main(view_count, *began, plane_offsets, depth_grad, *own, *packed)]
    transpose x0 -> x1, local copies, waits for them, and re-layouts: none -> 1.06 us  [local(): grad_features.reshape(scenes, 2, 2, VIEWS, WIN, WIN, C)]
    unnamed x26 -> x28, local copies, waits for them, and re-layouts: 0.05 us -> 1.09 us
    mul x0 -> x1, other arithmetic: none -> 0.67 us  [local(): depth * (jnp.arange(VIEWS) < view_count[:, None])[:, :, None]]
  transfers between devices with their start and end apart: 11 -> 11, of which waited for: 9 -> 10; matrix products, arithmetic and copies ran while one was open for 0% -> 3% of each run, Pallas kernels for 0% -> 2%
where the time goes in v4:
time: 57.3 us; the launch traced here: 57.1 us
  Pallas kernels  21.5 us (38%)
  waiting for transfers between devices  18.6 us (32%)
  starting transfers between devices  13 us (23%)
  local copies, waits for them, and re-layouts  2.18 us (4%)
  other arithmetic  0.94 us (2%)
  between operations  0.85 us (1%)
    ppermute x11, waiting for transfers between devices, exchange(): lax.ppermute(value, ('dp', 'fsdp'), [(i, i ^ mask) for i in range(count)])  18.6 us
    pallas_call x1, Pallas kernels, local(): main(view_count, *began, plane_offsets, depth_grad, *own, *packed)  17.8 us
    ppermute x11, starting transfers between devices, exchange(): lax.ppermute(value, ('dp', 'fsdp'), [(i, i ^ mask) for i in range(count)])  13 us
    pallas_call x1, Pallas kernels, local(): shard = pack(*own)  1.87 us
  transfers between devices with their start and end apart: 11, of which 10 were waited for; matrix products, arithmetic and copies ran while one was open for 3% of the time, Pallas kernels for 2%

profile of v4, /device:TPU:0, one launch (start us, length us, event | category | flops | bytes accessed | tf_op | source)
XLA Modules:
  0.0 57.1 jit_solution(18202624234455024998)
XLA Ops:
  0.7 1.9 %pack.1 = bf16[832,128]{1,0:T(8,128)(2,1)} custom-call(bf16[1,32]{1,0:T(2,128)(2,1)} %bitcast.22, bf16[1,32]{1,0:T(2,128)(2,1)} %bitcast.24, bf16[1,32]{1,0:T(2,128)(2,1)} %bitcast.26, bf16[32,384]{1,0:T(8,128)(2,1)} %refs_3_.3, bf16[32,128]{1,0:T(8,128)(2,1)} %refs_4_.3, bf16[32,384]{1,0:T(8,128)(2,1)} %refs_5_.3, bf16[32,128]{1,0:T(8,128)(2,1)} %refs_6_.3, ...), custom_call_target="tpu_custom_call" | custom-call | tf_op jit(solution)/shard_map/pack/pallas_call | solution.py:680
  2.6 3.0 %collective-permute-start = (bf16[832,128]{1,0:T(8,128)(2,1)}, bf16[832,128]{1,0:T(8,128)(2,1)S(1)}, u32[]{:S(2)}, u32[]{:S(2)}) collective-permute-start(bf16[832,128]{1,0:T(8,128)(2,1)} %pack.1), channel_id=1, source_target_pairs={{0,2},{1,3},{2,0},{3,1},{4,6},{5,7},{6,4},{7,5},{8,10},{9,11},{10,... | collective-permute-start | bytes 638984 | tf_op jit(solution)/shard_map/ppermute | solution.py:643
  5.6 1.0 %copy-done = bf16[2,4,256,128]{3,2,1,0:T(8,128)(2,1)S(1)} copy-done((bf16[2,4,256,128]{3,2,1,0:T(8,128)(2,1)S(1)}, bf16[2,4,256,128]{3,2,1,0:T(8,128)(2,1)}, u32[]{:S(2)}) %copy-start) | copy-done | bytes 524312
  6.7 0.9 %start.1 = (f32[4,512,128]{2,1,0:T(8,128)S(1)}, f32[4,512,128]{2,1,0:T(8,128)S(1)}, f32[4,512,128]{2,1,0:T(8,128)S(1)}) custom-call(bf16[2,4,256,128]{3,2,1,0:T(8,128)(2,1)S(1)} %copy-done), custom_call_target="tpu_custom_call" | custom-call | flops 2621440 | bytes 3670016 | tf_op jit(solution)/shard_map/start/pallas_call | solution.py:692
  7.6 3.4 %collective-permute-done.refs_11_ = bf16[832,128]{1,0:T(8,128)(2,1)S(1)} collective-permute-done((bf16[832,128]{1,0:T(8,128)(2,1)}, bf16[832,128]{1,0:T(8,128)(2,1)S(1)}, u32[]{:S(2)}, u32[]{:S(2)}) %collective-permute-start) | collective-permute-done | bytes 213024 | tf_op jit(solution)/shard_map/ppermute | solution.py:643
  11.1 1.4 %collective-permute-done.2.refs_12_ = bf16[832,128]{1,0:T(8,128)(2,1)S(1)} collective-permute-done((bf16[832,128]{1,0:T(8,128)(2,1)S(1)}, bf16[832,128]{1,0:T(8,128)(2,1)S(1)}, u32[]{:S(2)}, u32[]{:S(2)}) %collective-permute-start.2) | collective-permute-done | bytes 213024 | tf_op jit(solution)/shard_map/ppermute | solution.py:643
  12.7 17.8 %layer.1 = (f32[2,4,256]{2,1,0:T(4,128)S(1)}, f32[4,512,128]{2,1,0:T(8,128)S(1)}, bf16[2,832,128]{2,1,0:T(8,128)(2,1)S(1)}, bf16[2,832,128]{2,1,0:T(8,128)(2,1)S(1)}) custom-call(s32[2]{0:T(128)S(1)} %copy-done.13, f32[4,512,128]{2,1,0:T(8,128)S(1)} %get-tuple-element.36.x0s, f32[4,512,128]{2,1,0:T(8,128)S(1)} %get-tuple-element.37.xh_a, ...), custom_call_target="tpu_custom_call" | custom-call | tf_op jit(solution)/shard_map/layer/pallas_call | solution.py:741
  30.6 1.6 %collective-permute-done.3 = bf16[2,832,128]{2,1,0:T(8,128)(2,1)S(1)} collective-permute-done((bf16[2,832,128]{2,1,0:T(8,128)(2,1)S(1)}, bf16[2,832,128]{2,1,0:T(8,128)(2,1)S(1)}, u32[]{:S(2)}, u32[]{:S(2)}) %collective-permute-start.3) | collective-permute-done | bytes 426016 | tf_op jit(solution)/shard_map/ppermute | solution.py:643
  32.4 1.8 %collective-permute-start.4 = (bf16[416,128]{1,0:T(8,128)(2,1)S(1)}, bf16[416,128]{1,0:T(8,128)(2,1)S(1)}, u32[]{:S(2)}, u32[]{:S(2)}) collective-permute-start(bf16[416,128]{1,0:T(8,128)(2,1)S(1)} %get-tuple-element.54), channel_id=1, source_target_pairs={{0,2},{1,3},{2,0},{3,1},{4,6},{5,7},{6,4},{7,5},{8,10},{9,11},{10,... | collective-permute-start | bytes 319496 | tf_op jit(solution)/shard_map/ppermute | solution.py:643
  34.2 1.5 %collective-permute-start.5 = (bf16[416,128]{1,0:T(8,128)(2,1)S(1)}, bf16[416,128]{1,0:T(8,128)(2,1)S(1)}, u32[]{:S(2)}, u32[]{:S(2)}) collective-permute-start(bf16[416,128]{1,0:T(8,128)(2,1)S(1)} %get-tuple-element.56), channel_id=1, source_target_pairs={{0,4},{1,5},{2,6},{3,7},{4,0},{5,1},{6,2},{7,3},{8,12},{9,13},{10,... | collective-permute-start | bytes 319496 | tf_op jit(solution)/shard_map/ppermute | solution.py:643
  36.0 1.5 %collective-permute-done.4 = bf16[416,128]{1,0:T(8,128)(2,1)S(1)} collective-permute-done((bf16[416,128]{1,0:T(8,128)(2,1)S(1)}, bf16[416,128]{1,0:T(8,128)(2,1)S(1)}, u32[]{:S(2)}, u32[]{:S(2)}) %collective-permute-start.4) | collective-permute-done | bytes 106528 | tf_op jit(solution)/shard_map/ppermute | solution.py:643
  37.5 2.6 %collective-permute-done.5 = bf16[416,128]{1,0:T(8,128)(2,1)S(1)} collective-permute-done((bf16[416,128]{1,0:T(8,128)(2,1)S(1)}, bf16[416,128]{1,0:T(8,128)(2,1)S(1)}, u32[]{:S(2)}, u32[]{:S(2)}) %collective-permute-start.5) | collective-permute-done | bytes 106528 | tf_op jit(solution)/shard_map/ppermute | solution.py:643
  40.1 1.2 %collective-permute-done.6 = bf16[416,128]{1,0:T(8,128)(2,1)S(1)} collective-permute-done((bf16[416,128]{1,0:T(8,128)(2,1)S(1)}, bf16[416,128]{1,0:T(8,128)(2,1)S(1)}, u32[]{:S(2)}, u32[]{:S(2)}) %collective-permute-start.6) | collective-permute-done | bytes 106528 | tf_op jit(solution)/shard_map/ppermute | solution.py:643
  41.4 2.7 %collective-permute-start.7 = (bf16[416,128]{1,0:T(8,128)(2,1)S(1)}, bf16[416,128]{1,0:T(8,128)(2,1)S(1)}, u32[]{:S(2)}, u32[]{:S(2)}) collective-permute-start(bf16[416,128]{1,0:T(8,128)(2,1)S(1)} %fusion.1), channel_id=1, source_target_pairs={{0,16},{1,17},{2,18},{3,19},{4,20},{5,21},{6,22},{7,23},{8,24},{9,... | collective-permute-start | bytes 319496 | tf_op jit(solution)/shard_map/ppermute | solution.py:643
  44.1 4.1 %collective-permute-done.7 = bf16[416,128]{1,0:T(8,128)(2,1)S(1)} collective-permute-done((bf16[416,128]{1,0:T(8,128)(2,1)S(1)}, bf16[416,128]{1,0:T(8,128)(2,1)S(1)}, u32[]{:S(2)}, u32[]{:S(2)}) %collective-permute-start.7) | collective-permute-done | bytes 106528 | tf_op jit(solution)/shard_map/ppermute | solution.py:643
  48.2 1.9 %collective-permute-start.10 = (bf16[416,128]{1,0:T(8,128)(2,1)S(1)}, bf16[416,128]{1,0:T(8,128)(2,1)S(1)}, u32[]{:S(2)}, u32[]{:S(2)}) collective-permute-start(bf16[416,128]{1,0:T(8,128)(2,1)S(1)} %add.19.refs_0_), channel_id=1, source_target_pairs={{0,12},{1,13},{2,14},{3,15},{4,8},{5,9},{6,10},{7,11},{8,4},{9,5},... | collective-permute-start | bytes 319496 | tf_op jit(solution)/shard_map/ppermute | solution.py:643
  50.1 1.4 %collective-permute-start.8 = (bf16[416,128]{1,0:T(8,128)(2,1)S(1)}, bf16[416,128]{1,0:T(8,128)(2,1)S(1)}, u32[]{:S(2)}, u32[]{:S(2)}) collective-permute-start(bf16[416,128]{1,0:T(8,128)(2,1)S(1)} %add.19.refs_0_), channel_id=1, source_target_pairs={{0,8},{1,9},{2,10},{3,11},{4,12},{5,13},{6,14},{7,15},{8,0},{9,1},... | collective-permute-start | bytes 319496 | tf_op jit(solution)/shard_map/ppermute | solution.py:643
  51.5 0.3 collective-permute-start.9
  51.8 0.7 %broadcast_multiply_fusion = f32[2,4,256]{2,1,0:T(4,128)} fusion(f32[2,4,256]{2,1,0:T(4,128)S(1)} %get-tuple-element.40, f32[2,4]{1,0:T(2,128)S(1)} %compare_convert_fusion), kind=kLoop, calls=%fused_computation.7 | loop fusion | flops 2048 | bytes 16416 | tf_op jit(solution)/shard_map/mul | solution.py:783
  52.5 1.1 %copy.26 = f32[2,4,2,8,2,8,128]{6,5,4,3,2,1,0:T(8,128)} copy(f32[2,4,2,8,2,8,128]{6,5,3,1,4,2,0:T(8,128)S(1)} %bitcast.21) | data formatting | bytes 2097152 | tf_op jit(solution)/shard_map/transpose | solution.py:743
  53.5 0.4 collective-permute-done.10.refs_3_
  53.9 1.4 %collective-permute-done.8.refs_1_ = bf16[416,128]{1,0:T(8,128)(2,1)S(1)} collective-permute-done((bf16[416,128]{1,0:T(8,128)(2,1)S(1)}, bf16[416,128]{1,0:T(8,128)(2,1)S(1)}, u32[]{:S(2)}, u32[]{:S(2)}) %collective-permute-start.8) | collective-permute-done | bytes 106528 | tf_op jit(solution)/shard_map/ppermute | solution.py:643
  55.3 0.9 %collective-permute-done.9.refs_2_ = bf16[416,128]{1,0:T(8,128)(2,1)S(1)} collective-permute-done((bf16[416,128]{1,0:T(8,128)(2,1)S(1)}, bf16[416,128]{1,0:T(8,128)(2,1)S(1)}, u32[]{:S(2)}, u32[]{:S(2)}) %collective-permute-start.9) | collective-permute-done | bytes 106528 | tf_op jit(solution)/shard_map/ppermute | solution.py:643
  56.2 0.9 %unpack.1 = (f32[1,32]{1,0:T(1,128)}, f32[1,32]{1,0:T(1,128)}, f32[1,32]{1,0:T(1,128)}, f32[32,384]{1,0:T(8,128)}, f32[32,128]{1,0:T(8,128)}, /*index=5*/f32[32,...) custom-call(bf16[416,128]{1,0:T(8,128)(2,1)S(1)} %add.19.refs_0_, ...), custom_call_target="tpu_custom_call" | custom-call | tf_op jit(solution)/shard_map/unpack/pallas_call | solution.py:781
  (37 shorter events, 0.8 us)
Async XLA Ops:
  0.6 11.9 %copy-start.1 = (bf16[32,1152]{1,0:T(8,128)(2,1)S(1)}, bf16[32,1152]{1,0:T(8,128)(2,1)}, u32[]{:S(2)}) copy-start(bf16[32,1152]{1,0:T(8,128)(2,1)} %refs_9_.3) | copy-start | bytes 221188
  0.7 11.9 %copy-start.2 = (bf16[32,512]{1,0:T(8,128)(2,1)S(1)}, bf16[32,512]{1,0:T(8,128)(2,1)}, u32[]{:S(2)}) copy-start(bf16[32,512]{1,0:T(8,128)(2,1)} %refs_7_.3) | copy-start | bytes 98308
  0.7 11.9 %copy-start.3 = (bf16[128,128]{1,0:T(8,128)(2,1)S(1)}, bf16[128,128]{1,0:T(8,128)(2,1)}, u32[]{:S(2)}) copy-start(bf16[128,128]{1,0:T(8,128)(2,1)} %refs_8_.3) | copy-start | bytes 98308
  0.7 11.9 %copy-start.4 = (bf16[32,384]{1,0:T(8,128)(2,1)S(1)}, bf16[32,384]{1,0:T(8,128)(2,1)}, u32[]{:S(2)}) copy-start(bf16[32,384]{1,0:T(8,128)(2,1)} %refs_3_.3) | copy-start | bytes 73732
  0.7 11.9 %copy-start.5 = (bf16[32,384]{1,0:T(8,128)(2,1)S(1)}, bf16[32,384]{1,0:T(8,128)(2,1)}, u32[]{:S(2)}) copy-start(bf16[32,384]{1,0:T(8,128)(2,1)} %refs_5_.3) | copy-start | bytes 73732
  2.6 8.5 %collective-permute-start = (bf16[832,128]{1,0:T(8,128)(2,1)}, bf16[832,128]{1,0:T(8,128)(2,1)S(1)}, u32[]{:S(2)}, u32[]{:S(2)}) collective-permute-start(bf16[832,128]{1,0:T(8,128)(2,1)} %pack.1), channel_id=1, source_target_pairs={{0,2},{1,3},{2,0},{3,1},{4,6},{5,7},{6,4},{7,5},{8,10},{9,11},{10,... | collective-permute-start | bytes 638984 | tf_op jit(solution)/shard_map/ppermute | solution.py:643
  5.6 5.5 %collective-permute-start.1 = (bf16[832,128]{1,0:T(8,128)(2,1)}, bf16[832,128]{1,0:T(8,128)(2,1)S(1)}, u32[]{:S(2)}, u32[]{:S(2)}) collective-permute-start(bf16[832,128]{1,0:T(8,128)(2,1)} %pack.1), channel_id=1, source_target_pairs={{0,1},{1,0},{2,3},{3,2},{4,5},{5,4},{6,7},{7,6},{8,9},{9,8},{10,11... | collective-permute-start | bytes 638984 | tf_op jit(solution)/shard_map/ppermute | solution.py:643
  6.7 5.9 %copy-start.6 = (bf16[32,128]{1,0:T(8,128)(2,1)S(1)}, bf16[32,128]{1,0:T(8,128)(2,1)}, u32[]{:S(2)}) copy-start(bf16[32,128]{1,0:T(8,128)(2,1)} %refs_4_.3) | copy-start | bytes 24580
  6.7 5.9 %copy-start.7 = (bf16[32,128]{1,0:T(8,128)(2,1)S(1)}, bf16[32,128]{1,0:T(8,128)(2,1)}, u32[]{:S(2)}) copy-start(bf16[32,128]{1,0:T(8,128)(2,1)} %refs_6_.3) | copy-start | bytes 24580
  6.7 5.9 %copy-start.8 = (f32[2,4,256]{2,1,0:T(4,128)S(1)}, f32[2,4,256]{2,1,0:T(4,128)}, u32[]{:S(2)}) copy-start(f32[2,4,256]{2,1,0:T(4,128)} %depth_grad.1) | copy-start | bytes 24580
  6.7 5.9 %copy-start.13 = (s32[2]{0:T(128)S(1)}, s32[2]{0:T(128)}, u32[]{:S(2)}) copy-start(s32[2]{0:T(128)} %count_ref.1) | copy-start | bytes 28
  7.6 5.0 %copy-start.9 = (s32[2,4,128]{2,1,0:T(4,128)S(1)}, s32[2,4,128]{2,1,0:T(4,128)}, u32[]{:S(2)}) copy-start(s32[2,4,128]{2,1,0:T(4,128)} %offsets.1) | copy-start | bytes 12292
  11.1 1.6 %copy-start.10 = (bf16[32]{0:T(256)(128)(2,1)S(1)}, bf16[32]{0:T(256)(128)(2,1)}, u32[]{:S(2)}) copy-start(bf16[32]{0:T(256)(128)(2,1)} %param.18) | copy-start | bytes 196
  11.1 1.6 %copy-start.11 = (bf16[32]{0:T(256)(128)(2,1)S(1)}, bf16[32]{0:T(256)(128)(2,1)}, u32[]{:S(2)}) copy-start(bf16[32]{0:T(256)(128)(2,1)} %param.21) | copy-start | bytes 196
  11.1 1.6 %copy-start.12 = (bf16[32]{0:T(256)(128)(2,1)S(1)}, bf16[32]{0:T(256)(128)(2,1)}, u32[]{:S(2)}) copy-start(bf16[32]{0:T(256)(128)(2,1)} %param.24) | copy-start | bytes 196
  11.1 1.5 %collective-permute-start.2 = (bf16[832,128]{1,0:T(8,128)(2,1)S(1)}, bf16[832,128]{1,0:T(8,128)(2,1)S(1)}, u32[]{:S(2)}, u32[]{:S(2)}) collective-permute-start(bf16[832,128]{1,0:T(8,128)(2,1)S(1)} %collective-permute-done.refs_11_), channel_id=1, source_target_pairs={{0,1},{1,0},{2,3},{3,2},{4,5},{5,4},{6,7},{7,6},{8,9},{9,8},{10,11... | collective-permute-start | bytes 638984 | tf_op jit(solution)/shard_map/ppermute | solution.py:643
  30.4 1.8 %collective-permute-start.3 = (bf16[2,832,128]{2,1,0:T(8,128)(2,1)S(1)}, bf16[2,832,128]{2,1,0:T(8,128)(2,1)S(1)}, u32[]{:S(2)}, u32[]{:S(2)}) collective-permute-start(bf16[2,832,128]{2,1,0:T(8,128)(2,1)S(1)} %get-tuple-element.43), channel_id=1, source_target_pairs={{0,1},{1,0},{2,3},{3,2},{4,5},{5,4},{6,7},{7,6},{8,9},{9,8},{10,11... | collective-permute-start | bytes 1277960 | tf_op jit(solution)/shard_map/ppermute | solution.py:643
  32.4 5.1 %collective-permute-start.4 = (bf16[416,128]{1,0:T(8,128)(2,1)S(1)}, bf16[416,128]{1,0:T(8,128)(2,1)S(1)}, u32[]{:S(2)}, u32[]{:S(2)}) collective-permute-start(bf16[416,128]{1,0:T(8,128)(2,1)S(1)} %get-tuple-element.54), channel_id=1, source_target_pairs={{0,2},{1,3},{2,0},{3,1},{4,6},{5,7},{6,4},{7,5},{8,10},{9,11},{10,... | collective-permute-start | bytes 319496 | tf_op jit(solution)/shard_map/ppermute | solution.py:643
  34.2 5.9 %collective-permute-start.5 = (bf16[416,128]{1,0:T(8,128)(2,1)S(1)}, bf16[416,128]{1,0:T(8,128)(2,1)S(1)}, u32[]{:S(2)}, u32[]{:S(2)}) collective-permute-start(bf16[416,128]{1,0:T(8,128)(2,1)S(1)} %get-tuple-element.56), channel_id=1, source_target_pairs={{0,4},{1,5},{2,6},{3,7},{4,0},{5,1},{6,2},{7,3},{8,12},{9,13},{10,... | collective-permute-start | bytes 319496 | tf_op jit(solution)/shard_map/ppermute | solution.py:643
  35.7 5.6 %collective-permute-start.6 = (bf16[416,128]{1,0:T(8,128)(2,1)S(1)}, bf16[416,128]{1,0:T(8,128)(2,1)S(1)}, u32[]{:S(2)}, u32[]{:S(2)}) collective-permute-start(bf16[416,128]{1,0:T(8,128)(2,1)S(1)} %get-tuple-element.55), channel_id=1, source_target_pairs={{0,6},{1,7},{2,4},{3,5},{4,2},{5,3},{6,0},{7,1},{8,14},{9,15},{10,... | collective-permute-start | bytes 319496 | tf_op jit(solution)/shard_map/ppermute | solution.py:643
  41.4 6.8 %collective-permute-start.7 = (bf16[416,128]{1,0:T(8,128)(2,1)S(1)}, bf16[416,128]{1,0:T(8,128)(2,1)S(1)}, u32[]{:S(2)}, u32[]{:S(2)}) collective-permute-start(bf16[416,128]{1,0:T(8,128)(2,1)S(1)} %fusion.1), channel_id=1, source_target_pairs={{0,16},{1,17},{2,18},{3,19},{4,20},{5,21},{6,22},{7,23},{8,24},{9,... | collective-permute-start | bytes 319496 | tf_op jit(solution)/shard_map/ppermute | solution.py:643
  48.2 5.7 %collective-permute-start.10 = (bf16[416,128]{1,0:T(8,128)(2,1)S(1)}, bf16[416,128]{1,0:T(8,128)(2,1)S(1)}, u32[]{:S(2)}, u32[]{:S(2)}) collective-permute-start(bf16[416,128]{1,0:T(8,128)(2,1)S(1)} %add.19.refs_0_), channel_id=1, source_target_pairs={{0,12},{1,13},{2,14},{3,15},{4,8},{5,9},{6,10},{7,11},{8,4},{9,5},... | collective-permute-start | bytes 319496 | tf_op jit(solution)/shard_map/ppermute | solution.py:643
  50.1 5.2 %collective-permute-start.8 = (bf16[416,128]{1,0:T(8,128)(2,1)S(1)}, bf16[416,128]{1,0:T(8,128)(2,1)S(1)}, u32[]{:S(2)}, u32[]{:S(2)}) collective-permute-start(bf16[416,128]{1,0:T(8,128)(2,1)S(1)} %add.19.refs_0_), channel_id=1, source_target_pairs={{0,8},{1,9},{2,10},{3,11},{4,12},{5,13},{6,14},{7,15},{8,0},{9,1},... | collective-permute-start | bytes 319496 | tf_op jit(solution)/shard_map/ppermute | solution.py:643
  51.5 4.7 %collective-permute-start.9 = (bf16[416,128]{1,0:T(8,128)(2,1)S(1)}, bf16[416,128]{1,0:T(8,128)(2,1)S(1)}, u32[]{:S(2)}, u32[]{:S(2)}) collective-permute-start(bf16[416,128]{1,0:T(8,128)(2,1)S(1)} %add.19.refs_0_), channel_id=1, source_target_pairs={{0,4},{1,5},{2,6},{3,7},{4,0},{5,1},{6,2},{7,3},{8,12},{9,13},{10,... | collective-permute-start | bytes 319496 | tf_op jit(solution)/shard_map/ppermute | solution.py:643
  (1 other events, 1.0 us)

commit v5 on v4

--- a/solution.py
+++ b/solution.py
@@ -60,8 +60,7 @@
     d_xhat = d_normed * gain
     mean_d = jnp.mean(d_xhat, -1, keepdims=True)
     mean_dx = jnp.mean(d_xhat * xhat, -1, keepdims=True)
-    d_gain = jnp.sum((d_normed * xhat).reshape(-1, 8, C), 0)
-    return rstd * (d_xhat - mean_d - xhat * mean_dx), d_gain
+    return rstd * (d_xhat - mean_d - xhat * mean_dx)
 
 
 def split_two(value):
@@ -78,7 +77,7 @@
 
 
 def rows_of(parts):
-    return -(-(sum(BLOCKS) * (C // parts) + GAIN_ROWS) // 32) * 32
+    return -(-sum(BLOCKS) * (C // parts) // 32) * 32
 
 
 def place_of(parts):
@@ -119,13 +118,12 @@
         one.wait()
     total = gain_lines(parts, [scratch.at[which] for which in range(3)])
     out[at : at + GAIN_ROWS, :] = total.astype(BF16)
-    if at + GAIN_ROWS < out.shape[0]:
-        out[at + GAIN_ROWS :, :] = jnp.zeros((out.shape[0] - at - GAIN_ROWS, C), BF16)
     for one in copies[3:]:
         one.wait()
 
 
 def unpack_kernel(parts, *refs):
+    gains, weights, refs = refs[0], refs[1], refs[2:]
     terms = (len(refs) - 11) // 2
     own, other, outs = refs[:terms], refs[terms : 2 * terms], refs[2 * terms :]
     rows = C // parts
@@ -133,7 +131,7 @@
     whole = outs[-1]
     half = own[0].shape[0]
     for first, pieces in ((side, own), (1 - side, other)):
-        whole[pl.ds(pl.multiple_of(first * half, 16), half), :] = sum(piece[...].astype(F32) for piece in pieces)
+        whole[pl.ds(pl.multiple_of(first * half, 8), half), :] = sum(piece[...].astype(F32) for piece in pieces)
     at = 0
     for out, blocks in zip(outs[3:10], BLOCKS):
         if out.shape[0] == blocks * rows and out.shape[1] == C:
@@ -142,17 +140,29 @@
             for block in range(blocks):
                 out[:, block * C : (block + 1) * C] = whole[at + block * rows : at + (block + 1) * rows, :]
         at += blocks * rows
-    lane = iota((C, rows), 0)
-    place = (lane == iota((C, rows), 1) + me * rows).astype(F32)
-    picked = lax.dot_general(
-        whole[at : at + GAIN_ROWS, :],
-        place,
-        (((1,), (0,)), ((), ())),
-        precision=lax.Precision.HIGHEST,
-        preferred_element_type=F32,
-    )
+    eye = (iota((rows, rows), 0) == iota((rows, rows), 1)).astype(F32)
+    place = (iota((rows, C), 1) == iota((rows, C), 0) + me * rows).astype(BF16)
+    gain_rows = mm_nt(gains[...].astype(BF16), place)
     for which in range(3):
-        outs[which][...] = picked[which : which + 1]
+        grad = outs[3 + 2 * which]
+        at = sum(BLOCKS[: 2 * which]) * rows
+        column = jnp.zeros((rows, C), F32)
+        for block in range(grad.shape[1] // C):
+            weight = weights[at + block * rows : at + (block + 1) * rows, :].astype(F32)
+            column = column + weight * grad[:, block * C : (block + 1) * C]
+        column = jnp.sum(column, -1, keepdims=True)
+        outs[which][...] = jnp.sum(eye * column, 0, keepdims=True) / gain_rows[which : which + 1]
+
+
+def finish_kernel(scenes, d_packed, d_first, xhats, rstds, turned, gains, out):
+    for scene in range(scenes):
+        for half in range(2):
+            step = 2 * scene + half
+            for side in range(2):
+                spot = slice(side * TOK, (side + 1) * TOK)
+                d_normed = mm(d_packed[step, spot, :], turned[...])
+                d_hidden = norm_backward(d_normed, xhats[step, spot, :], rstds[step, spot, :], gains[0:1, :])
+                out[scene, :, half, :, side] = (d_first[step, spot, :] + d_hidden).reshape(VIEWS, WIN, WIN, C)
 
 
 def merge(*threads, apart=0.0):
@@ -186,7 +196,19 @@
     return jnp.concatenate(pieces, 0)
 
 
-def start_kernel(scenes, features, x0s, xhats, rstds):
+def start_kernel(
+    scenes, count, features, shard, offsets, depth_grad,
+    lives, bias, x0s, xhats, rstds, shard_out, offsets_out, grad_out,
+):
+    of_key = iota((TOK, TOK), 1) // (WIN * WIN)
+    of_query = iota((TOK, TOK), 0) // (WIN * WIN)
+    for scene in range(scenes):
+        live = count[scene]
+        lives[scene] = jnp.broadcast_to(live, (8, C))
+        bias[scene] = jnp.where((of_key < live) & (of_key != of_query), 0.0, MASKED)
+    shard_out[...] = shard[...]
+    offsets_out[...] = offsets[...]
+    grad_out[...] = depth_grad[...]
     for scene in range(scenes):
         for half in range(2):
             step = 2 * scene + half
@@ -206,7 +228,8 @@
 def main_kernel(
     scenes,
     parts,
-    count_ref,
+    lives,
+    bias,
     x0s,
     xh_a,
     rs_a,
@@ -214,16 +237,17 @@
     depth_grad,
     *refs,
 ):
-    own_gains, own, packed, refs = refs[:3], refs[3:10], refs[10 : 9 + parts], refs[9 + parts :]
+    packed, refs = refs[:parts], refs[parts:]
     (
     depth_out,
-    grad_out,
+    d_packs,
+    d_firsts,
+    t_sq,
+    gains,
     keep_out,
     send_out,
     w_sq, w_so, w_cq, w_co, w_fi, w_fo, w_rf,
-    t_sq, t_so, t_cq, t_co, t_fi, t_fo, t_rf, b_rf,
-    gains,
-    bias,
+    t_so, t_cq, t_co, t_fi, t_fo, t_rf, b_rf,
     x2s,
     xh_b, xh_c, rs_b, rs_c,
     no_a, no_b, no_c,
@@ -233,30 +257,25 @@
     low, rev,
     pads, taps, back_taps,
     tables, eye, flip, hots,
-    g_sq, g_so, g_cq, g_co, g_fi, g_fo, g_rf, g_gain,
+    g_sq, g_so, g_cq, g_co, g_fi, g_fo, g_rf,
     ) = refs
     rows = C // parts
     me, side_of_rows = place_of(parts)
 
-    total = gain_lines(parts, own_gains)
-    for apart in range(parts):
+    total = jnp.zeros((GAIN_ROWS, C), F32)
+    for apart, piece in enumerate(packed):
         shard = me ^ apart
         at = 0
-        for which, (ref, blocks) in enumerate(zip((w_sq, w_so, w_cq, w_co, w_fi, w_fo, w_rf), BLOCKS)):
+        for ref, blocks in zip((w_sq, w_so, w_cq, w_co, w_fi, w_fo, w_rf), BLOCKS):
             height = blocks * rows if ref is w_fo else rows
             spot = pl.ds(pl.multiple_of(shard * height, 16), height)
-            if apart == 0:
-                ref[spot, :] = own[which][...]
-            elif ref is w_fo:
-                ref[spot, :] = packed[apart - 1][at : at + height, :]
+            if ref is w_fo:
+                ref[spot, :] = piece[at : at + height, :]
             else:
                 for block in range(blocks):
-                    ref[spot, block * C : (block + 1) * C] = packed[apart - 1][
-                        at + block * rows : at + (block + 1) * rows, :
-                    ]
+                    ref[spot, block * C : (block + 1) * C] = piece[at + block * rows : at + (block + 1) * rows, :]
             at += blocks * rows
-        if apart > 0:
-            total = total + packed[apart - 1][at : at + GAIN_ROWS, :].astype(F32)
+        total = total + piece[at : at + GAIN_ROWS, :].astype(F32)
     gains[...] = total[:8]
     for source, target in ((w_sq, t_sq), (w_so, t_so), (w_cq, t_cq), (w_co, t_co)):
         for block in range(source.shape[1] // C):
@@ -273,8 +292,12 @@
         ref[9 * C :, :C] = jnp.zeros((3 * C, C), BF16)
         ref[: 3 * C, C:] = jnp.zeros((3 * C, C), BF16)
 
-    for ref in (g_sq, g_so, g_cq, g_co, g_fi, g_fo, g_rf, g_gain, pads, hots):
+    for ref in (g_sq, g_so, g_cq, g_co, g_fi, g_fo, g_rf, pads, hots):
         ref[...] = jnp.zeros_like(ref)
+    empty = rows_of(parts) - sum(BLOCKS) * rows
+    if empty:
+        for ref in (keep_out, send_out):
+            ref[...] = jnp.zeros_like(ref)
     for ref in (taps, back_taps):
         for scene in range(scenes):
             ref[scene, :, :HV, :] = jnp.zeros((VIEWS, HV, 3 * C), BF16)
@@ -288,12 +311,6 @@
     tables[3 * HV : 4 * HV, :] = jnp.where(row < HV - 1, 1.0, 0.0)
     eye[...] = jnp.where(iota((HALF, HALF), 0) == iota((HALF, HALF), 1), 1.0, 0.0)
     flip[...] = (iota((HALF, HALF), 0) + iota((HALF, HALF), 1) == HALF - 1).astype(BF16)
-    of_key = iota((TOK, TOK), 1) // (WIN * WIN)
-    of_query = iota((TOK, TOK), 0) // (WIN * WIN)
-    for scene in range(scenes):
-        live = count_ref[scene]
-        bias[scene] = jnp.where((of_key < live) & (of_key != of_query), 0.0, MASKED)
-
     gain_a = gains[0:1, :]
     gain_b = gains[1:2, :]
     gain_c = gains[2:3, :]
@@ -386,12 +403,13 @@
         )
 
     def head(scene):
-        live = count_ref[scene]
+        live = lives[scene, 0:1, :]
         goes_on = {1: live > 2, 2: live > 3}
 
         def partner_of(ref, view, at):
             if view in goes_on:
-                return jnp.where(goes_on[view], ref[scene, view + 1, at, :], ref[scene, 0, at, :])
+                after, first = ref[scene, view + 1, at, :], ref[scene, 0, at, :]
+                return jnp.where(goes_on[view], after.astype(F32), first.astype(F32)).astype(BF16)
             return ref[scene, (view + 1) % VIEWS, at, :]
 
         for view in views:
@@ -495,8 +513,7 @@
         d2 = []
         for side in both:
             spot = places[side]
-            d_hidden, d_gain = norm_backward(d_normed[side], xh_c[step, spot, :], rs_c[step, spot, :], gain_c)
-            g_gain[2] += d_gain
+            d_hidden = norm_backward(d_normed[side], xh_c[step, spot, :], rs_c[step, spot, :], gain_c)
             d2.append(d3[side] + d_hidden)
             yield 150
         d_low = [d2[side].astype(BF16) for side in both]
@@ -531,8 +548,7 @@
         d1 = []
         for side in both:
             spot = places[side]
-            d_hidden, d_gain = norm_backward(d_normed[side], xh_b[step, spot, :], rs_b[step, spot, :], gain_b)
-            g_gain[1] += d_gain
+            d_hidden = norm_backward(d_normed[side], xh_b[step, spot, :], rs_b[step, spot, :], gain_b)
             d1.append(d2[side] + d_hidden)
             yield 150
         d_low = [d1[side].astype(BF16) for side in both]
@@ -558,25 +574,46 @@
             d_keys = joined([mm_tn(d_raw[side][at], qkv[side][at, :C]) for at in windows[:VIEWS]])
             d_packed[side] = jnp.concatenate([d_query, d_keys] + d_packed[side], -1).astype(BF16)
             yield 150
-        d_normed = []
-        for side in both:
-            d_normed.append(mm(d_packed[side], t_sq[...]))
-            yield 100
+        for side in both:
+            d_packs[step, places[side], :] = d_packed[side]
+            d_firsts[step, places[side], :] = d1[side]
+            yield 50
         g_sq[...] += mm_tn(no_a[step], joined(d_packed))
         yield 200
-        for side in both:
-            spot = places[side]
-            d_hidden, d_gain = norm_backward(d_normed[side], xh_a[step, spot, :], rs_a[step, spot, :], gain_a)
-            g_gain[0] += d_gain
-            grad_out[step, spot, :] = d1[side] + d_hidden
-            yield 150
 
     def chain(*threads):
         for thread in threads:
             yield from thread
 
-    def feeds(scene):
-        return chain(feed(scene, 0), feed(scene, 1))
+    grads = (g_sq, g_so, g_cq, g_co, g_fi, w_fo, g_rf)
+
+    def ship(*chosen):
+        bits = bits_of(parts)
+        half_rows = rows_of(parts) // 2
+        for ref, blocks, before in zip(grads, BLOCKS, (sum(BLOCKS[:i]) for i in range(len(BLOCKS)))):
+            if not any(ref is one for one in chosen):
+                continue
+            for apart in range(parts):
+                shard = me ^ apart
+                slot = sum(((apart >> bit) & 1) << (bits - 1 - bit) for bit in range(bits))
+                dest = (keep_out, send_out)[slot // (parts // 2)].at[slot % (parts // 2)]
+                for block in range(blocks):
+                    if ref is w_fo:
+                        spot = pl.ds(pl.multiple_of(shard * (blocks * rows) + block * rows, 16), rows)
+                        value = ref[spot, :]
+                    else:
+                        spot = pl.ds(pl.multiple_of(shard * rows, 16), rows)
+                        value = ref[spot, block * C : (block + 1) * C].astype(BF16)
+                    for start in range(0, rows, 16):
+                        which, offset = divmod((before + block) * rows + start, half_rows)
+                        spot = pl.ds(pl.multiple_of((side_of_rows ^ which) * half_rows + offset, 16), 16)
+                        dest[spot, :] = value[start : start + 16]
+                yield 40
+
+    def turn_back():
+        for block in range(FFH // C):
+            w_fo[block * C : (block + 1) * C, :] = g_fo[:, block * C : (block + 1) * C].T.astype(BF16)
+            yield 30
 
     def whole_of(thread, total):
         return paced(thread, 1.0 / total)
@@ -593,42 +630,8 @@
     merge(*attends(0), *attends(1), apart=0.02)
     merge(feeds(0), feeds(1))
     merge(whole_of(head(0), 7600), whole_of(head(1), 7600), apart=0.05)
-    merge(*backs((0, 0), (0, 1), (1, 0), (1, 1)), apart=0.04)
-
-    bits = bits_of(parts)
-    line = iota((GAIN_ROWS, C), 0)
-    gain_rows = jnp.zeros((GAIN_ROWS, C), F32)
-    for which in range(3):
-        gain_rows = jnp.where(line == which, jnp.sum(g_gain[which], 0, keepdims=True), gain_rows)
-    gain_rows = gain_rows.astype(BF16)
-    for block in range(FFH // C):
-        w_fo[block * C : (block + 1) * C, :] = g_fo[:, block * C : (block + 1) * C].T.astype(BF16)
-    half_rows = rows_of(parts) // 2
-    first = side_of_rows
-    for apart in range(parts):
-        shard = me ^ apart
-        slot = sum(((apart >> bit) & 1) << (bits - 1 - bit) for bit in range(bits))
-        dest = (keep_out, send_out)[slot // (parts // 2)].at[slot % (parts // 2)]
-
-        def put(at, value):
-            height = value.shape[0]
-            which, offset = divmod(at, half_rows)
-            assert offset + height <= half_rows
-            dest[pl.ds(pl.multiple_of((first ^ which) * half_rows + offset, 16), height), :] = value
-
-        at = 0
-        for ref, blocks in zip((g_sq, g_so, g_cq, g_co, g_fi, w_fo, g_rf), BLOCKS):
-            for block in range(blocks):
-                if ref is w_fo:
-                    spot = pl.ds(pl.multiple_of(shard * (blocks * rows) + block * rows, 16), rows)
-                    put(at, ref[spot, :])
-                else:
-                    spot = pl.ds(pl.multiple_of(shard * rows, 16), rows)
-                    put(at, ref[spot, block * C : (block + 1) * C].astype(BF16))
-                at += rows
-        put(at, gain_rows)
-        if at + GAIN_ROWS < rows_of(parts):
-            put(at + GAIN_ROWS, jnp.zeros((rows_of(parts) - at - GAIN_ROWS, C), BF16))
+    merge(*backs((0, 0), (0, 1), (1, 0), (1, 1)), whole_of(ship(g_rf), 160), apart=0.02)
+    merge(chain(turn_back(), ship(w_fo)), ship(g_sq, g_so, g_cq, g_co, g_fi))
 
 
 VMEM = pl.BlockSpec(memory_space=pltpu.VMEM)
@@ -668,7 +671,7 @@
 
     pack = pl.pallas_call(
         functools.partial(pack_kernel, parts),
-        out_shape=jax.ShapeDtypeStruct((shard_rows, C), BF16),
+        out_shape=jax.ShapeDtypeStruct((sum(BLOCKS) * rows + GAIN_ROWS, C), BF16),
         in_specs=[HBM] * 10,
         out_specs=VMEM,
         scratch_shapes=[pltpu.VMEM((3, 1, rows), BF16), pltpu.SemaphoreType.DMA((3 + sum(BLOCKS),))],
@@ -682,14 +685,19 @@
     span = 2 * TOK
     start = pl.pallas_call(
         functools.partial(start_kernel, scenes),
-        out_shape=(jax.ShapeDtypeStruct((steps, span, C), F32),) * 3,
-        in_specs=[VMEM],
-        out_specs=(VMEM,) * 3,
+        out_shape=(
+            jax.ShapeDtypeStruct((scenes, 8, C), jnp.int32),
+            jax.ShapeDtypeStruct((scenes, TOK, TOK), F32),
+        )
+        + (jax.ShapeDtypeStruct((steps, span, C), F32),) * 3
+        + tuple(jax.ShapeDtypeStruct(piece.shape, piece.dtype) for piece in (shard, plane_offsets, depth_grad)),
+        in_specs=[SMEM] + [VMEM] * 4,
+        out_specs=(VMEM,) * 8,
         compiler_params=small,
         cost_estimate=pl.CostEstimate(flops=10 * features.size, bytes_accessed=14 * features.size, transcendentals=0),
         name="start",
     )
-    began = start(features)
+    began = start(view_count, features, shard, plane_offsets, depth_grad)
 
     packed = {0: shard}
     for bit in reversed(range(bits_of(parts))):
@@ -697,15 +705,13 @@
         if len(packed) == 1:
             came, began = lax.optimization_barrier((came, began))
         packed |= came
-    packed = [packed[apart] for apart in range(1, parts)]
+    packed = [packed[apart] for apart in range(parts)]
 
     scratch = [
         ((C, 3 * C), BF16), ((C, C), BF16), ((C, 3 * C), BF16), ((C, C), BF16),
         ((C, FFH), BF16), ((FFH, C), BF16), ((C, 9 * PLANES), BF16),
-        ((3 * C, C), BF16), ((C, C), BF16), ((3 * C, C), BF16), ((C, C), BF16),
+        ((C, C), BF16), ((3 * C, C), BF16), ((C, C), BF16),
         ((FFH, C), BF16), ((C, FFH), BF16), ((12 * PLANES, 2 * C), BF16), ((12 * PLANES, 2 * C), BF16),
-        ((8, C), F32),
-        ((scenes, TOK, TOK), F32),
         ((steps, span, C), F32),
     ]
     scratch += [((steps, span, C), F32)] * 4
@@ -721,27 +727,40 @@
         ((scenes, VIEWS, PIX + 2 * HV, 3 * C), BF16), ((scenes, VIEWS, PIX + 2 * HV, 3 * C), BF16),
         ((4 * HV, C), F32), ((HALF, HALF), F32), ((HALF, HALF), BF16), ((scenes, 2, VIEWS, 2 * C, C), BF16),
         ((C, 3 * C), F32), ((C, C), F32), ((C, 3 * C), F32), ((C, C), F32),
-        ((C, FFH), F32), ((C, FFH), F32), ((C, 9 * PLANES), F32), ((3, 8, C), F32),
+        ((C, FFH), F32), ((C, FFH), F32), ((C, 9 * PLANES), F32),
     ]
     main = pl.pallas_call(
         functools.partial(main_kernel, scenes, parts),
         out_shape=(
             jax.ShapeDtypeStruct((scenes, VIEWS, PIX), F32),
+            jax.ShapeDtypeStruct((steps, span, 3 * C), BF16),
             jax.ShapeDtypeStruct((steps, span, C), F32),
+            jax.ShapeDtypeStruct((3 * C, C), BF16),
+            jax.ShapeDtypeStruct((8, C), F32),
             jax.ShapeDtypeStruct((parts // 2, shard_rows, C), BF16),
             jax.ShapeDtypeStruct((parts // 2, shard_rows, C), BF16),
         ),
-        in_specs=[SMEM] + [VMEM] * (14 + parts),
-        out_specs=(VMEM,) * 4,
-        scratch_shapes=[pltpu.VMEM(shape, kind) for shape, kind in scratch]
-,
+        in_specs=[VMEM] * (7 + parts),
+        out_specs=(VMEM,) * 7,
+        scratch_shapes=[pltpu.VMEM(shape, kind) for shape, kind in scratch],
         compiler_params=pltpu.CompilerParams(vmem_limit_bytes=46 * MIB),
         name="layer",
     )
-    depth, grad_features, keep, send = main(view_count, *began, plane_offsets, depth_grad, *own, *packed)
-
-    grad_features = grad_features.reshape(scenes, 2, 2, VIEWS, WIN, WIN, C).transpose(0, 3, 1, 4, 2, 5, 6)
-    grad_features = grad_features.reshape(features.shape)
+    lives, bias, x0s, xhats, rstds, packed[0], plane_offsets, depth_grad = began
+    depth, d_packs, d_firsts, turned, gains, keep, send = main(
+        lives, bias, x0s, xhats, rstds, plane_offsets, depth_grad, *packed
+    )
+
+    finish = pl.pallas_call(
+        functools.partial(finish_kernel, scenes),
+        out_shape=jax.ShapeDtypeStruct((scenes, VIEWS, 2, WIN, 2, WIN, C), F32),
+        in_specs=[VMEM] * 6,
+        out_specs=VMEM,
+        compiler_params=small,
+        cost_estimate=pl.CostEstimate(flops=6 * C * features.size, bytes_accessed=16 * features.size, transcendentals=0),
+        name="finish",
+    )
+    grad_features = finish(d_packs, d_firsts, xhats, rstds, turned, gains).reshape(features.shape)
 
     for bit in range(bits_of(parts)):
         if bit > 0:
@@ -761,9 +780,9 @@
         along = exchange(grads, 0, 2)
         swapped = exchange(grads, 0, 1)
         corner = exchange(grads, 0, 3)
-        own, other = (grads, along), (swapped, corner)
+        mine, other = (grads, along), (swapped, corner)
     else:
-        own, other = (grads,), (exchange(grads, 0, 1),)
+        mine, other = (grads,), (exchange(grads, 0, 1),)
 
     unpack = pl.pallas_call(
         functools.partial(unpack_kernel, parts),
@@ -772,13 +791,15 @@
             jax.ShapeDtypeStruct(piece.shape, F32)
             for piece in (self_qkv, self_out, cross_qkv, cross_out, ff_in, ff_out, refine)
         ),
-        in_specs=[VMEM] * (2 * len(own)),
+        in_specs=[VMEM] * (2 + 2 * len(mine)),
         out_specs=(VMEM,) * 10,
         scratch_shapes=[pltpu.VMEM((shard_rows, C), F32)],
         compiler_params=small,
         name="unpack",
     )
-    ga, gb, gc, d_sq, d_so, d_cq, d_co, d_fi, d_fo, d_rf = unpack(*own, *other)
+    ga, gb, gc, d_sq, d_so, d_cq, d_co, d_fi, d_fo, d_rf = unpack(
+        gains, packed[0], *mine, *other
+    )
     return (
         depth * (jnp.arange(VIEWS) < view_count[:, None])[:, :, None],
         grad_features,

time: 57.3 us -> 55.5 us (0.969)
  waiting for transfers between devices: 18.6 us -> 13.6 us
  local copies, waits for them, and re-layouts: 2.18 us -> 4.07 us
  starting transfers between devices: 13 us -> 13.8 us
    ppermute x11, waiting for transfers between devices: 18.6 us -> 13.6 us  [exchange(): lax.ppermute(value, ('dp', 'fsdp'), [(i, i ^ mask) for i in range(count)])]
    unnamed x28 -> x12, local copies, waits for them, and re-layouts: 1.09 us -> 4.05 us
    transpose x1 -> x0, local copies, waits for them, and re-layouts: 1.06 us -> none  [local(): grad_features.reshape(scenes, 2, 2, VIEWS, WIN, WIN, C)]
    ppermute x11, starting transfers between devices: 13 us -> 13.8 us  [exchange(): lax.ppermute(value, ('dp', 'fsdp'), [(i, i ^ mask) for i in range(count)])]
    pallas_call x3 -> x4, Pallas kernels: 19.6 us -> 20.2 us  [the longest x1 16 us: local(): main(lives, bias, x0s, xhats, rstds, plane_offsets, depth_grad, *packed)]
  transfers between devices with their start and end apart: 11 -> 11, of which waited for: 10 -> 8; matrix products, arithmetic and copies ran while one was open for 3% -> 1% of each run, Pallas kernels for 2% -> 6%
where the time goes in v5:
time: 55.5 us; the launch traced here: 55.1 us
  Pallas kernels  22 us (40%)
  starting transfers between devices  13.8 us (25%)
  waiting for transfers between devices  13.6 us (25%)
  local copies, waits for them, and re-layouts  4.07 us (7%)
  other arithmetic  0.94 us (2%)
  between operations  0.72 us (1%)
    pallas_call x1, Pallas kernels, local(): main(lives, bias, x0s, xhats, rstds, plane_offsets, depth_grad, *packed)  16 us
    ppermute x11, starting transfers between devices, exchange(): lax.ppermute(value, ('dp', 'fsdp'), [(i, i ^ mask) for i in range(count)])  13.8 us
    ppermute x11, waiting for transfers between devices, exchange(): lax.ppermute(value, ('dp', 'fsdp'), [(i, i ^ mask) for i in range(count)])  13.6 us
    unnamed x12, local copies, waits for them, and re-layouts  4.05 us
    pallas_call x1, Pallas kernels, local(): shard = pack(*own)  1.86 us
    pallas_call x1, Pallas kernels, local(): finish(d_packs, d_firsts, xhats, rstds, turned, gains)  1.86 us
    pallas_call x1, Pallas kernels, local(): began = start(view_count, features, shard, plane_offsets, depth_grad)  1.5 us
  transfers between devices with their start and end apart: 11, of which 8 were waited for; matrix products, arithmetic and copies ran while one was open for 1% of the time, Pallas kernels for 6%

profile of v5, /device:TPU:0, one launch (start us, length us, event | category | flops | bytes accessed | tf_op | source)
XLA Modules:
  0.0 55.1 jit_solution(16392355503768373053)
XLA Ops:
  0.6 1.9 %pack.1.shard = bf16[816,128]{1,0:T(8,128)(2,1)} custom-call(bf16[1,32]{1,0:T(2,128)(2,1)} %bitcast.19, bf16[1,32]{1,0:T(2,128)(2,1)} %bitcast.20, bf16[1,32]{1,0:T(2,128)(2,1)} %bitcast.21, bf16[32,384]{1,0:T(8,128)(2,1)} %refs_3_.1, bf16[32,128]{1,0:T(8,128)(2,1)} %refs_4_.1, bf16[32,384]{1,0:T(8,128)(2,1)} %refs_5_.1, bf16[32,128]{1,0:T(8,128)(2,1)} %refs_6_.1, ...), custom_call_target="tpu_custom_call" | custom-call | tf_op jit(solution)/shard_map/pack/pallas_call | solution.py:683
  2.5 3.0 %collective-permute-start = (bf16[816,128]{1,0:T(8,128)(2,1)}, bf16[816,128]{1,0:T(8,128)(2,1)S(1)}, u32[]{:S(2)}, u32[]{:S(2)}) collective-permute-start(bf16[816,128]{1,0:T(8,128)(2,1)} %pack.1.shard), channel_id=1, source_target_pairs={{0,2},{1,3},{2,0},{3,1},{4,6},{5,7},{6,4},{7,5},{8,10},{9,11},{10,... | collective-permute-start | bytes 626696 | tf_op jit(solution)/shard_map/ppermute | solution.py:646
  5.5 1.0 %copy-done = bf16[816,128]{1,0:T(8,128)(2,1)S(1)} copy-done((bf16[816,128]{1,0:T(8,128)(2,1)S(1)}, bf16[816,128]{1,0:T(8,128)(2,1)}, u32[]{:S(2)}) %copy-start) | copy-done | bytes 208920
  6.5 1.0 %copy-done.1 = bf16[2,4,256,128]{3,2,1,0:T(8,128)(2,1)S(1)} copy-done((bf16[2,4,256,128]{3,2,1,0:T(8,128)(2,1)S(1)}, bf16[2,4,256,128]{3,2,1,0:T(8,128)(2,1)}, u32[]{:S(2)}) %copy-start.1) | copy-done | bytes 524312
  7.6 0.7 %copy-done.2 = f32[2,4,256]{2,1,0:T(4,128)S(1)} copy-done((f32[2,4,256]{2,1,0:T(4,128)S(1)}, f32[2,4,256]{2,1,0:T(4,128)}, u32[]{:S(2)}) %copy-start.2) | copy-done | bytes 8216
  8.3 0.7 %copy-done.3 = s32[2,4,128]{2,1,0:T(4,128)S(1)} copy-done((s32[2,4,128]{2,1,0:T(4,128)S(1)}, s32[2,4,128]{2,1,0:T(4,128)}, u32[]{:S(2)}) %copy-start.3) | copy-done | bytes 4120
  9.6 1.5 %start.1 = (s32[2,8,128]{2,1,0:T(8,128)S(1)}, f32[2,256,256]{2,1,0:T(8,128)S(1)}, f32[4,512,128]{2,1,0:T(8,128)S(1)}, f32[4,512,128]{2,1,0:T(8,128)S(1)}, f32[4,...) custom-call(s32[2]{0:T(128)S(1)} %copy-done.4, ...), custom_call_target="tpu_custom_call" | custom-call | flops 2621440 | bytes 3670016 | tf_op jit(solution)/shard_map/start/pallas_call | solution.py:700
  11.7 1.1 %collective-permute-done.2.refs_3_ = bf16[816,128]{1,0:T(8,128)(2,1)S(1)} collective-permute-done((bf16[816,128]{1,0:T(8,128)(2,1)S(1)}, bf16[816,128]{1,0:T(8,128)(2,1)S(1)}, u32[]{:S(2)}, u32[]{:S(2)}) %collective-permute-start.2) | collective-permute-done | bytes 208928 | tf_op jit(solution)/shard_map/ppermute | solution.py:646
  12.7 16.0 %layer.1 = (f32[2,4,256]{2,1,0:T(4,128)S(1)}, bf16[4,512,384]{2,1,0:T(8,128)(2,1)S(1)}, f32[4,512,128]{2,1,0:T(8,128)S(1)}, bf16[384,128]{1,0:T(8,128)(2,1)S(1)}...) custom-call(s32[2,8,128]{2,1,0:T(8,128)S(1)} %get-tuple-element.54.lives, ...), custom_call_target="tpu_custom_call" | custom-call | tf_op jit(solution)/shard_map/layer/pallas_call | solution.py:750
  29.2 1.4 %collective-permute-done.3 = bf16[2,800,128]{2,1,0:T(8,128)(2,1)S(1)} collective-permute-done((bf16[2,800,128]{2,1,0:T(8,128)(2,1)S(1)}, bf16[2,800,128]{2,1,0:T(8,128)(2,1)S(1)}, u32[]{:S(2)}, u32[]{:S(2)}) %collective-permute-start.3) | collective-permute-done | bytes 409632 | tf_op jit(solution)/shard_map/ppermute | solution.py:646
  30.7 1.4 %collective-permute-start.4 = (bf16[400,128]{1,0:T(8,128)(2,1)S(1)}, bf16[400,128]{1,0:T(8,128)(2,1)S(1)}, u32[]{:S(2)}, u32[]{:S(2)}) collective-permute-start(bf16[400,128]{1,0:T(8,128)(2,1)S(1)} %get-tuple-element.80), channel_id=1, source_target_pairs={{0,2},{1,3},{2,0},{3,1},{4,6},{5,7},{6,4},{7,5},{8,10},{9,11},{10,... | collective-permute-start | bytes 307208 | tf_op jit(solution)/shard_map/ppermute | solution.py:646
  32.1 1.5 %collective-permute-start.5 = (bf16[400,128]{1,0:T(8,128)(2,1)S(1)}, bf16[400,128]{1,0:T(8,128)(2,1)S(1)}, u32[]{:S(2)}, u32[]{:S(2)}) collective-permute-start(bf16[400,128]{1,0:T(8,128)(2,1)S(1)} %get-tuple-element.82), channel_id=1, source_target_pairs={{0,4},{1,5},{2,6},{3,7},{4,0},{5,1},{6,2},{7,3},{8,12},{9,13},{10,... | collective-permute-start | bytes 307208 | tf_op jit(solution)/shard_map/ppermute | solution.py:646
  34.3 1.7 %collective-permute-done.4 = bf16[400,128]{1,0:T(8,128)(2,1)S(1)} collective-permute-done((bf16[400,128]{1,0:T(8,128)(2,1)S(1)}, bf16[400,128]{1,0:T(8,128)(2,1)S(1)}, u32[]{:S(2)}, u32[]{:S(2)}) %collective-permute-start.4) | collective-permute-done | bytes 102432 | tf_op jit(solution)/shard_map/ppermute | solution.py:646
  35.9 1.6 %collective-permute-done.5 = bf16[400,128]{1,0:T(8,128)(2,1)S(1)} collective-permute-done((bf16[400,128]{1,0:T(8,128)(2,1)S(1)}, bf16[400,128]{1,0:T(8,128)(2,1)S(1)}, u32[]{:S(2)}, u32[]{:S(2)}) %collective-permute-start.5) | collective-permute-done | bytes 102432 | tf_op jit(solution)/shard_map/ppermute | solution.py:646
  37.6 1.7 %collective-permute-done.6 = bf16[400,128]{1,0:T(8,128)(2,1)S(1)} collective-permute-done((bf16[400,128]{1,0:T(8,128)(2,1)S(1)}, bf16[400,128]{1,0:T(8,128)(2,1)S(1)}, u32[]{:S(2)}, u32[]{:S(2)}) %collective-permute-start.6) | collective-permute-done | bytes 102432 | tf_op jit(solution)/shard_map/ppermute | solution.py:646
  39.4 2.6 %collective-permute-start.7 = (bf16[400,128]{1,0:T(8,128)(2,1)S(1)}, bf16[400,128]{1,0:T(8,128)(2,1)S(1)}, u32[]{:S(2)}, u32[]{:S(2)}) collective-permute-start(bf16[400,128]{1,0:T(8,128)(2,1)S(1)} %fusion.1), channel_id=1, source_target_pairs={{0,16},{1,17},{2,18},{3,19},{4,20},{5,21},{6,22},{7,23},{8,24},{9,... | collective-permute-start | bytes 307208 | tf_op jit(solution)/shard_map/ppermute | solution.py:646
  42.1 4.3 %collective-permute-done.7 = bf16[400,128]{1,0:T(8,128)(2,1)S(1)} collective-permute-done((bf16[400,128]{1,0:T(8,128)(2,1)S(1)}, bf16[400,128]{1,0:T(8,128)(2,1)S(1)}, u32[]{:S(2)}, u32[]{:S(2)}) %collective-permute-start.7) | collective-permute-done | bytes 102432 | tf_op jit(solution)/shard_map/ppermute | solution.py:646
  46.4 1.8 %collective-permute-start.10 = (bf16[400,128]{1,0:T(8,128)(2,1)S(1)}, bf16[400,128]{1,0:T(8,128)(2,1)S(1)}, u32[]{:S(2)}, u32[]{:S(2)}) collective-permute-start(bf16[400,128]{1,0:T(8,128)(2,1)S(1)} %add.19.refs_2_), channel_id=1, source_target_pairs={{0,12},{1,13},{2,14},{3,15},{4,8},{5,9},{6,10},{7,11},{8,4},{9,5},... | collective-permute-start | bytes 307208 | tf_op jit(solution)/shard_map/ppermute | solution.py:646
  48.2 1.4 %collective-permute-start.8 = (bf16[400,128]{1,0:T(8,128)(2,1)S(1)}, bf16[400,128]{1,0:T(8,128)(2,1)S(1)}, u32[]{:S(2)}, u32[]{:S(2)}) collective-permute-start(bf16[400,128]{1,0:T(8,128)(2,1)S(1)} %add.19.refs_2_), channel_id=1, source_target_pairs={{0,8},{1,9},{2,10},{3,11},{4,12},{5,13},{6,14},{7,15},{8,0},{9,1},... | collective-permute-start | bytes 307208 | tf_op jit(solution)/shard_map/ppermute | solution.py:646
  50.0 0.7 %broadcast_multiply_fusion = f32[2,4,256]{2,1,0:T(4,128)} fusion(f32[2,4,256]{2,1,0:T(4,128)S(1)} %get-tuple-element.63, f32[2,4]{1,0:T(2,128)S(1)} %compare_convert_fusion), kind=kLoop, calls=%fused_computation.7 | loop fusion | flops 2048 | bytes 16416 | tf_op jit(solution)/shard_map/mul | solution.py:804
  50.6 1.9 %finish.1 = f32[2,4,2,8,2,8,128]{6,5,4,3,2,1,0:T(8,128)} custom-call(bf16[4,512,384]{2,1,0:T(8,128)(2,1)S(1)} %get-tuple-element.64.d_packed, f32[4,512,128]{2,1,0:T(8,128)S(1)} %get-tuple-element.65.d_first, f32[4,512,128]{2,1,0:T(8,128)S(1)} %get-tuple-element.57.xh_a.xhats, f32[4,512,128]{2,1,0:T(8,128)S(1)} %get-tuple-element.58.rs_a.rstds, ...), custom_call_target="tpu_custom_call" | custom-call | flops 201326592 | bytes 4194304 | tf_op jit(solution)/shard_map/finish/pallas_call | solution.py:763
  52.5 0.8 %collective-permute-done.8.refs_3_ = bf16[400,128]{1,0:T(8,128)(2,1)S(1)} collective-permute-done((bf16[400,128]{1,0:T(8,128)(2,1)S(1)}, bf16[400,128]{1,0:T(8,128)(2,1)S(1)}, u32[]{:S(2)}, u32[]{:S(2)}) %collective-permute-start.8) | collective-permute-done | bytes 102432 | tf_op jit(solution)/shard_map/ppermute | solution.py:646
  53.3 0.9 %collective-permute-done.9.refs_4_ = bf16[400,128]{1,0:T(8,128)(2,1)S(1)} collective-permute-done((bf16[400,128]{1,0:T(8,128)(2,1)S(1)}, bf16[400,128]{1,0:T(8,128)(2,1)S(1)}, u32[]{:S(2)}, u32[]{:S(2)}) %collective-permute-start.9) | collective-permute-done | bytes 102432 | tf_op jit(solution)/shard_map/ppermute | solution.py:646
  54.3 0.8 %unpack.1 = (f32[1,32]{1,0:T(1,128)}, f32[1,32]{1,0:T(1,128)}, f32[1,32]{1,0:T(1,128)}, f32[32,384]{1,0:T(8,128)}, f32[32,128]{1,0:T(8,128)}, /*index=5*/f32[32,...) custom-call(f32[8,128]{1,0:T(8,128)S(1)} %get-tuple-element.67.gains.refs_0_, ...), custom_call_target="tpu_custom_call" | custom-call | tf_op jit(solution)/shard_map/unpack/pallas_call | solution.py:800
  (21 shorter events, 3.0 us)
Async XLA Ops:
  2.5 8.6 %collective-permute-start = (bf16[816,128]{1,0:T(8,128)(2,1)}, bf16[816,128]{1,0:T(8,128)(2,1)S(1)}, u32[]{:S(2)}, u32[]{:S(2)}) collective-permute-start(bf16[816,128]{1,0:T(8,128)(2,1)} %pack.1.shard), channel_id=1, source_target_pairs={{0,2},{1,3},{2,0},{3,1},{4,6},{5,7},{6,4},{7,5},{8,10},{9,11},{10,... | collective-permute-start | bytes 626696 | tf_op jit(solution)/shard_map/ppermute | solution.py:646
  5.5 6.1 %collective-permute-start.1 = (bf16[816,128]{1,0:T(8,128)(2,1)}, bf16[816,128]{1,0:T(8,128)(2,1)S(1)}, u32[]{:S(2)}, u32[]{:S(2)}) collective-permute-start(bf16[816,128]{1,0:T(8,128)(2,1)} %pack.1.shard), channel_id=1, source_target_pairs={{0,1},{1,0},{2,3},{3,2},{4,5},{5,4},{6,7},{7,6},{8,9},{9,8},{10,11... | collective-permute-start | bytes 626696 | tf_op jit(solution)/shard_map/ppermute | solution.py:646
  5.5 1.0 %copy-start = (bf16[816,128]{1,0:T(8,128)(2,1)S(1)}, bf16[816,128]{1,0:T(8,128)(2,1)}, u32[]{:S(2)}) copy-start(bf16[816,128]{1,0:T(8,128)(2,1)} %pack.1.shard) | copy-start | bytes 626692
  6.5 1.0 %copy-start.1 = (bf16[2,4,256,128]{3,2,1,0:T(8,128)(2,1)S(1)}, bf16[2,4,256,128]{3,2,1,0:T(8,128)(2,1)}, u32[]{:S(2)}) copy-start(bf16[2,4,256,128]{3,2,1,0:T(8,128)(2,1)} %features.1) | copy-start | bytes 1572868
  7.6 0.7 %copy-start.2 = (f32[2,4,256]{2,1,0:T(4,128)S(1)}, f32[2,4,256]{2,1,0:T(4,128)}, u32[]{:S(2)}) copy-start(f32[2,4,256]{2,1,0:T(4,128)} %depth_grad.1) | copy-start | bytes 24580
  8.2 0.7 %copy-start.3 = (s32[2,4,128]{2,1,0:T(4,128)S(1)}, s32[2,4,128]{2,1,0:T(4,128)}, u32[]{:S(2)}) copy-start(s32[2,4,128]{2,1,0:T(4,128)} %offsets.1) | copy-start | bytes 12292
  8.9 0.7 %copy-start.4 = (s32[2]{0:T(128)S(1)}, s32[2]{0:T(128)}, u32[]{:S(2)}) copy-start(s32[2]{0:T(128)} %count.1) | copy-start | bytes 28
  11.1 1.6 %collective-permute-start.2 = (bf16[816,128]{1,0:T(8,128)(2,1)S(1)}, bf16[816,128]{1,0:T(8,128)(2,1)S(1)}, u32[]{:S(2)}, u32[]{:S(2)}) collective-permute-start(bf16[816,128]{1,0:T(8,128)(2,1)S(1)} %collective-permute-done.refs_2_), channel_id=1, source_target_pairs={{0,1},{1,0},{2,3},{3,2},{4,5},{5,4},{6,7},{7,6},{8,9},{9,8},{10,11... | collective-permute-start | bytes 626696 | tf_op jit(solution)/shard_map/ppermute | solution.py:646
  28.7 13.3 %copy-start.5 = (s32[2]{0:T(128)S(1)}, s32[2]{0:T(128)}, u32[]{:S(2)}) copy-start(s32[2]{0:T(128)} %count.1) | copy-start | bytes 28
  28.7 1.8 %collective-permute-start.3 = (bf16[2,800,128]{2,1,0:T(8,128)(2,1)S(1)}, bf16[2,800,128]{2,1,0:T(8,128)(2,1)S(1)}, u32[]{:S(2)}, u32[]{:S(2)}) collective-permute-start(bf16[2,800,128]{2,1,0:T(8,128)(2,1)S(1)} %get-tuple-element.69), channel_id=1, source_target_pairs={{0,1},{1,0},{2,3},{3,2},{4,5},{5,4},{6,7},{7,6},{8,9},{9,8},{10,11... | collective-permute-start | bytes 1228808 | tf_op jit(solution)/shard_map/ppermute | solution.py:646
  30.7 5.2 %collective-permute-start.4 = (bf16[400,128]{1,0:T(8,128)(2,1)S(1)}, bf16[400,128]{1,0:T(8,128)(2,1)S(1)}, u32[]{:S(2)}, u32[]{:S(2)}) collective-permute-start(bf16[400,128]{1,0:T(8,128)(2,1)S(1)} %get-tuple-element.80), channel_id=1, source_target_pairs={{0,2},{1,3},{2,0},{3,1},{4,6},{5,7},{6,4},{7,5},{8,10},{9,11},{10,... | collective-permute-start | bytes 307208 | tf_op jit(solution)/shard_map/ppermute | solution.py:646
  32.1 5.4 %collective-permute-start.5 = (bf16[400,128]{1,0:T(8,128)(2,1)S(1)}, bf16[400,128]{1,0:T(8,128)(2,1)S(1)}, u32[]{:S(2)}, u32[]{:S(2)}) collective-permute-start(bf16[400,128]{1,0:T(8,128)(2,1)S(1)} %get-tuple-element.82), channel_id=1, source_target_pairs={{0,4},{1,5},{2,6},{3,7},{4,0},{5,1},{6,2},{7,3},{8,12},{9,13},{10,... | collective-permute-start | bytes 307208 | tf_op jit(solution)/shard_map/ppermute | solution.py:646
  33.6 5.7 %collective-permute-start.6 = (bf16[400,128]{1,0:T(8,128)(2,1)S(1)}, bf16[400,128]{1,0:T(8,128)(2,1)S(1)}, u32[]{:S(2)}, u32[]{:S(2)}) collective-permute-start(bf16[400,128]{1,0:T(8,128)(2,1)S(1)} %get-tuple-element.81), channel_id=1, source_target_pairs={{0,6},{1,7},{2,4},{3,5},{4,2},{5,3},{6,0},{7,1},{8,14},{9,15},{10,... | collective-permute-start | bytes 307208 | tf_op jit(solution)/shard_map/ppermute | solution.py:646
  39.4 7.0 %collective-permute-start.7 = (bf16[400,128]{1,0:T(8,128)(2,1)S(1)}, bf16[400,128]{1,0:T(8,128)(2,1)S(1)}, u32[]{:S(2)}, u32[]{:S(2)}) collective-permute-start(bf16[400,128]{1,0:T(8,128)(2,1)S(1)} %fusion.1), channel_id=1, source_target_pairs={{0,16},{1,17},{2,18},{3,19},{4,20},{5,21},{6,22},{7,23},{8,24},{9,... | collective-permute-start | bytes 307208 | tf_op jit(solution)/shard_map/ppermute | solution.py:646
  46.4 6.1 %collective-permute-start.10 = (bf16[400,128]{1,0:T(8,128)(2,1)S(1)}, bf16[400,128]{1,0:T(8,128)(2,1)S(1)}, u32[]{:S(2)}, u32[]{:S(2)}) collective-permute-start(bf16[400,128]{1,0:T(8,128)(2,1)S(1)} %add.19.refs_2_), channel_id=1, source_target_pairs={{0,12},{1,13},{2,14},{3,15},{4,8},{5,9},{6,10},{7,11},{8,4},{9,5},... | collective-permute-start | bytes 307208 | tf_op jit(solution)/shard_map/ppermute | solution.py:646
  48.2 5.1 %collective-permute-start.8 = (bf16[400,128]{1,0:T(8,128)(2,1)S(1)}, bf16[400,128]{1,0:T(8,128)(2,1)S(1)}, u32[]{:S(2)}, u32[]{:S(2)}) collective-permute-start(bf16[400,128]{1,0:T(8,128)(2,1)S(1)} %add.19.refs_2_), channel_id=1, source_target_pairs={{0,8},{1,9},{2,10},{3,11},{4,12},{5,13},{6,14},{7,15},{8,0},{9,1},... | collective-permute-start | bytes 307208 | tf_op jit(solution)/shard_map/ppermute | solution.py:646
  49.6 4.7 %collective-permute-start.9 = (bf16[400,128]{1,0:T(8,128)(2,1)S(1)}, bf16[400,128]{1,0:T(8,128)(2,1)S(1)}, u32[]{:S(2)}, u32[]{:S(2)}) collective-permute-start(bf16[400,128]{1,0:T(8,128)(2,1)S(1)} %add.19.refs_2_), channel_id=1, source_target_pairs={{0,4},{1,5},{2,6},{3,7},{4,0},{5,1},{6,2},{7,3},{8,12},{9,13},{10,... | collective-permute-start | bytes 307208 | tf_op jit(solution)/shard_map/ppermute | solution.py:646

commit v6 on v5

--- a/solution.py
+++ b/solution.py
@@ -675,12 +675,12 @@
         in_specs=[HBM] * 10,
         out_specs=VMEM,
         scratch_shapes=[pltpu.VMEM((3, 1, rows), BF16), pltpu.SemaphoreType.DMA((3 + sum(BLOCKS),))],
-        compiler_params=pltpu.CompilerParams(vmem_limit_bytes=60 * MIB),
+        compiler_params=pltpu.CompilerParams(vmem_limit_bytes=8 * MIB),
         name="pack",
     )
     own = [gain.reshape(1, rows) for gain in (gain_self, gain_cross, gain_ff)]
     own += [self_qkv, self_out, cross_qkv, cross_out, ff_in, ff_out, refine]
-    shard = pack(*own)
+    shard = pack(*[pltpu.with_memory_space_constraint(one, pltpu.HBM) for one in own])
     steps = scenes * (HV // WIN)
     span = 2 * TOK
     start = pl.pallas_call(
@@ -762,11 +762,10 @@
     )
     grad_features = finish(d_packs, d_firsts, xhats, rstds, turned, gains).reshape(features.shape)
 
-    for bit in range(bits_of(parts)):
-        if bit > 0:
-            keep, send = keep[: keep.shape[0] // 2], keep[keep.shape[0] // 2 :]
-        if bit < bits_of(parts) - 1:
-            keep = keep + exchange(send, 1 << bit, 0)
+    for bit in range(bits_of(parts) - 1):
+        middle = keep.shape[0] // 2
+        onward = keep[middle:] + exchange(send[middle:], 1 << bit, 0)
+        keep, send = keep[:middle] + exchange(send[:middle], 1 << bit, 0), onward
     last = parts // 2
     half = shard_rows // 2
     beside = exchange(send[0, :half], last, 0)

time: 55.5 us -> 53.8 us (0.969)
  local copies, waits for them, and re-layouts: 4.07 us -> 3.14 us
  Pallas kernels: 22 us -> 21.4 us
    unnamed x12 -> x10, local copies, waits for them, and re-layouts: 4.05 us -> 3.09 us
    pallas_call x1, Pallas kernels: 1.86 us -> 1.18 us  [local(): pack(*[pltpu.with_memory_space_constraint(one, pltpu.HBM) for one in own])]
    ppermute x11 -> x12, waiting for transfers between devices: 13.6 us -> 13.8 us  [exchange(): lax.ppermute(value, ('dp', 'fsdp'), [(i, i ^ mask) for i in range(count)])]
    ppermute x11 -> x12, starting transfers between devices: 13.8 us -> 13.6 us  [exchange(): lax.ppermute(value, ('dp', 'fsdp'), [(i, i ^ mask) for i in range(count)])]
  transfers between devices with their start and end apart: 11 -> 12, of which waited for: 8 -> 10; matrix products, arithmetic and copies ran while one was open for 1% -> 1% of each run, Pallas kernels for 6% -> 6%
where the time goes in v6:
time: 53.8 us; the launch traced here: 53.5 us
  Pallas kernels  21.4 us (40%)
  waiting for transfers between devices  13.8 us (26%)
  starting transfers between devices  13.6 us (25%)
  local copies, waits for them, and re-layouts  3.14 us (6%)
  other arithmetic  0.89 us (2%)
  between operations  0.72 us (1%)
    pallas_call x1, Pallas kernels, local(): main(lives, bias, x0s, xhats, rstds, plane_offsets, depth_grad, *packed)  16 us
    ppermute x12, waiting for transfers between devices, exchange(): lax.ppermute(value, ('dp', 'fsdp'), [(i, i ^ mask) for i in range(count)])  13.8 us
    ppermute x12, starting transfers between devices, exchange(): lax.ppermute(value, ('dp', 'fsdp'), [(i, i ^ mask) for i in range(count)])  13.6 us
    unnamed x10, local copies, waits for them, and re-layouts  3.09 us
    pallas_call x1, Pallas kernels, local(): finish(d_packs, d_firsts, xhats, rstds, turned, gains)  1.86 us
    pallas_call x1, Pallas kernels, local(): began = start(view_count, features, shard, plane_offsets, depth_grad)  1.5 us
    pallas_call x1, Pallas kernels, local(): pack(*[pltpu.with_memory_space_constraint(one, pltpu.HBM) for one in own])  1.18 us
  transfers between devices with their start and end apart: 12, of which 10 were waited for; matrix products, arithmetic and copies ran while one was open for 1% of the time, Pallas kernels for 6%

profile of v6, /device:TPU:0, one launch (start us, length us, event | category | flops | bytes accessed | tf_op | source)
XLA Modules:
  0.0 53.5 jit_solution(2274527484046850286)
XLA Ops:
  0.6 1.2 %pack.1.shard = bf16[816,128]{1,0:T(8,128)(2,1)S(1)} custom-call(bf16[1,32]{1,0:T(2,128)(2,1)} %bitcast.19, bf16[1,32]{1,0:T(2,128)(2,1)} %bitcast.20, bf16[1,32]{1,0:T(2,128)(2,1)} %bitcast.21, bf16[32,384]{1,0:T(8,128)(2,1)} %refs_3_.1, bf16[32,128]{1,0:T(8,128)(2,1)} %refs_4_.1, bf16[32,384]{1,0:T(8,128)(2,1)} %refs_5_.1, bf16[32,128]{1,0:T(8,128)(2,1)} %refs_6_.1, ...), custom_call_target="tpu_custom_call" | custom-call | tf_op jit(solution)/shard_map/pack/pallas_call | solution.py:683
  1.8 3.0 %collective-permute-start = (bf16[816,128]{1,0:T(8,128)(2,1)S(1)}, bf16[816,128]{1,0:T(8,128)(2,1)S(1)}, u32[]{:S(2)}, u32[]{:S(2)}) collective-permute-start(bf16[816,128]{1,0:T(8,128)(2,1)S(1)} %pack.1.shard), channel_id=1, source_target_pairs={{0,2},{1,3},{2,0},{3,1},{4,6},{5,7},{6,4},{7,5},{8,10},{9,11},{10,... | collective-permute-start | bytes 626696 | tf_op jit(solution)/shard_map/ppermute | solution.py:646
  4.9 1.0 %copy-done = bf16[2,4,256,128]{3,2,1,0:T(8,128)(2,1)S(1)} copy-done((bf16[2,4,256,128]{3,2,1,0:T(8,128)(2,1)S(1)}, bf16[2,4,256,128]{3,2,1,0:T(8,128)(2,1)}, u32[]{:S(2)}) %copy-start) | copy-done | bytes 524312
  5.9 0.7 %copy-done.1 = f32[2,4,256]{2,1,0:T(4,128)S(1)} copy-done((f32[2,4,256]{2,1,0:T(4,128)S(1)}, f32[2,4,256]{2,1,0:T(4,128)}, u32[]{:S(2)}) %copy-start.1) | copy-done | bytes 8216
  6.6 0.7 %copy-done.2 = s32[2,4,128]{2,1,0:T(4,128)S(1)} copy-done((s32[2,4,128]{2,1,0:T(4,128)S(1)}, s32[2,4,128]{2,1,0:T(4,128)}, u32[]{:S(2)}) %copy-start.2) | copy-done | bytes 4120
  7.3 0.7 %copy-done.3 = s32[2]{0:T(128)S(1)} copy-done((s32[2]{0:T(128)S(1)}, s32[2]{0:T(128)}, u32[]{:S(2)}) %copy-start.3) | copy-done | bytes 32
  8.0 1.5 %start.1 = (s32[2,8,128]{2,1,0:T(8,128)S(1)}, f32[2,256,256]{2,1,0:T(8,128)S(1)}, f32[4,512,128]{2,1,0:T(8,128)S(1)}, f32[4,512,128]{2,1,0:T(8,128)S(1)}, f32[4,...) custom-call(s32[2]{0:T(128)S(1)} %copy-done.3, ...), custom_call_target="tpu_custom_call" | custom-call | flops 2621440 | bytes 3670016 | tf_op jit(solution)/shard_map/start/pallas_call | solution.py:700
  9.5 0.6 %collective-permute-done.refs_2_ = bf16[816,128]{1,0:T(8,128)(2,1)S(1)} collective-permute-done((bf16[816,128]{1,0:T(8,128)(2,1)S(1)}, bf16[816,128]{1,0:T(8,128)(2,1)S(1)}, u32[]{:S(2)}, u32[]{:S(2)}) %collective-permute-start) | collective-permute-done | bytes 208928 | tf_op jit(solution)/shard_map/ppermute | solution.py:646
  10.0 1.4 %collective-permute-done.2.refs_3_ = bf16[816,128]{1,0:T(8,128)(2,1)S(1)} collective-permute-done((bf16[816,128]{1,0:T(8,128)(2,1)S(1)}, bf16[816,128]{1,0:T(8,128)(2,1)S(1)}, u32[]{:S(2)}, u32[]{:S(2)}) %collective-permute-start.2) | collective-permute-done | bytes 208928 | tf_op jit(solution)/shard_map/ppermute | solution.py:646
  11.5 16.0 %layer.1 = (f32[2,4,256]{2,1,0:T(4,128)S(1)}, bf16[4,512,384]{2,1,0:T(8,128)(2,1)S(1)}, f32[4,512,128]{2,1,0:T(8,128)S(1)}, bf16[384,128]{1,0:T(8,128)(2,1)S(1)}...) custom-call(s32[2,8,128]{2,1,0:T(8,128)S(1)} %get-tuple-element.54.lives, ...), custom_call_target="tpu_custom_call" | custom-call | tf_op jit(solution)/shard_map/layer/pallas_call | solution.py:750
  28.1 0.9 %collective-permute-done.3 = bf16[1,800,128]{2,1,0:T(8,128)(2,1)S(1)} collective-permute-done((bf16[1,800,128]{2,1,0:T(8,128)(2,1)S(1)}, bf16[1,800,128]{2,1,0:T(8,128)(2,1)S(1)}, u32[]{:S(2)}, u32[]{:S(2)}) %collective-permute-start.3) | collective-permute-done | bytes 204832 | tf_op jit(solution)/shard_map/ppermute | solution.py:646
  29.4 1.8 %collective-permute-start.5 = (bf16[400,128]{1,0:T(8,128)(2,1)S(1)}, bf16[400,128]{1,0:T(8,128)(2,1)S(1)}, u32[]{:S(2)}, u32[]{:S(2)}) collective-permute-start(bf16[400,128]{1,0:T(8,128)(2,1)S(1)} %get-tuple-element.84), channel_id=1, source_target_pairs={{0,2},{1,3},{2,0},{3,1},{4,6},{5,7},{6,4},{7,5},{8,10},{9,11},{10,... | collective-permute-start | bytes 307208 | tf_op jit(solution)/shard_map/ppermute | solution.py:646
  31.2 1.4 %collective-permute-start.7 = (bf16[400,128]{1,0:T(8,128)(2,1)S(1)}, bf16[400,128]{1,0:T(8,128)(2,1)S(1)}, u32[]{:S(2)}, u32[]{:S(2)}) collective-permute-start(bf16[400,128]{1,0:T(8,128)(2,1)S(1)} %get-tuple-element.85), channel_id=1, source_target_pairs={{0,6},{1,7},{2,4},{3,5},{4,2},{5,3},{6,0},{7,1},{8,14},{9,15},{10,... | collective-permute-start | bytes 307208 | tf_op jit(solution)/shard_map/ppermute | solution.py:646
  33.1 2.9 %collective-permute-done.5 = bf16[400,128]{1,0:T(8,128)(2,1)S(1)} collective-permute-done((bf16[400,128]{1,0:T(8,128)(2,1)S(1)}, bf16[400,128]{1,0:T(8,128)(2,1)S(1)}, u32[]{:S(2)}, u32[]{:S(2)}) %collective-permute-start.5) | collective-permute-done | bytes 102432 | tf_op jit(solution)/shard_map/ppermute | solution.py:646
  36.0 1.8 %collective-permute-done.7 = bf16[400,128]{1,0:T(8,128)(2,1)S(1)} collective-permute-done((bf16[400,128]{1,0:T(8,128)(2,1)S(1)}, bf16[400,128]{1,0:T(8,128)(2,1)S(1)}, u32[]{:S(2)}, u32[]{:S(2)}) %collective-permute-start.7) | collective-permute-done | bytes 102432 | tf_op jit(solution)/shard_map/ppermute | solution.py:646
  38.1 2.8 %collective-permute-start.8 = (bf16[400,128]{1,0:T(8,128)(2,1)S(1)}, bf16[400,128]{1,0:T(8,128)(2,1)S(1)}, u32[]{:S(2)}, u32[]{:S(2)}) collective-permute-start(bf16[400,128]{1,0:T(8,128)(2,1)S(1)} %fusion.1), channel_id=1, source_target_pairs={{0,16},{1,17},{2,18},{3,19},{4,20},{5,21},{6,22},{7,23},{8,24},{9,... | collective-permute-start | bytes 307208 | tf_op jit(solution)/shard_map/ppermute | solution.py:646
  40.9 4.4 %collective-permute-done.8 = bf16[400,128]{1,0:T(8,128)(2,1)S(1)} collective-permute-done((bf16[400,128]{1,0:T(8,128)(2,1)S(1)}, bf16[400,128]{1,0:T(8,128)(2,1)S(1)}, u32[]{:S(2)}, u32[]{:S(2)}) %collective-permute-start.8) | collective-permute-done | bytes 102432 | tf_op jit(solution)/shard_map/ppermute | solution.py:646
  45.3 1.5 %collective-permute-start.10 = (bf16[400,128]{1,0:T(8,128)(2,1)S(1)}, bf16[400,128]{1,0:T(8,128)(2,1)S(1)}, u32[]{:S(2)}, u32[]{:S(2)}) collective-permute-start(bf16[400,128]{1,0:T(8,128)(2,1)S(1)} %add.23.refs_2_), channel_id=1, source_target_pairs={{0,4},{1,5},{2,6},{3,7},{4,0},{5,1},{6,2},{7,3},{8,12},{9,13},{10,... | collective-permute-start | bytes 307208 | tf_op jit(solution)/shard_map/ppermute | solution.py:646
  46.9 0.7 %collective-permute-start.11 = (bf16[400,128]{1,0:T(8,128)(2,1)S(1)}, bf16[400,128]{1,0:T(8,128)(2,1)S(1)}, u32[]{:S(2)}, u32[]{:S(2)}) collective-permute-start(bf16[400,128]{1,0:T(8,128)(2,1)S(1)} %add.23.refs_2_), channel_id=1, source_target_pairs={{0,12},{1,13},{2,14},{3,15},{4,8},{5,9},{6,10},{7,11},{8,4},{9,5},... | collective-permute-start | bytes 307208 | tf_op jit(solution)/shard_map/ppermute | solution.py:646
  47.5 1.4 %collective-permute-start.9 = (bf16[400,128]{1,0:T(8,128)(2,1)S(1)}, bf16[400,128]{1,0:T(8,128)(2,1)S(1)}, u32[]{:S(2)}, u32[]{:S(2)}) collective-permute-start(bf16[400,128]{1,0:T(8,128)(2,1)S(1)} %add.23.refs_2_), channel_id=1, source_target_pairs={{0,8},{1,9},{2,10},{3,11},{4,12},{5,13},{6,14},{7,15},{8,0},{9,1},... | collective-permute-start | bytes 307208 | tf_op jit(solution)/shard_map/ppermute | solution.py:646
  48.9 0.7 %broadcast_multiply_fusion = f32[2,4,256]{2,1,0:T(4,128)} fusion(f32[2,4,256]{2,1,0:T(4,128)S(1)} %get-tuple-element.63, f32[2,4]{1,0:T(2,128)S(1)} %compare_convert_fusion), kind=kLoop, calls=%fused_computation.9 | loop fusion | flops 2048 | bytes 16416 | tf_op jit(solution)/shard_map/mul | solution.py:803
  49.6 1.9 %finish.1 = f32[2,4,2,8,2,8,128]{6,5,4,3,2,1,0:T(8,128)} custom-call(bf16[4,512,384]{2,1,0:T(8,128)(2,1)S(1)} %get-tuple-element.64.d_packed, f32[4,512,128]{2,1,0:T(8,128)S(1)} %get-tuple-element.65.d_first, f32[4,512,128]{2,1,0:T(8,128)S(1)} %get-tuple-element.57.xh_a.xhats, f32[4,512,128]{2,1,0:T(8,128)S(1)} %get-tuple-element.58.rs_a.rstds, ...), custom_call_target="tpu_custom_call" | custom-call | flops 201326592 | bytes 4194304 | tf_op jit(solution)/shard_map/finish/pallas_call | solution.py:763
  51.4 1.0 %collective-permute-done.11.refs_5_ = bf16[400,128]{1,0:T(8,128)(2,1)S(1)} collective-permute-done((bf16[400,128]{1,0:T(8,128)(2,1)S(1)}, bf16[400,128]{1,0:T(8,128)(2,1)S(1)}, u32[]{:S(2)}, u32[]{:S(2)}) %collective-permute-start.11) | collective-permute-done | bytes 102432 | tf_op jit(solution)/shard_map/ppermute | solution.py:646
  52.6 0.8 %unpack.1 = (f32[1,32]{1,0:T(1,128)}, f32[1,32]{1,0:T(1,128)}, f32[1,32]{1,0:T(1,128)}, f32[32,384]{1,0:T(8,128)}, f32[32,128]{1,0:T(8,128)}, /*index=5*/f32[32,...) custom-call(f32[8,128]{1,0:T(8,128)S(1)} %get-tuple-element.67.gains.refs_0_, ...), custom_call_target="tpu_custom_call" | custom-call | tf_op jit(solution)/shard_map/unpack/pallas_call | solution.py:799
  (23 shorter events, 2.0 us)
Async XLA Ops:
  1.8 8.2 %collective-permute-start = (bf16[816,128]{1,0:T(8,128)(2,1)S(1)}, bf16[816,128]{1,0:T(8,128)(2,1)S(1)}, u32[]{:S(2)}, u32[]{:S(2)}) collective-permute-start(bf16[816,128]{1,0:T(8,128)(2,1)S(1)} %pack.1.shard), channel_id=1, source_target_pairs={{0,2},{1,3},{2,0},{3,1},{4,6},{5,7},{6,4},{7,5},{8,10},{9,11},{10,... | collective-permute-start | bytes 626696 | tf_op jit(solution)/shard_map/ppermute | solution.py:646
  4.9 5.2 %collective-permute-start.1 = (bf16[816,128]{1,0:T(8,128)(2,1)S(1)}, bf16[816,128]{1,0:T(8,128)(2,1)S(1)}, u32[]{:S(2)}, u32[]{:S(2)}) collective-permute-start(bf16[816,128]{1,0:T(8,128)(2,1)S(1)} %pack.1.shard), channel_id=1, source_target_pairs={{0,1},{1,0},{2,3},{3,2},{4,5},{5,4},{6,7},{7,6},{8,9},{9,8},{10,11... | collective-permute-start | bytes 626696 | tf_op jit(solution)/shard_map/ppermute | solution.py:646
  4.9 1.0 %copy-start = (bf16[2,4,256,128]{3,2,1,0:T(8,128)(2,1)S(1)}, bf16[2,4,256,128]{3,2,1,0:T(8,128)(2,1)}, u32[]{:S(2)}) copy-start(bf16[2,4,256,128]{3,2,1,0:T(8,128)(2,1)} %features.1) | copy-start | bytes 1572868
  5.9 0.7 %copy-start.1 = (f32[2,4,256]{2,1,0:T(4,128)S(1)}, f32[2,4,256]{2,1,0:T(4,128)}, u32[]{:S(2)}) copy-start(f32[2,4,256]{2,1,0:T(4,128)} %depth_grad.1) | copy-start | bytes 24580
  6.6 0.7 %copy-start.2 = (s32[2,4,128]{2,1,0:T(4,128)S(1)}, s32[2,4,128]{2,1,0:T(4,128)}, u32[]{:S(2)}) copy-start(s32[2,4,128]{2,1,0:T(4,128)} %offsets.1) | copy-start | bytes 12292
  7.3 0.7 %copy-start.3 = (s32[2]{0:T(128)S(1)}, s32[2]{0:T(128)}, u32[]{:S(2)}) copy-start(s32[2]{0:T(128)} %count.1) | copy-start | bytes 28
  10.0 1.5 %collective-permute-start.2 = (bf16[816,128]{1,0:T(8,128)(2,1)S(1)}, bf16[816,128]{1,0:T(8,128)(2,1)S(1)}, u32[]{:S(2)}, u32[]{:S(2)}) collective-permute-start(bf16[816,128]{1,0:T(8,128)(2,1)S(1)} %collective-permute-done.refs_2_), channel_id=1, source_target_pairs={{0,1},{1,0},{2,3},{3,2},{4,5},{5,4},{6,7},{7,6},{8,9},{9,8},{10,11... | collective-permute-start | bytes 626696 | tf_op jit(solution)/shard_map/ppermute | solution.py:646
  27.5 13.4 %copy-start.4 = (s32[2]{0:T(128)S(1)}, s32[2]{0:T(128)}, u32[]{:S(2)}) copy-start(s32[2]{0:T(128)} %count.1) | copy-start | bytes 28
  27.5 1.5 %collective-permute-start.3 = (bf16[1,800,128]{2,1,0:T(8,128)(2,1)S(1)}, bf16[1,800,128]{2,1,0:T(8,128)(2,1)S(1)}, u32[]{:S(2)}, u32[]{:S(2)}) collective-permute-start(bf16[1,800,128]{2,1,0:T(8,128)(2,1)S(1)} %get-tuple-element.82), channel_id=1, source_target_pairs={{0,1},{1,0},{2,3},{3,2},{4,5},{5,4},{6,7},{7,6},{8,9},{9,8},{10,11... | collective-permute-start | bytes 614408 | tf_op jit(solution)/shard_map/ppermute | solution.py:646
  27.7 1.6 %collective-permute-start.4 = (bf16[1,800,128]{2,1,0:T(8,128)(2,1)S(1)}, bf16[1,800,128]{2,1,0:T(8,128)(2,1)S(1)}, u32[]{:S(2)}, u32[]{:S(2)}) collective-permute-start(bf16[1,800,128]{2,1,0:T(8,128)(2,1)S(1)} %get-tuple-element.83), channel_id=1, source_target_pairs={{0,1},{1,0},{2,3},{3,2},{4,5},{5,4},{6,7},{7,6},{8,9},{9,8},{10,11... | collective-permute-start | bytes 614408 | tf_op jit(solution)/shard_map/ppermute | solution.py:646
  29.4 6.6 %collective-permute-start.5 = (bf16[400,128]{1,0:T(8,128)(2,1)S(1)}, bf16[400,128]{1,0:T(8,128)(2,1)S(1)}, u32[]{:S(2)}, u32[]{:S(2)}) collective-permute-start(bf16[400,128]{1,0:T(8,128)(2,1)S(1)} %get-tuple-element.84), channel_id=1, source_target_pairs={{0,2},{1,3},{2,0},{3,1},{4,6},{5,7},{6,4},{7,5},{8,10},{9,11},{10,... | collective-permute-start | bytes 307208 | tf_op jit(solution)/shard_map/ppermute | solution.py:646
  31.2 6.5 %collective-permute-start.7 = (bf16[400,128]{1,0:T(8,128)(2,1)S(1)}, bf16[400,128]{1,0:T(8,128)(2,1)S(1)}, u32[]{:S(2)}, u32[]{:S(2)}) collective-permute-start(bf16[400,128]{1,0:T(8,128)(2,1)S(1)} %get-tuple-element.85), channel_id=1, source_target_pairs={{0,6},{1,7},{2,4},{3,5},{4,2},{5,3},{6,0},{7,1},{8,14},{9,15},{10,... | collective-permute-start | bytes 307208 | tf_op jit(solution)/shard_map/ppermute | solution.py:646
  32.7 5.3 %collective-permute-start.6 = (bf16[400,128]{1,0:T(8,128)(2,1)S(1)}, bf16[400,128]{1,0:T(8,128)(2,1)S(1)}, u32[]{:S(2)}, u32[]{:S(2)}) collective-permute-start(bf16[400,128]{1,0:T(8,128)(2,1)S(1)} %slice_bitcast_fusion.1), channel_id=1, source_target_pairs={{0,4},{1,5},{2,6},{3,7},{4,0},{5,1},{6,2},{7,3},{8,12},{9,13},{10,... | collective-permute-start | bytes 307208 | tf_op jit(solution)/shard_map/ppermute | solution.py:646
  38.1 7.2 %collective-permute-start.8 = (bf16[400,128]{1,0:T(8,128)(2,1)S(1)}, bf16[400,128]{1,0:T(8,128)(2,1)S(1)}, u32[]{:S(2)}, u32[]{:S(2)}) collective-permute-start(bf16[400,128]{1,0:T(8,128)(2,1)S(1)} %fusion.1), channel_id=1, source_target_pairs={{0,16},{1,17},{2,18},{3,19},{4,20},{5,21},{6,22},{7,23},{8,24},{9,... | collective-permute-start | bytes 307208 | tf_op jit(solution)/shard_map/ppermute | solution.py:646
  45.3 6.1 %collective-permute-start.10 = (bf16[400,128]{1,0:T(8,128)(2,1)S(1)}, bf16[400,128]{1,0:T(8,128)(2,1)S(1)}, u32[]{:S(2)}, u32[]{:S(2)}) collective-permute-start(bf16[400,128]{1,0:T(8,128)(2,1)S(1)} %add.23.refs_2_), channel_id=1, source_target_pairs={{0,4},{1,5},{2,6},{3,7},{4,0},{5,1},{6,2},{7,3},{8,12},{9,13},{10,... | collective-permute-start | bytes 307208 | tf_op jit(solution)/shard_map/ppermute | solution.py:646
  46.9 5.6 %collective-permute-start.11 = (bf16[400,128]{1,0:T(8,128)(2,1)S(1)}, bf16[400,128]{1,0:T(8,128)(2,1)S(1)}, u32[]{:S(2)}, u32[]{:S(2)}) collective-permute-start(bf16[400,128]{1,0:T(8,128)(2,1)S(1)} %add.23.refs_2_), channel_id=1, source_target_pairs={{0,12},{1,13},{2,14},{3,15},{4,8},{5,9},{6,10},{7,11},{8,4},{9,5},... | collective-permute-start | bytes 307208 | tf_op jit(solution)/shard_map/ppermute | solution.py:646
  47.5 5.1 %collective-permute-start.9 = (bf16[400,128]{1,0:T(8,128)(2,1)S(1)}, bf16[400,128]{1,0:T(8,128)(2,1)S(1)}, u32[]{:S(2)}, u32[]{:S(2)}) collective-permute-start(bf16[400,128]{1,0:T(8,128)(2,1)S(1)} %add.23.refs_2_), channel_id=1, source_target_pairs={{0,8},{1,9},{2,10},{3,11},{4,12},{5,13},{6,14},{7,15},{8,0},{9,1},... | collective-permute-start | bytes 307208 | tf_op jit(solution)/shard_map/ppermute | solution.py:646

commit v7 on v6

--- a/solution.py
+++ b/solution.py
@@ -198,7 +198,7 @@
 
 def start_kernel(
     scenes, count, features, shard, offsets, depth_grad,
-    lives, bias, x0s, xhats, rstds, shard_out, offsets_out, grad_out,
+    lives, bias, x0s, xhats, rstds, shard_out, hots, incoming,
 ):
     of_key = iota((TOK, TOK), 1) // (WIN * WIN)
     of_query = iota((TOK, TOK), 0) // (WIN * WIN)
@@ -207,8 +207,20 @@
         lives[scene] = jnp.broadcast_to(live, (8, C))
         bias[scene] = jnp.where((of_key < live) & (of_key != of_query), 0.0, MASKED)
     shard_out[...] = shard[...]
-    offsets_out[...] = offsets[...]
-    grad_out[...] = depth_grad[...]
+    row = iota((HV, C), 0)
+    eye = jnp.where(iota((HALF, HALF), 0) == iota((HALF, HALF), 1), 1.0, 0.0)
+    hots[...] = jnp.zeros_like(hots)
+    for scene in range(scenes):
+        for view in range(VIEWS):
+            shift = offsets[scene, view : view + 1, :]
+            hot = (shift == row).astype(BF16)
+            hots[scene, 0, view, 0:HV, :] = hot
+            hots[scene, 0, view, C : C + HV, :] = hot
+            hots[scene, 1, view, 0:HV, :] = (shift == HV - 1 - row).astype(BF16)
+            for part in range(2):
+                at = slice(part * HALF, (part + 1) * HALF)
+                column = jnp.sum(eye * depth_grad[scene, view : view + 1, at], 1, keepdims=True)
+                incoming[scene, view, at, :] = jnp.broadcast_to(column, (HALF, C))
     for scene in range(scenes):
         for half in range(2):
             step = 2 * scene + half
@@ -233,8 +245,8 @@
     x0s,
     xh_a,
     rs_a,
-    offsets,
-    depth_grad,
+    hots,
+    incoming,
     *refs,
 ):
     packed, refs = refs[:parts], refs[parts:]
@@ -256,7 +268,7 @@
     x3s, d3s,
     low, rev,
     pads, taps, back_taps,
-    tables, eye, flip, hots,
+    tables, eye, flip,
     g_sq, g_so, g_cq, g_co, g_fi, g_fo, g_rf,
     ) = refs
     rows = C // parts
@@ -292,7 +304,7 @@
         ref[9 * C :, :C] = jnp.zeros((3 * C, C), BF16)
         ref[: 3 * C, C:] = jnp.zeros((3 * C, C), BF16)
 
-    for ref in (g_sq, g_so, g_cq, g_co, g_fi, g_fo, g_rf, pads, hots):
+    for ref in (g_sq, g_so, g_cq, g_co, g_fi, g_fo, g_rf, pads):
         ref[...] = jnp.zeros_like(ref)
     empty = rows_of(parts) - sum(BLOCKS) * rows
     if empty:
@@ -414,10 +426,6 @@
 
         for view in views:
             low[scene, view] = x3s[scene, view].reshape(PIX, C).astype(BF16)
-            shift = offsets[scene, view : view + 1, :]
-            hots[scene, 0, view, 0:HV, :] = (shift == row).astype(BF16)
-            hots[scene, 0, view, C : C + HV, :] = (shift == row).astype(BF16)
-            hots[scene, 1, view, 0:HV, :] = (shift == HV - 1 - row).astype(BF16)
         yield 300
         for view in views:
             rev[scene, view] = unpaired(mm(flip[...], paired(low[scene, view])).astype(BF16))
@@ -444,11 +452,9 @@
             inverse = 1.0 / jnp.sum(expo, -1, keepdims=True)
             depth = jnp.sum(expo * depth_values, -1, keepdims=True) * inverse
             valid = jnp.where(view < live, 1.0, 0.0)
-            incoming = []
             for at in upper:
                 depth_out[scene, view : view + 1, at] = jnp.sum(eye[...] * depth[at], 0, keepdims=True)
-                incoming.append(jnp.sum(eye[...] * depth_grad[scene, view : view + 1, at], 1, keepdims=True))
-            weight = joined(incoming) * (inverse * valid)
+            weight = incoming[scene, view] * (inverse * valid)
             d_refined.append(expo * (weight * depth_values - weight * depth))
             yield 250
         for view in views:
@@ -690,14 +696,19 @@
             jax.ShapeDtypeStruct((scenes, TOK, TOK), F32),
         )
         + (jax.ShapeDtypeStruct((steps, span, C), F32),) * 3
-        + tuple(jax.ShapeDtypeStruct(piece.shape, piece.dtype) for piece in (shard, plane_offsets, depth_grad)),
+        + (
+            jax.ShapeDtypeStruct(shard.shape, BF16),
+            jax.ShapeDtypeStruct((scenes, 2, VIEWS, 2 * C, C), BF16),
+            jax.ShapeDtypeStruct((scenes, VIEWS, PIX, C), F32),
+        ),
         in_specs=[SMEM] + [VMEM] * 4,
         out_specs=(VMEM,) * 8,
         compiler_params=small,
         cost_estimate=pl.CostEstimate(flops=10 * features.size, bytes_accessed=14 * features.size, transcendentals=0),
         name="start",
     )
-    began = start(view_count, features, shard, plane_offsets, depth_grad)
+    hbm = [pltpu.with_memory_space_constraint(one, pltpu.HBM) for one in (features, plane_offsets, depth_grad)]
+    began = start(view_count, hbm[0], shard, hbm[1], hbm[2])
 
     packed = {0: shard}
     for bit in reversed(range(bits_of(parts))):
@@ -725,7 +736,7 @@
         ((scenes, VIEWS, PIX, C), BF16), ((scenes, VIEWS, PIX, C), BF16),
         ((scenes, 2, VIEWS, PIX + 16, C), F32),
         ((scenes, VIEWS, PIX + 2 * HV, 3 * C), BF16), ((scenes, VIEWS, PIX + 2 * HV, 3 * C), BF16),
-        ((4 * HV, C), F32), ((HALF, HALF), F32), ((HALF, HALF), BF16), ((scenes, 2, VIEWS, 2 * C, C), BF16),
+        ((4 * HV, C), F32), ((HALF, HALF), F32), ((HALF, HALF), BF16),
         ((C, 3 * C), F32), ((C, C), F32), ((C, 3 * C), F32), ((C, C), F32),
         ((C, FFH), F32), ((C, FFH), F32), ((C, 9 * PLANES), F32),
     ]
@@ -743,12 +754,12 @@
         in_specs=[VMEM] * (7 + parts),
         out_specs=(VMEM,) * 7,
         scratch_shapes=[pltpu.VMEM(shape, kind) for shape, kind in scratch],
-        compiler_params=pltpu.CompilerParams(vmem_limit_bytes=46 * MIB),
+        compiler_params=pltpu.CompilerParams(vmem_limit_bytes=43 * MIB),
         name="layer",
     )
-    lives, bias, x0s, xhats, rstds, packed[0], plane_offsets, depth_grad = began
+    lives, bias, x0s, xhats, rstds, packed[0], hots, incoming = began
     depth, d_packs, d_firsts, turned, gains, keep, send = main(
-        lives, bias, x0s, xhats, rstds, plane_offsets, depth_grad, *packed
+        lives, bias, x0s, xhats, rstds, hots, incoming, *packed
     )
 
     finish = pl.pallas_call(

time: 53.8 us -> 53.4 us (level)
  local copies, waits for them, and re-layouts: 3.14 us -> 0.71 us
  waiting for transfers between devices: 13.8 us -> 15.3 us
  Pallas kernels: 21.4 us -> 22 us
    unnamed x10 -> x4, local copies, waits for them, and re-layouts: 3.09 us -> 0.66 us
    ppermute x12, waiting for transfers between devices: 13.8 us -> 15.3 us  [exchange(): lax.ppermute(value, ('dp', 'fsdp'), [(i, i ^ mask) for i in range(count)])]
    pallas_call x2, Pallas kernels: 17.5 us -> 18.1 us  [the longest x1 15.7 us: local(): main(lives, bias, x0s, xhats, rstds, hots, incoming, *packed)]
  transfers between devices with their start and end apart: 12 -> 12, of which waited for: 10 -> 10; matrix products, arithmetic and copies ran while one was open for 1% -> 1% of each run, Pallas kernels for 6% -> 8%
where the time goes in v7:
time: 53.4 us; the launch traced here: 53.1 us
  Pallas kernels  22 us (41%)
  waiting for transfers between devices  15.3 us (29%)
  starting transfers between devices  13.6 us (25%)
  other arithmetic  0.87 us (2%)
  between operations  0.72 us (1%)
  local copies, waits for them, and re-layouts  0.71 us (1%)
    pallas_call x1, Pallas kernels, local(): main(lives, bias, x0s, xhats, rstds, hots, incoming, *packed)  15.7 us
    ppermute x12, waiting for transfers between devices, exchange(): lax.ppermute(value, ('dp', 'fsdp'), [(i, i ^ mask) for i in range(count)])  15.3 us
    ppermute x12, starting transfers between devices, exchange(): lax.ppermute(value, ('dp', 'fsdp'), [(i, i ^ mask) for i in range(count)])  13.6 us
    pallas_call x1, Pallas kernels, local(): began = start(view_count, hbm[0], shard, hbm[1], hbm[2])  2.46 us
    pallas_call x1, Pallas kernels, local(): finish(d_packs, d_firsts, xhats, rstds, turned, gains)  1.81 us
    pallas_call x1, Pallas kernels, local(): pack(*[pltpu.with_memory_space_constraint(one, pltpu.HBM) for one in own])  1.18 us
  transfers between devices with their start and end apart: 12, of which 10 were waited for; matrix products, arithmetic and copies ran while one was open for 1% of the time, Pallas kernels for 8%

profile of v7, /device:TPU:0, one launch (start us, length us, event | category | flops | bytes accessed | tf_op | source)
XLA Modules:
  0.0 53.1 jit_solution(5464559844920027490)
XLA Ops:
  0.6 1.2 %pack.1.shard = bf16[816,128]{1,0:T(8,128)(2,1)S(1)} custom-call(bf16[1,32]{1,0:T(2,128)(2,1)} %bitcast.19, bf16[1,32]{1,0:T(2,128)(2,1)} %bitcast.20, bf16[1,32]{1,0:T(2,128)(2,1)} %bitcast.21, bf16[32,384]{1,0:T(8,128)(2,1)} %refs_3_.1, bf16[32,128]{1,0:T(8,128)(2,1)} %refs_4_.1, bf16[32,384]{1,0:T(8,128)(2,1)} %refs_5_.1, bf16[32,128]{1,0:T(8,128)(2,1)} %refs_6_.1, ...), custom_call_target="tpu_custom_call" | custom-call | tf_op jit(solution)/shard_map/pack/pallas_call | solution.py:689
  1.8 3.0 %collective-permute-start = (bf16[816,128]{1,0:T(8,128)(2,1)S(1)}, bf16[816,128]{1,0:T(8,128)(2,1)S(1)}, u32[]{:S(2)}, u32[]{:S(2)}) collective-permute-start(bf16[816,128]{1,0:T(8,128)(2,1)S(1)} %pack.1.shard), channel_id=1, source_target_pairs={{0,2},{1,3},{2,0},{3,1},{4,6},{5,7},{6,4},{7,5},{8,10},{9,11},{10,... | collective-permute-start | bytes 626696 | tf_op jit(solution)/shard_map/ppermute | solution.py:652
  4.9 0.7 %copy-done = s32[2]{0:T(128)S(1)} copy-done((s32[2]{0:T(128)S(1)}, s32[2]{0:T(128)}, u32[]{:S(2)}) %copy-start) | copy-done | bytes 32
  5.5 2.5 %start.1 = (s32[2,8,128]{2,1,0:T(8,128)S(1)}, f32[2,256,256]{2,1,0:T(8,128)S(1)}, f32[4,512,128]{2,1,0:T(8,128)S(1)}, f32[4,512,128]{2,1,0:T(8,128)S(1)}, f32[4,...) custom-call(s32[2]{0:T(128)S(1)} %copy-done, ...), custom_call_target="tpu_custom_call" | custom-call | flops 2621440 | bytes 3670016 | tf_op jit(solution)/shard_map/start/pallas_call | solution.py:711
  8.0 2.0 %collective-permute-done.refs_2_ = bf16[816,128]{1,0:T(8,128)(2,1)S(1)} collective-permute-done((bf16[816,128]{1,0:T(8,128)(2,1)S(1)}, bf16[816,128]{1,0:T(8,128)(2,1)S(1)}, u32[]{:S(2)}, u32[]{:S(2)}) %collective-permute-start) | collective-permute-done | bytes 208928 | tf_op jit(solution)/shard_map/ppermute | solution.py:652
  10.0 1.5 %collective-permute-done.2.refs_3_ = bf16[816,128]{1,0:T(8,128)(2,1)S(1)} collective-permute-done((bf16[816,128]{1,0:T(8,128)(2,1)S(1)}, bf16[816,128]{1,0:T(8,128)(2,1)S(1)}, u32[]{:S(2)}, u32[]{:S(2)}) %collective-permute-start.2) | collective-permute-done | bytes 208928 | tf_op jit(solution)/shard_map/ppermute | solution.py:652
  11.5 15.7 %layer.1 = (f32[2,4,256]{2,1,0:T(4,128)S(1)}, bf16[4,512,384]{2,1,0:T(8,128)(2,1)S(1)}, f32[4,512,128]{2,1,0:T(8,128)S(1)}, bf16[384,128]{1,0:T(8,128)(2,1)S(1)}...) custom-call(s32[2,8,128]{2,1,0:T(8,128)S(1)} %get-tuple-element.54.lives, ...), custom_call_target="tpu_custom_call" | custom-call | tf_op jit(solution)/shard_map/layer/pallas_call | solution.py:761
  27.4 0.4 collective-permute-start.4
  27.8 0.9 %collective-permute-done.3 = bf16[1,800,128]{2,1,0:T(8,128)(2,1)S(1)} collective-permute-done((bf16[1,800,128]{2,1,0:T(8,128)(2,1)S(1)}, bf16[1,800,128]{2,1,0:T(8,128)(2,1)S(1)}, u32[]{:S(2)}, u32[]{:S(2)}) %collective-permute-start.3) | collective-permute-done | bytes 204832 | tf_op jit(solution)/shard_map/ppermute | solution.py:652
  28.7 0.3 collective-permute-done.4
  29.1 1.8 %collective-permute-start.5 = (bf16[400,128]{1,0:T(8,128)(2,1)S(1)}, bf16[400,128]{1,0:T(8,128)(2,1)S(1)}, u32[]{:S(2)}, u32[]{:S(2)}) collective-permute-start(bf16[400,128]{1,0:T(8,128)(2,1)S(1)} %get-tuple-element.84), channel_id=1, source_target_pairs={{0,2},{1,3},{2,0},{3,1},{4,6},{5,7},{6,4},{7,5},{8,10},{9,11},{10,... | collective-permute-start | bytes 307208 | tf_op jit(solution)/shard_map/ppermute | solution.py:652
  30.9 1.4 %collective-permute-start.7 = (bf16[400,128]{1,0:T(8,128)(2,1)S(1)}, bf16[400,128]{1,0:T(8,128)(2,1)S(1)}, u32[]{:S(2)}, u32[]{:S(2)}) collective-permute-start(bf16[400,128]{1,0:T(8,128)(2,1)S(1)} %get-tuple-element.85), channel_id=1, source_target_pairs={{0,6},{1,7},{2,4},{3,5},{4,2},{5,3},{6,0},{7,1},{8,14},{9,15},{10,... | collective-permute-start | bytes 307208 | tf_op jit(solution)/shard_map/ppermute | solution.py:652
  32.3 0.4 collective-permute-start.6
  32.7 2.9 %collective-permute-done.5 = bf16[400,128]{1,0:T(8,128)(2,1)S(1)} collective-permute-done((bf16[400,128]{1,0:T(8,128)(2,1)S(1)}, bf16[400,128]{1,0:T(8,128)(2,1)S(1)}, u32[]{:S(2)}, u32[]{:S(2)}) %collective-permute-start.5) | collective-permute-done | bytes 102432 | tf_op jit(solution)/shard_map/ppermute | solution.py:652
  35.7 1.8 %collective-permute-done.7 = bf16[400,128]{1,0:T(8,128)(2,1)S(1)} collective-permute-done((bf16[400,128]{1,0:T(8,128)(2,1)S(1)}, bf16[400,128]{1,0:T(8,128)(2,1)S(1)}, u32[]{:S(2)}, u32[]{:S(2)}) %collective-permute-start.7) | collective-permute-done | bytes 102432 | tf_op jit(solution)/shard_map/ppermute | solution.py:652
  37.7 2.8 %collective-permute-start.8 = (bf16[400,128]{1,0:T(8,128)(2,1)S(1)}, bf16[400,128]{1,0:T(8,128)(2,1)S(1)}, u32[]{:S(2)}, u32[]{:S(2)}) collective-permute-start(bf16[400,128]{1,0:T(8,128)(2,1)S(1)} %fusion.1), channel_id=1, source_target_pairs={{0,16},{1,17},{2,18},{3,19},{4,20},{5,21},{6,22},{7,23},{8,24},{9,... | collective-permute-start | bytes 307208 | tf_op jit(solution)/shard_map/ppermute | solution.py:652
  40.6 4.4 %collective-permute-done.8 = bf16[400,128]{1,0:T(8,128)(2,1)S(1)} collective-permute-done((bf16[400,128]{1,0:T(8,128)(2,1)S(1)}, bf16[400,128]{1,0:T(8,128)(2,1)S(1)}, u32[]{:S(2)}, u32[]{:S(2)}) %collective-permute-start.8) | collective-permute-done | bytes 102432 | tf_op jit(solution)/shard_map/ppermute | solution.py:652
  45.0 1.5 %collective-permute-start.10 = (bf16[400,128]{1,0:T(8,128)(2,1)S(1)}, bf16[400,128]{1,0:T(8,128)(2,1)S(1)}, u32[]{:S(2)}, u32[]{:S(2)}) collective-permute-start(bf16[400,128]{1,0:T(8,128)(2,1)S(1)} %add.23.refs_2_), channel_id=1, source_target_pairs={{0,4},{1,5},{2,6},{3,7},{4,0},{5,1},{6,2},{7,3},{8,12},{9,13},{10,... | collective-permute-start | bytes 307208 | tf_op jit(solution)/shard_map/ppermute | solution.py:652
  46.5 0.7 %collective-permute-start.11 = (bf16[400,128]{1,0:T(8,128)(2,1)S(1)}, bf16[400,128]{1,0:T(8,128)(2,1)S(1)}, u32[]{:S(2)}, u32[]{:S(2)}) collective-permute-start(bf16[400,128]{1,0:T(8,128)(2,1)S(1)} %add.23.refs_2_), channel_id=1, source_target_pairs={{0,12},{1,13},{2,14},{3,15},{4,8},{5,9},{6,10},{7,11},{8,4},{9,5},... | collective-permute-start | bytes 307208 | tf_op jit(solution)/shard_map/ppermute | solution.py:652
  47.2 1.4 %collective-permute-start.9 = (bf16[400,128]{1,0:T(8,128)(2,1)S(1)}, bf16[400,128]{1,0:T(8,128)(2,1)S(1)}, u32[]{:S(2)}, u32[]{:S(2)}) collective-permute-start(bf16[400,128]{1,0:T(8,128)(2,1)S(1)} %add.23.refs_2_), channel_id=1, source_target_pairs={{0,8},{1,9},{2,10},{3,11},{4,12},{5,13},{6,14},{7,15},{8,0},{9,1},... | collective-permute-start | bytes 307208 | tf_op jit(solution)/shard_map/ppermute | solution.py:652
  48.6 0.7 %broadcast_multiply_fusion = f32[2,4,256]{2,1,0:T(4,128)} fusion(f32[2,4,256]{2,1,0:T(4,128)S(1)} %get-tuple-element.63, f32[2,4]{1,0:T(2,128)S(1)} %compare_convert_fusion), kind=kLoop, calls=%fused_computation.9 | loop fusion | flops 2048 | bytes 16416 | tf_op jit(solution)/shard_map/mul | solution.py:814
  49.2 1.8 %finish.1 = f32[2,4,2,8,2,8,128]{6,5,4,3,2,1,0:T(8,128)} custom-call(bf16[4,512,384]{2,1,0:T(8,128)(2,1)S(1)} %get-tuple-element.64.d_packed, f32[4,512,128]{2,1,0:T(8,128)S(1)} %get-tuple-element.65.d_first, f32[4,512,128]{2,1,0:T(8,128)S(1)} %get-tuple-element.57.xh_a.xhats, f32[4,512,128]{2,1,0:T(8,128)S(1)} %get-tuple-element.58.rs_a.rstds, ...), custom_call_target="tpu_custom_call" | custom-call | flops 201326592 | bytes 4194304 | tf_op jit(solution)/shard_map/finish/pallas_call | solution.py:774
  51.0 1.1 %collective-permute-done.11.refs_5_ = bf16[400,128]{1,0:T(8,128)(2,1)S(1)} collective-permute-done((bf16[400,128]{1,0:T(8,128)(2,1)S(1)}, bf16[400,128]{1,0:T(8,128)(2,1)S(1)}, u32[]{:S(2)}, u32[]{:S(2)}) %collective-permute-start.11) | collective-permute-done | bytes 102432 | tf_op jit(solution)/shard_map/ppermute | solution.py:652
  52.3 0.8 %unpack.1 = (f32[1,32]{1,0:T(1,128)}, f32[1,32]{1,0:T(1,128)}, f32[1,32]{1,0:T(1,128)}, f32[32,384]{1,0:T(8,128)}, f32[32,128]{1,0:T(8,128)}, /*index=5*/f32[32,...) custom-call(f32[8,128]{1,0:T(8,128)S(1)} %get-tuple-element.67.gains.refs_0_, ...), custom_call_target="tpu_custom_call" | custom-call | tf_op jit(solution)/shard_map/unpack/pallas_call | solution.py:810
  (17 shorter events, 0.9 us)
Async XLA Ops:
  1.8 8.2 %collective-permute-start = (bf16[816,128]{1,0:T(8,128)(2,1)S(1)}, bf16[816,128]{1,0:T(8,128)(2,1)S(1)}, u32[]{:S(2)}, u32[]{:S(2)}) collective-permute-start(bf16[816,128]{1,0:T(8,128)(2,1)S(1)} %pack.1.shard), channel_id=1, source_target_pairs={{0,2},{1,3},{2,0},{3,1},{4,6},{5,7},{6,4},{7,5},{8,10},{9,11},{10,... | collective-permute-start | bytes 626696 | tf_op jit(solution)/shard_map/ppermute | solution.py:652
  4.9 5.2 %collective-permute-start.1 = (bf16[816,128]{1,0:T(8,128)(2,1)S(1)}, bf16[816,128]{1,0:T(8,128)(2,1)S(1)}, u32[]{:S(2)}, u32[]{:S(2)}) collective-permute-start(bf16[816,128]{1,0:T(8,128)(2,1)S(1)} %pack.1.shard), channel_id=1, source_target_pairs={{0,1},{1,0},{2,3},{3,2},{4,5},{5,4},{6,7},{7,6},{8,9},{9,8},{10,11... | collective-permute-start | bytes 626696 | tf_op jit(solution)/shard_map/ppermute | solution.py:652
  4.9 0.7 %copy-start = (s32[2]{0:T(128)S(1)}, s32[2]{0:T(128)}, u32[]{:S(2)}) copy-start(s32[2]{0:T(128)} %count.1) | copy-start | bytes 28
  10.0 1.5 %collective-permute-start.2 = (bf16[816,128]{1,0:T(8,128)(2,1)S(1)}, bf16[816,128]{1,0:T(8,128)(2,1)S(1)}, u32[]{:S(2)}, u32[]{:S(2)}) collective-permute-start(bf16[816,128]{1,0:T(8,128)(2,1)S(1)} %collective-permute-done.refs_2_), channel_id=1, source_target_pairs={{0,1},{1,0},{2,3},{3,2},{4,5},{5,4},{6,7},{7,6},{8,9},{9,8},{10,11... | collective-permute-start | bytes 626696 | tf_op jit(solution)/shard_map/ppermute | solution.py:652
  27.2 13.4 %copy-start.1 = (s32[2]{0:T(128)S(1)}, s32[2]{0:T(128)}, u32[]{:S(2)}) copy-start(s32[2]{0:T(128)} %count.1) | copy-start | bytes 28
  27.2 1.5 %collective-permute-start.3 = (bf16[1,800,128]{2,1,0:T(8,128)(2,1)S(1)}, bf16[1,800,128]{2,1,0:T(8,128)(2,1)S(1)}, u32[]{:S(2)}, u32[]{:S(2)}) collective-permute-start(bf16[1,800,128]{2,1,0:T(8,128)(2,1)S(1)} %get-tuple-element.82), channel_id=1, source_target_pairs={{0,1},{1,0},{2,3},{3,2},{4,5},{5,4},{6,7},{7,6},{8,9},{9,8},{10,11... | collective-permute-start | bytes 614408 | tf_op jit(solution)/shard_map/ppermute | solution.py:652
  27.4 1.6 %collective-permute-start.4 = (bf16[1,800,128]{2,1,0:T(8,128)(2,1)S(1)}, bf16[1,800,128]{2,1,0:T(8,128)(2,1)S(1)}, u32[]{:S(2)}, u32[]{:S(2)}) collective-permute-start(bf16[1,800,128]{2,1,0:T(8,128)(2,1)S(1)} %get-tuple-element.83), channel_id=1, source_target_pairs={{0,1},{1,0},{2,3},{3,2},{4,5},{5,4},{6,7},{7,6},{8,9},{9,8},{10,11... | collective-permute-start | bytes 614408 | tf_op jit(solution)/shard_map/ppermute | solution.py:652
  29.1 6.6 %collective-permute-start.5 = (bf16[400,128]{1,0:T(8,128)(2,1)S(1)}, bf16[400,128]{1,0:T(8,128)(2,1)S(1)}, u32[]{:S(2)}, u32[]{:S(2)}) collective-permute-start(bf16[400,128]{1,0:T(8,128)(2,1)S(1)} %get-tuple-element.84), channel_id=1, source_target_pairs={{0,2},{1,3},{2,0},{3,1},{4,6},{5,7},{6,4},{7,5},{8,10},{9,11},{10,... | collective-permute-start | bytes 307208 | tf_op jit(solution)/shard_map/ppermute | solution.py:652
  30.9 6.5 %collective-permute-start.7 = (bf16[400,128]{1,0:T(8,128)(2,1)S(1)}, bf16[400,128]{1,0:T(8,128)(2,1)S(1)}, u32[]{:S(2)}, u32[]{:S(2)}) collective-permute-start(bf16[400,128]{1,0:T(8,128)(2,1)S(1)} %get-tuple-element.85), channel_id=1, source_target_pairs={{0,6},{1,7},{2,4},{3,5},{4,2},{5,3},{6,0},{7,1},{8,14},{9,15},{10,... | collective-permute-start | bytes 307208 | tf_op jit(solution)/shard_map/ppermute | solution.py:652
  32.3 5.3 %collective-permute-start.6 = (bf16[400,128]{1,0:T(8,128)(2,1)S(1)}, bf16[400,128]{1,0:T(8,128)(2,1)S(1)}, u32[]{:S(2)}, u32[]{:S(2)}) collective-permute-start(bf16[400,128]{1,0:T(8,128)(2,1)S(1)} %slice_bitcast_fusion.1), channel_id=1, source_target_pairs={{0,4},{1,5},{2,6},{3,7},{4,0},{5,1},{6,2},{7,3},{8,12},{9,13},{10,... | collective-permute-start | bytes 307208 | tf_op jit(solution)/shard_map/ppermute | solution.py:652
  37.7 7.2 %collective-permute-start.8 = (bf16[400,128]{1,0:T(8,128)(2,1)S(1)}, bf16[400,128]{1,0:T(8,128)(2,1)S(1)}, u32[]{:S(2)}, u32[]{:S(2)}) collective-permute-start(bf16[400,128]{1,0:T(8,128)(2,1)S(1)} %fusion.1), channel_id=1, source_target_pairs={{0,16},{1,17},{2,18},{3,19},{4,20},{5,21},{6,22},{7,23},{8,24},{9,... | collective-permute-start | bytes 307208 | tf_op jit(solution)/shard_map/ppermute | solution.py:652
  45.0 6.0 %collective-permute-start.10 = (bf16[400,128]{1,0:T(8,128)(2,1)S(1)}, bf16[400,128]{1,0:T(8,128)(2,1)S(1)}, u32[]{:S(2)}, u32[]{:S(2)}) collective-permute-start(bf16[400,128]{1,0:T(8,128)(2,1)S(1)} %add.23.refs_2_), channel_id=1, source_target_pairs={{0,4},{1,5},{2,6},{3,7},{4,0},{5,1},{6,2},{7,3},{8,12},{9,13},{10,... | collective-permute-start | bytes 307208 | tf_op jit(solution)/shard_map/ppermute | solution.py:652
  46.5 5.6 %collective-permute-start.11 = (bf16[400,128]{1,0:T(8,128)(2,1)S(1)}, bf16[400,128]{1,0:T(8,128)(2,1)S(1)}, u32[]{:S(2)}, u32[]{:S(2)}) collective-permute-start(bf16[400,128]{1,0:T(8,128)(2,1)S(1)} %add.23.refs_2_), channel_id=1, source_target_pairs={{0,12},{1,13},{2,14},{3,15},{4,8},{5,9},{6,10},{7,11},{8,4},{9,5},... | collective-permute-start | bytes 307208 | tf_op jit(solution)/shard_map/ppermute | solution.py:652
  47.2 5.1 %collective-permute-start.9 = (bf16[400,128]{1,0:T(8,128)(2,1)S(1)}, bf16[400,128]{1,0:T(8,128)(2,1)S(1)}, u32[]{:S(2)}, u32[]{:S(2)}) collective-permute-start(bf16[400,128]{1,0:T(8,128)(2,1)S(1)} %add.23.refs_2_), channel_id=1, source_target_pairs={{0,8},{1,9},{2,10},{3,11},{4,12},{5,13},{6,14},{7,15},{8,0},{9,1},... | collective-permute-start | bytes 307208 | tf_op jit(solution)/shard_map/ppermute | solution.py:652
